TPU v7x, 256 devices: a whole 4x4x8 slice. The times are simulated.
256 devices in a mesh: blk: 64 (over y, z, core), span: 4 (over x).
Axes of the slice: x: 4, y: 4, z: 8, core: 2. Of those that a mesh axis runs over, the one named last changes fastest.
Arguments:
- velocity: float32 [3, 1024, 128, 128], P(None, 'blk', 'span'), may hold values from -6 to 6
- stretch: float32 [3, 1024, 128, 128], P(None, 'blk', 'span'), may hold values from 0.5 to 2
- coupling: float32 [1024, 128, 128], P('blk', 'span'), may hold values from 0.05 to 0.5
- strengths: bfloat16 [32768, 128], P(('blk', 'span')), may hold values from -6 to 6
- remesh: bfloat16 [2097152, 128], P(('blk', 'span')), may hold values from -0.5 to 0.5
- green_left: bfloat16 [128, 128], replicated, may hold values from -0.5 to 0.5
- green_right: bfloat16 [128, 128], replicated, may hold values from -0.5 to 0.5
- tile_owner: int32 [16384, 1], replicated, may hold values from 0 to 63; in each aligned block of 64 rows (0 to 63, 64 to 127, ...) at most 2 rows name the same one
- tile_place: int32 [16384], replicated, may hold values from 0 to 11
- row_dest: int32 [393216, 1], replicated, may hold values from 0 to 63; in each aligned block of 1536 rows (0 to 1535, 1536 to 3071, ...) at most 48 rows name the same one
- row_place: int32 [393216], replicated, may hold values from 0 to 8191
Outputs:
- velocity_next: float32 [3, 1024, 128, 128], P(None, 'blk', 'span')
- strengths_next: float32 [32768, 128], P(('blk', 'span'))
Inputs may be any that keep to these rules, and one draw needn't show every extreme that they name: `tile_owner`: among the 64 tiles of one box, no chord block is named by more than 2, and one is named by exactly 2. `row_dest`: among the 1536 rows of one grid block, no chord block is named by more than 48, and one is named by exactly 48.
All inputs are finite; a program needn't handle non-finite values.
Results may differ from a plain program's by a relative error of at most 0.004.
Values may be sent and summed in bfloat16 or wider, within the bound.
No kernel may reach another device: no remote copies, remote signals or barrier semaphores. Data moves between devices by JAX's collectives and lax.ppermute only.
A program may use at most 128 MiB of HBM per device.

v0:
```python
import jax
import jax.numpy as jnp
from jax import lax
from jax.experimental import pallas as pl
from jax.experimental.pallas import tpu as pltpu
from jax.sharding import PartitionSpec as P

step_size = 0.05
viscosity = 0.4
blend = 0.5

EDGE = 128
REACH = 3
SIDE = 8
GROUP = 16


def pieces_kernel(remesh_ref, strengths_ref, left_ref, out_ref, scratch):
    vortex = jnp.dot(
        remesh_ref[...], strengths_ref[...], preferred_element_type=jnp.float32
    ).astype(jnp.bfloat16)
    left = left_ref[...]
    for pair in range(GROUP // 2):
        first = vortex[(2 * pair) * EDGE : (2 * pair + 1) * EDGE]
        second = vortex[(2 * pair + 1) * EDGE : (2 * pair + 2) * EDGE]
        both = jnp.dot(
            left, jnp.concatenate([first, second], axis=1), preferred_element_type=jnp.float32
        )
        for half in range(2):
            tile = 2 * pair + half
            for quarter in range(4):
                for side in range(2):
                    start = quarter * 32 + side * 16
                    scratch[
                        side, pl.ds(quarter * 16 * GROUP + tile, 16, stride=GROUP), :
                    ] = both[start : start + 16, half * EDGE : (half + 1) * EDGE]
    for side in range(2):
        out_ref[:, :, side * EDGE : (side + 1) * EDGE] = (
            scratch[side].astype(jnp.bfloat16).reshape(64, GROUP, EDGE)
        )


def tile_pieces(remesh, strengths, left):
    tiles = remesh.shape[0] // EDGE
    return pl.pallas_call(
        pieces_kernel,
        grid=(tiles // GROUP,),
        in_specs=[
            pl.BlockSpec((GROUP * EDGE, EDGE), lambda g: (g, 0)),
            pl.BlockSpec((EDGE, EDGE), lambda g: (0, 0)),
            pl.BlockSpec((EDGE, EDGE), lambda g: (0, 0)),
        ],
        out_specs=pl.BlockSpec((64, GROUP, 2 * EDGE), lambda g: (0, g, 0)),
        out_shape=jax.ShapeDtypeStruct((64, tiles, 2 * EDGE), jnp.bfloat16),
        scratch_shapes=[pltpu.VMEM((2, 64 * GROUP, EDGE), jnp.float32)],
        compiler_params=pltpu.CompilerParams(vmem_limit_bytes=32 * 1024 * 1024),
    )(remesh, strengths, left)


def gather_kernel(index_ref, remesh_ref, out_ref, wide, picked):
    wide[...] = remesh_ref[...].astype(jnp.float32)

    def some(step, carry):
        for k in range(16):
            slot = step * 16 + k
            picked[pl.ds(slot, 1), :] = wide[pl.ds(index_ref[slot], 1), :]
        return carry

    lax.fori_loop(0, out_ref.shape[0] // 16, some, 0)
    out_ref[...] = picked[...].astype(jnp.bfloat16)


def gathered_rows(index, remesh):
    slots = index.shape[0]
    return pl.pallas_call(
        gather_kernel,
        in_specs=[
            pl.BlockSpec(memory_space=pltpu.SMEM),
            pl.BlockSpec(memory_space=pltpu.VMEM),
        ],
        out_specs=pl.BlockSpec(memory_space=pltpu.VMEM),
        out_shape=jax.ShapeDtypeStruct((slots, EDGE), jnp.bfloat16),
        scratch_shapes=[
            pltpu.VMEM(remesh.shape, jnp.float32),
            pltpu.VMEM((slots, EDGE), jnp.float32),
        ],
        compiler_params=pltpu.CompilerParams(vmem_limit_bytes=40 * 1024 * 1024),
        cost_estimate=pl.CostEstimate(flops=0, bytes_accessed=16 * 1024 * 1024, transcendentals=0),
    )(index, remesh)


def grid_kernel(
    sums_ref,
    low_ref,
    high_ref,
    right_ref,
    fields_ref,
    next_ref,
    rows_ref,
    centre_sums,
    side_sums,
    target,
    first,
    second,
):
    right = right_ref[...]
    span = 32
    wide = span + 2 * SIDE
    for side in range(2):
        centre_sums[side] = jnp.dot(
            sums_ref[:, side * EDGE : (side + 1) * EDGE], right, preferred_element_type=jnp.float32
        )
    side_sums[0] = jnp.dot(low_ref[...], right, preferred_element_type=jnp.float32)
    side_sums[1] = jnp.dot(high_ref[...], right, preferred_element_type=jnp.float32)
    for component in range(3):
        for layer in range(20):
            chord = layer - 2
            quarter = chord % 4
            entry = component * 4 + chord // 4 if 0 <= chord < 16 else 12 + component
            for side in range(2):
                target[component, layer, SIDE + 16 * side : SIDE + 16 * side + 16, :] = centre_sums[
                    side, pl.ds(quarter * 256 + entry, 16, stride=16), :
                ]
            target[component, layer, SIDE - 2 : SIDE, :] = side_sums[
                0, pl.ds(quarter * 32 + entry, 2, stride=16), :
            ]
            target[component, layer, SIDE + span : SIDE + span + 2, :] = side_sums[
                1, pl.ds(quarter * 32 + entry, 2, stride=16), :
            ]

    lanes = lax.broadcasted_iota(jnp.int32, (wide, EDGE), 1)
    not_last = lanes < EDGE - 1
    not_first = lanes > 0

    def after(value, direction):
        if direction == 1:
            return pltpu.roll(value, wide - 1, 0)
        return jnp.where(not_last, pltpu.roll(value, EDGE - 1, 1), 0.0)

    def before(value, direction):
        if direction == 1:
            return pltpu.roll(value, 1, 0)
        return jnp.where(not_first, pltpu.roll(value, 1, 1), 0.0)

    def advanced(source, at, layer, target_layer):
        centre = [source[c, at] for c in range(3)]
        stretch = [fields_ref[3 + d, layer] for d in range(3)]
        rate = fields_ref[6, layer]
        squares = [(step_size * viscosity) * s * s for s in stretch]
        carried = [(0.5 * step_size) * s * u for s, u in zip(stretch, centre)]
        results = []
        for c in range(3):
            value = centre[c]
            twice = 2.0 * value
            change = rate * (target[c, target_layer] - value)
            for d in range(3):
                if d == 0:
                    ahead, behind = source[c, at + 1], source[c, at - 1]
                else:
                    ahead, behind = after(value, d), before(value, d)
                change = change + squares[d] * (ahead + behind - twice)
                change = change - carried[d] * (ahead - behind)
            results.append(value + change)
        return results

    def first_step(layer, carry):
        results = advanced(fields_ref, layer + 1, layer + 1, layer)
        for c in range(3):
            first[c, layer] = results[c]
        return carry

    lax.fori_loop(0, 20, first_step, 0)

    def second_step(layer, carry):
        results = advanced(first, layer + 1, layer + 2, layer + 1)
        for c in range(3):
            second[c, layer] = results[c]
        return carry

    lax.fori_loop(0, 18, second_step, 0)

    def curl(layer, carry):
        centre = [second[c, layer + 1] for c in range(3)]
        half = [0.5 * fields_ref[3 + d, layer + 3] for d in range(3)]

        def slope(d, c):
            if d == 0:
                return half[0] * (second[c, layer + 2] - second[c, layer])
            return half[d] * (after(centre[c], d) - before(centre[c], d))

        parts = (
            slope(1, 2) - slope(2, 1),
            slope(2, 0) - slope(0, 2),
            slope(0, 1) - slope(1, 0),
        )
        for c in range(3):
            rows_ref[c, layer] = parts[c][SIDE : SIDE + span].astype(jnp.bfloat16)
            next_ref[c, layer] = centre[c][SIDE : SIDE + span]
        return carry

    lax.fori_loop(0, 16, curl, 0)


def grid_update(sums, low, high, right, fields):
    wide = 32 + 2 * SIDE
    vmem = pl.BlockSpec(memory_space=pltpu.VMEM)
    return pl.pallas_call(
        grid_kernel,
        in_specs=[vmem] * 5,
        out_specs=[vmem] * 2,
        out_shape=[
            jax.ShapeDtypeStruct((3, 16, 32, EDGE), jnp.float32),
            jax.ShapeDtypeStruct((3, 16, 32, EDGE), jnp.bfloat16),
        ],
        scratch_shapes=[
            pltpu.VMEM((2, 1024, EDGE), jnp.float32),
            pltpu.VMEM((2, 128, EDGE), jnp.float32),
            pltpu.VMEM((3, 20, wide, EDGE), jnp.float32),
            pltpu.VMEM((3, 20, wide, EDGE), jnp.float32),
            pltpu.VMEM((3, 18, wide, EDGE), jnp.float32),
        ],
        compiler_params=pltpu.CompilerParams(vmem_limit_bytes=40 * 1024 * 1024),
    )(sums, low, high, right, fields)


def exchanged(block, axis, dim, width):
    count = lax.axis_size(axis)
    forward = [(i, i + 1) for i in range(count - 1)]
    backward = [(target, source) for source, target in forward]
    low = lax.ppermute(
        lax.slice_in_dim(block, block.shape[dim] - width, None, axis=dim), axis, forward
    )
    high = lax.ppermute(lax.slice_in_dim(block, 0, width, axis=dim), axis, backward)
    return low, high


def slot_ranks(destination, block_count):
    count = destination.shape[0]
    one_hot = (destination[:, None] == jnp.arange(block_count, dtype=jnp.int32)[None, :]).astype(
        jnp.bfloat16
    )
    positions = jnp.arange(count, dtype=jnp.int32)
    lower = (positions[:, None] > positions[None, :]).astype(jnp.bfloat16)
    before = jnp.dot(lower, one_hot, preferred_element_type=jnp.float32)
    return jnp.sum(before * one_hot.astype(jnp.float32), axis=1).astype(jnp.int32)


def arrival_places(destination, places, receiver, capacity):
    count = destination.shape[1]
    to_me = destination == receiver
    positions = jnp.arange(count, dtype=jnp.int32)
    upper = (positions[:, None] < positions[None, :]).astype(jnp.bfloat16)
    rank = jnp.dot(
        to_me.astype(jnp.bfloat16), upper, preferred_element_type=jnp.float32
    ).astype(jnp.int32)
    rank = jnp.where(to_me, rank, -1)
    matches = rank[:, None, :] == jnp.arange(capacity, dtype=jnp.int32)[None, :, None]
    return jnp.sum(jnp.where(matches, places[:, None, :], 0), axis=2).reshape(-1)


def shards(
    velocity,
    stretch,
    coupling,
    strengths,
    remesh,
    green_left,
    green_right,
    tile_owner,
    tile_place,
    row_dest,
    row_place,
):
    blocks = lax.axis_size("blk")
    spans = lax.axis_size("span")
    my_block = lax.axis_index("blk")
    my_span = lax.axis_index("span")
    tile_count = remesh.shape[0] // EDGE
    grid_count = velocity.shape[0] * velocity.shape[1] * velocity.shape[2]
    row_cap = 2 * grid_count // blocks

    pieces = tile_pieces(remesh, strengths, green_left)
    held = (
        velocity,
        stretch,
        coupling,
        tile_owner,
        tile_place,
        row_dest,
        row_place,
    )
    pieces, held = lax.optimization_barrier((pieces, held))
    velocity, stretch, coupling, tile_owner, tile_place, row_dest, row_place = held
    arrived = lax.all_to_all(pieces, "blk", split_axis=0, concat_axis=0, tiled=True)

    def mine(values, count):
        return lax.dynamic_index_in_dim(
            values.reshape(blocks, spans, count), my_span, 1, keepdims=False
        )

    owners = mine(tile_owner, tile_count).reshape(-1)
    places = mine(tile_place, tile_count).reshape(-1)
    position = owners * 12 + places
    entry = jnp.arange(16, dtype=jnp.int32)[None, :]
    block = jnp.arange(blocks, dtype=jnp.int32)[:, None]
    quarter = my_block // 16
    outer = jnp.where(
        quarter >= 2, (block - 1) * 12 + (entry - 12) * 4 + 3, (block + 1) * 12 + (entry - 12) * 4
    )
    outer_block = jnp.where(quarter >= 2, block - 1, block + 1)
    outer = jnp.where((outer_block >= 0) & (outer_block < blocks) & (entry < 15), outer, -1)
    wanted = jnp.where(entry < 12, block * 12 + entry, outer).reshape(-1)
    tile_picker = (wanted[:, None] == position[None, :]).astype(jnp.bfloat16)

    fields = jnp.concatenate([velocity, stretch, coupling[None]], axis=0)
    low, high = exchanged(fields, "blk", 1, REACH)
    fields = jnp.concatenate([low, fields, high], axis=1)
    low, high = exchanged(fields, "span", 2, REACH)
    blank = jnp.zeros(fields.shape[:2] + (SIDE - REACH, EDGE), fields.dtype)
    fields = jnp.concatenate([blank, low, fields, high, blank], axis=2)

    destinations = mine(row_dest, grid_count)
    row_places = mine(row_place, grid_count)
    dest_mine = lax.dynamic_index_in_dim(destinations, my_block, 0, keepdims=False)
    row_slot = dest_mine * row_cap + slot_ranks(dest_mine, blocks)
    row_spreader = (
        row_slot[None, :] == jnp.arange(blocks * row_cap, dtype=jnp.int32)[:, None]
    ).astype(jnp.bfloat16)
    row_where = arrival_places(destinations, row_places, my_block, row_cap)
    remesh_rows = gathered_rows(row_where, remesh)

    arrived, tile_picker, fields, row_spreader, remesh_rows = lax.optimization_barrier(
        (arrived, tile_picker, fields, row_spreader, remesh_rows)
    )
    sums = jnp.dot(
        tile_picker, arrived.reshape(-1, 2 * EDGE), preferred_element_type=jnp.float32
    ).astype(jnp.bfloat16)
    sums = lax.all_to_all(
        sums.reshape(blocks, 16, 2 * EDGE), "blk", split_axis=0, concat_axis=0, tiled=True
    )
    split = sums.reshape(4, 16, 16, 2 * EDGE)
    forward = [(i, i + 1) for i in range(spans - 1)]
    backward = [(i + 1, i) for i in range(spans - 1)]
    low = lax.ppermute(split[:, 14:16, :, EDGE:], "span", forward)
    high = lax.ppermute(split[:, 0:2, :, :EDGE], "span", backward)
    current, vorticity = grid_update(
        sums.reshape(-1, 2 * EDGE),
        low.reshape(-1, EDGE),
        high.reshape(-1, EDGE),
        green_right,
        fields,
    )
    outgoing = jnp.dot(
        row_spreader, vorticity.reshape(grid_count, EDGE), preferred_element_type=jnp.float32
    ).astype(jnp.bfloat16)
    incoming = lax.all_to_all(
        outgoing.reshape(blocks, row_cap, EDGE), "blk", split_axis=0, concat_axis=0, tiled=True
    )
    spread = lax.dot_general(
        remesh_rows,
        incoming.reshape(-1, EDGE),
        (((0,), (0,)), ((), ())),
        preferred_element_type=jnp.float32,
    )
    return current, (1.0 - blend) * strengths.astype(jnp.float32) + blend * spread


def solution(mesh):
    placed = (
        P(None, "blk", "span", None),
        P(None, "blk", "span", None),
        P("blk", "span", None),
        P(("blk", "span"), None),
        P(("blk", "span"), None),
        P(),
        P(),
        P(),
        P(),
        P(),
        P(),
    )
    return jax.shard_map(
        shards,
        mesh=mesh,
        in_specs=placed,
        out_specs=(P(None, "blk", "span", None), P(("blk", "span"), None)),
        check_vma=False,
    )
```

profile of v0, /device:TPU:1, one launch (start us, length us, event | category | flops | bytes accessed | tf_op | source)
XLA Modules:
  0.0 181.7 jit_solution(14648295798353490550)
XLA Ops:
  0.6 1.6 copy-done.1
  3.7 3.9 %shard_map.122 = bf16[64,64,256]{2,1,0:T(8,128)(2,1)} custom-call(bf16[8192,128]{1,0:T(8,128)(2,1)S(1)} %copy-done.1, bf16[128,128]{1,0:T(8,128)(2,1)S(1)} %copy-done.3, bf16[128,128]{1,0:T(8,128)(2,1)S(1)} %copy-done.5), custom_call_target="tpu_custom_call" | custom-call | tf_op jit(solution)/shard_map/pallas_call | solution.py:45
  7.7 13.5 %all-to-all-start = ((bf16[64,64,256]{2,1,0:T(8,128)(2,1)}), bf16[64,64,256]{2,1,0:T(8,128)(2,1)}, u32[]{:S(2)}, u32[]{:S(2)}) async-start(bf16[64,64,256]{2,1,0:T(8,128)(2,1)} %shard_map.122), calls=%async_computation | async-start | bytes 4194304 | tf_op jit(solution)/shard_map/all_to_all | solution.py:294
  21.2 0.9 pad_maximum_fusion.3
  22.1 3.5 %collective-permute-start = (f32[7,3,32,128]{3,2,1,0:T(8,128)}, f32[7,3,32,128]{3,2,1,0:T(8,128)}, u32[]{:S(2)}, u32[]{:S(2)}) collective-permute-start(f32[7,3,32,128]{3,2,1,0:T(8,128)} %get-tuple-element.34), channel_id=1, source_target_pairs={{0,4},{4,8},{8,12},{12,16},{16,20},{20,24},{24,28},{28,32},{32,36}... | collective-permute-start | bytes 1032200 | tf_op jit(solution)/shard_map/ppermute | solution.py:230
  25.7 1.9 %collective-permute-start.1 = (f32[7,3,32,128]{3,2,1,0:T(8,128)}, f32[7,3,32,128]{3,2,1,0:T(8,128)}, u32[]{:S(2)}, u32[]{:S(2)}) collective-permute-start(f32[7,3,32,128]{3,2,1,0:T(8,128)} %get-tuple-element.35), channel_id=1, source_target_pairs={{4,0},{8,4},{12,8},{16,12},{20,16},{24,20},{28,24},{32,28},{36,32}... | collective-permute-start | bytes 1032200 | tf_op jit(solution)/shard_map/ppermute | solution.py:233
  28.4 0.8 reduce.12
  29.7 14.7 %reduce.13 = s32[393216]{0:T(1024)S(1)} reduce(s32[393216,1]{0,1:T(1,128)} %param.20, s32[]{:T(128)} %broadcast.170), dimensions={1}, to_apply=%get-tuple-element.23.reduce_sub_computation.3 | reduce | bytes 3145732 | tf_op jit(solution)/shard_map/optimization_barrier | solution.py:292
  45.0 1.0 fusion.6
  46.0 2.0 %reshape.199 = s32[64,4,1536]{2,1,0:T(4,128)S(1)} reshape(s32[393216]{0:T(1024)} %param.21) | data formatting | bytes 3145728 | tf_op jit(solution)/shard_map/reshape | solution.py:298
  48.0 5.5 %compare_convert_fusion = bf16[1024,4096]{1,0:T(8,128)(2,1)} fusion(s32[4096]{0:T(1024)S(1)} %add.147, s32[1024]{0:T(1024)S(1)} %reshape.210), kind=kLoop, calls=%fused_computation.4 | loop fusion | flops 8388608 | bytes 8409088 | tf_op jit(solution)/shard_map/convert_element_type | solution.py:313
  53.6 8.3 %fusion = bf16[3072,1536]{1,0:T(8,128)(2,1)} fusion(s32[1536]{0:T(1024)S(1)} %convert_add_fusion), kind=kLoop, calls=%fused_computation.3 | loop fusion | flops 9437184 | bytes 9443328 | tf_op jit(solution)/shard_map/convert_element_type | solution.py:328
  61.9 0.8 constant_dynamic-slice_fusion
  63.5 6.6 %collective-permute-done = f32[7,3,32,128]{3,2,1,0:T(8,128)} collective-permute-done((f32[7,3,32,128]{3,2,1,0:T(8,128)}, f32[7,3,32,128]{3,2,1,0:T(8,128)}, u32[]{:S(2)}, u32[]{:S(2)}) %collective-permute-start) | collective-permute-done | bytes 344096 | tf_op jit(solution)/shard_map/ppermute | solution.py:230
  70.1 2.1 %collective-permute-done.1 = f32[7,3,32,128]{3,2,1,0:T(8,128)} collective-permute-done((f32[7,3,32,128]{3,2,1,0:T(8,128)}, f32[7,3,32,128]{3,2,1,0:T(8,128)}, u32[]{:S(2)}, u32[]{:S(2)}) %collective-permute-start.1) | collective-permute-done | bytes 344096 | tf_op jit(solution)/shard_map/ppermute | solution.py:233
  72.2 1.4 pad_maximum_fusion
  73.6 1.5 copy-done.7
  75.1 0.9 fusion.15
  76.0 1.3 collective-permute-start.3
  77.3 4.0 %collective-permute-start.2 = (f32[7,22,3,128]{3,2,1,0:T(4,128)}, f32[7,22,3,128]{3,2,1,0:T(4,128)S(1)}, u32[]{:S(2)}, u32[]{:S(2)}) collective-permute-start(f32[7,22,3,128]{3,2,1,0:T(4,128)} %get-tuple-element.33), channel_id=1, source_target_pairs={{0,1},{1,2},{2,3},{4,5},{5,6},{6,7},{8,9},{9,10},{10,11},{12,13},{... | collective-permute-start | bytes 709640 | tf_op jit(solution)/shard_map/ppermute | solution.py:230
  81.3 2.8 %select_reduce_fusion = s32[64,48]{1,0:T(8,128)S(1)} fusion(s32[64,1536]{1,0:T(8,128)S(1)} %bitcast.35, s32[64,1536]{1,0:T(8,128)S(1)} %fusion.5), kind=kLoop, calls=%fused_computation | loop fusion | flops 14152704 | bytes 798720 | tf_op jit(solution)/shard_map/reduce_sum | solution.py:258
  84.2 4.5 %shard_map.123 = bf16[3072,128]{1,0:T(8,128)(2,1)S(1)} custom-call(s32[3072]{0:T(1024)S(1)} %reshape.200.index_ref, bf16[8192,128]{1,0:T(8,128)(2,1)S(1)} %copy-done.2), custom_call_target="tpu_custom_call" | custom-call | bytes 16777216 | tf_op jit(solution)/shard_map/pallas_call | solution.py:75
  88.8 12.0 %concatenate.11.fields_ref = f32[7,22,48,128]{3,2,1,0:T(8,128)} concatenate(f32[7,22,5,128]{3,2,1,0:T(8,128)S(1)} %broadcast_in_dim.55, f32[7,22,3,128]{3,2,1,0:T(4,128)S(1)} %collective-permute-done.2, f32[7,22,32,128]{3,2,1,0:T(8,128)} %copy-done.7, f32[7,22,3,128]{3,2,1,0:T(4,128)S(1)} %collective-permute-done.3, f32[7,22,5,128]{3,2,1,0:T(8,128)S(1)} %broadcast_in_dim.55), dimensions={2} | concatenate | bytes 7569408 | tf_op jit(solution)/shard_map/concatenate | solution.py:320
  100.8 6.5 %convolution_convert_fusion.1 = bf16[1024,256]{1,0:T(8,128)(2,1)S(1)} fusion(bf16[1024,4096]{1,0:T(8,128)(2,1)} %compare_convert_fusion, bf16[4096,256]{1,0:T(8,128)(2,1)} %bitcast.2), kind=kOutput, calls=%fused_computation.14 | convolution fusion | flops 2147745792 | bytes 11010048 | tf_op jit(solution)/shard_map/dot_general | solution.py:335
  107.3 27.1 %all_to_all.15 = bf16[64,16,256]{2,1,0:T(8,128)(2,1)S(1)} all-to-all(bf16[64,16,256]{2,1,0:T(8,128)(2,1)S(1)} %bitcast.39), channel_id=1, replica_groups=mesh['blk'=64,'span'=4] {'blk'}, dimensions={0} | all-to-all | bytes 1048576 | tf_op jit(solution)/shard_map/all_to_all | solution.py:338
  134.4 1.3 collective-permute-start.5
  135.7 4.1 %collective-permute-start.4 = (bf16[4,2,16,128]{3,2,1,0:T(8,128)(2,1)S(1)}, bf16[4,2,16,128]{3,2,1,0:T(8,128)(2,1)S(1)}, u32[]{:S(2)}, u32[]{:S(2)}) collective-permute-start(bf16[4,2,16,128]{3,2,1,0:T(8,128)(2,1)S(1)} %get-tuple-element.37), channel_id=1, source_target_pairs={{0,1},{1,2},{2,3},{4,5},{5,6},{6,7},{8,9},{9,10},{10,11},{12,13},{... | collective-permute-start | bytes 98312 | tf_op jit(solution)/shard_map/ppermute | solution.py:344
  139.8 1.0 collective-permute-done.4
  140.8 7.1 %shard_map.124 = (f32[3,16,32,128]{3,2,1,0:T(8,128)}, bf16[3,16,32,128]{3,2,1,0:T(8,128)(2,1)S(1)}) custom-call(bf16[1024,256]{1,0:T(8,128)(2,1)S(1)} %bitcast.28, bf16[128,128]{1,0:T(8,128)(2,1)S(1)} %bitcast.30, bf16[128,128]{1,0:T(8,128)(2,1)S(1)} %bitcast.29, bf16[128,128]{1,0:T(8,128)(2,1)S(1)} %copy-done.6, f32[7,22,48,128]{3,2,1,0:T(8,128)S(1)} %copy-done), custom_call_target="tpu_custom_call" | custom-call | tf_op jit(solution)/shard_map/pallas_call | solution.py:207
  148.0 2.6 %convolution_convert_fusion = bf16[3072,128]{1,0:T(8,128)(2,1)S(1)} fusion(bf16[3072,1536]{1,0:T(8,128)(2,1)S(1)} %bitcast.33, bf16[1536,128]{1,0:T(8,128)(2,1)S(1)} %bitcast.31), kind=kOutput, calls=%fused_computation.9 | convolution fusion | flops 1208352768 | bytes 10616832 | tf_op jit(solution)/shard_map/dot_general | solution.py:353
  150.6 30.1 %all_to_all.16 = bf16[64,48,128]{2,1,0:T(8,128)(2,1)S(1)} all-to-all(bf16[64,48,128]{2,1,0:T(8,128)(2,1)S(1)} %bitcast.38), channel_id=1, replica_groups=mesh['blk'=64,'span'=4] {'blk'}, dimensions={0} | all-to-all | bytes 1572864 | tf_op jit(solution)/shard_map/all_to_all | solution.py:356
  180.6 1.0 fusion.7
  (59 shorter events, 4.2 us)
Async XLA Ops:
  0.6 1.6 copy-start.1
  2.2 0.8 copy-start.3
  3.0 0.8 copy-start.5
  7.7 13.5 %copy-start.8 = (f32[3,16,32,128]{3,2,1,0:T(8,128)S(1)}, f32[3,16,32,128]{3,2,1,0:T(8,128)}, u32[]{:S(2)}) copy-start(f32[3,16,32,128]{3,2,1,0:T(8,128)} %param.12) | copy-start | bytes 2359300
  7.7 13.5 %copy-start.10 = (f32[3,16,32,128]{3,2,1,0:T(8,128)S(1)}, f32[3,16,32,128]{3,2,1,0:T(8,128)}, u32[]{:S(2)}) copy-start(f32[3,16,32,128]{3,2,1,0:T(8,128)} %param.11) | copy-start | bytes 2359300
  7.7 13.5 %copy-start.12 = (f32[16,32,128]{2,1,0:T(8,128)S(1)}, f32[16,32,128]{2,1,0:T(8,128)}, u32[]{:S(2)}) copy-start(f32[16,32,128]{2,1,0:T(8,128)} %param.13) | copy-start | bytes 786436
  7.7 20.7 %copy-start.14 = (s32[16384,1]{0,1:T(1,128)S(1)}, s32[16384,1]{0,1:T(1,128)}, u32[]{:S(2)}) copy-start(s32[16384,1]{0,1:T(1,128)} %param.18) | copy-start | bytes 196612
  7.7 93.1 %all-to-all-start = ((bf16[64,64,256]{2,1,0:T(8,128)(2,1)}), bf16[64,64,256]{2,1,0:T(8,128)(2,1)}, u32[]{:S(2)}, u32[]{:S(2)}) async-start(bf16[64,64,256]{2,1,0:T(8,128)(2,1)} %shard_map.122), calls=%async_computation | async-start | bytes 4194304 | tf_op jit(solution)/shard_map/all_to_all | solution.py:294
  21.2 8.1 %copy-start.13 = (s32[16384]{0:T(1024)S(1)}, s32[16384]{0:T(1024)}, u32[]{:S(2)}) copy-start(s32[16384]{0:T(1024)} %param.19) | copy-start | bytes 196612
  22.1 48.0 %collective-permute-start = (f32[7,3,32,128]{3,2,1,0:T(8,128)}, f32[7,3,32,128]{3,2,1,0:T(8,128)}, u32[]{:S(2)}, u32[]{:S(2)}) collective-permute-start(f32[7,3,32,128]{3,2,1,0:T(8,128)} %get-tuple-element.34), channel_id=1, source_target_pairs={{0,4},{4,8},{8,12},{12,16},{16,20},{20,24},{24,28},{28,32},{32,36}... | collective-permute-start | bytes 1032200 | tf_op jit(solution)/shard_map/ppermute | solution.py:230
  25.7 46.5 %collective-permute-start.1 = (f32[7,3,32,128]{3,2,1,0:T(8,128)}, f32[7,3,32,128]{3,2,1,0:T(8,128)}, u32[]{:S(2)}, u32[]{:S(2)}) collective-permute-start(f32[7,3,32,128]{3,2,1,0:T(8,128)} %get-tuple-element.35), channel_id=1, source_target_pairs={{4,0},{8,4},{12,8},{16,12},{20,16},{24,20},{28,24},{32,28},{36,32}... | collective-permute-start | bytes 1032200 | tf_op jit(solution)/shard_map/ppermute | solution.py:233
  62.7 9.5 %copy-start.9 = (f32[3,16,32,128]{3,2,1,0:T(8,128)S(1)}, f32[3,16,32,128]{3,2,1,0:T(8,128)}, u32[]{:S(2)}) copy-start(f32[3,16,32,128]{3,2,1,0:T(8,128)} %param.12) | copy-start | bytes 2359300
  62.7 9.5 %copy-start.11 = (f32[3,16,32,128]{3,2,1,0:T(8,128)S(1)}, f32[3,16,32,128]{3,2,1,0:T(8,128)}, u32[]{:S(2)}) copy-start(f32[3,16,32,128]{3,2,1,0:T(8,128)} %param.11) | copy-start | bytes 2359300
  63.5 20.7 %copy-start.2 = (bf16[8192,128]{1,0:T(8,128)(2,1)S(1)}, bf16[8192,128]{1,0:T(8,128)(2,1)}, u32[]{:S(2)}) copy-start(bf16[8192,128]{1,0:T(8,128)(2,1)} %remesh_ref.3) | copy-start | bytes 6291460
  73.6 1.5 copy-start.7
  76.0 12.7 %collective-permute-start.3 = (f32[7,22,3,128]{3,2,1,0:T(4,128)}, f32[7,22,3,128]{3,2,1,0:T(4,128)S(1)}, u32[]{:S(2)}, u32[]{:S(2)}) collective-permute-start(f32[7,22,3,128]{3,2,1,0:T(4,128)} %get-tuple-element.32), channel_id=1, source_target_pairs={{1,0},{2,1},{3,2},{5,4},{6,5},{7,6},{9,8},{10,9},{11,10},{13,12},{... | collective-permute-start | bytes 709640 | tf_op jit(solution)/shard_map/ppermute | solution.py:233
  77.3 11.4 %collective-permute-start.2 = (f32[7,22,3,128]{3,2,1,0:T(4,128)}, f32[7,22,3,128]{3,2,1,0:T(4,128)S(1)}, u32[]{:S(2)}, u32[]{:S(2)}) collective-permute-start(f32[7,22,3,128]{3,2,1,0:T(4,128)} %get-tuple-element.33), channel_id=1, source_target_pairs={{0,1},{1,2},{2,3},{4,5},{5,6},{6,7},{8,9},{9,10},{10,11},{12,13},{... | collective-permute-start | bytes 709640 | tf_op jit(solution)/shard_map/ppermute | solution.py:230
  100.8 47.2 %slice-start = ((s8[9437184]{0:T(1024)(128)(4,1)}), s8[4194304]{0:T(1024)(128)(4,1)S(1)}, s32[]{:S(2)}) async-start(s8[9437184]{0:T(1024)(128)(4,1)} %bitcast.32), calls=%async_computation.3 | async-start | bytes 8388608
  100.8 40.0 %copy-start = (f32[7,22,48,128]{3,2,1,0:T(8,128)S(1)}, f32[7,22,48,128]{3,2,1,0:T(8,128)}, u32[]{:S(2)}) copy-start(f32[7,22,48,128]{3,2,1,0:T(8,128)} %concatenate.11.fields_ref) | copy-start | bytes 11354116
  100.8 40.0 %copy-start.6 = (bf16[128,128]{1,0:T(8,128)(2,1)S(1)}, bf16[128,128]{1,0:T(8,128)(2,1)}, u32[]{:S(2)}) copy-start(bf16[128,128]{1,0:T(8,128)(2,1)} %right_ref.1) | copy-start | bytes 98308
  100.8 47.1 %slice-start.1 = ((s8[9437184]{0:T(1024)(128)(4,1)}), s8[4194304]{0:T(1024)(128)(4,1)S(1)}, s32[]{:S(2)}) async-start(s8[9437184]{0:T(1024)(128)(4,1)} %bitcast.32), calls=%async_computation.4 | async-start | bytes 8388608
  100.8 47.1 %slice-start.2 = ((s8[9437184]{0:T(1024)(128)(4,1)}), s8[1048576]{0:T(1024)(128)(4,1)S(1)}, s32[]{:S(2)}) async-start(s8[9437184]{0:T(1024)(128)(4,1)} %bitcast.32), calls=%async_computation.5 | async-start | bytes 2097152
  134.4 5.4 %collective-permute-start.5 = (bf16[4,2,16,128]{3,2,1,0:T(8,128)(2,1)S(1)}, bf16[4,2,16,128]{3,2,1,0:T(8,128)(2,1)S(1)}, u32[]{:S(2)}, u32[]{:S(2)}) collective-permute-start(bf16[4,2,16,128]{3,2,1,0:T(8,128)(2,1)S(1)} %get-tuple-element.36), channel_id=1, source_target_pairs={{1,0},{2,1},{3,2},{5,4},{6,5},{7,6},{9,8},{10,9},{11,10},{13,12},{... | collective-permute-start | bytes 98312 | tf_op jit(solution)/shard_map/ppermute | solution.py:345
  135.7 5.1 %collective-permute-start.4 = (bf16[4,2,16,128]{3,2,1,0:T(8,128)(2,1)S(1)}, bf16[4,2,16,128]{3,2,1,0:T(8,128)(2,1)S(1)}, u32[]{:S(2)}, u32[]{:S(2)}) collective-permute-start(bf16[4,2,16,128]{3,2,1,0:T(8,128)(2,1)S(1)} %get-tuple-element.37), channel_id=1, source_target_pairs={{0,1},{1,2},{2,3},{4,5},{5,6},{6,7},{8,9},{9,10},{10,11},{12,13},{... | collective-permute-start | bytes 98312 | tf_op jit(solution)/shard_map/ppermute | solution.py:344
  148.0 32.7 %copy-start.4 = (bf16[128,128]{1,0:T(8,128)(2,1)S(1)}, bf16[128,128]{1,0:T(8,128)(2,1)}, u32[]{:S(2)}) copy-start(bf16[128,128]{1,0:T(8,128)(2,1)} %strengths_ref.1) | copy-start | bytes 98308
where the time goes:
time: 183 us; the launch traced here: 182 us
  blocking collectives  57.1 us (31%)
  other arithmetic  34.7 us (19%)
  starting transfers between devices  29.6 us (16%)
  local copies, waits for them, and re-layouts  22 us (12%)
  Pallas kernels  15.6 us (9%)
  matrix products  11.8 us (6%)
  waiting for transfers between devices  9.68 us (5%)
    all_to_all x1, blocking collectives, shards(): lax.all_to_all(outgoing.reshape(blocks, row_cap, EDGE), 'blk', split_axis...  30.1 us
    all_to_all x1, blocking collectives, shards(): lax.all_to_all(sums.reshape(blocks, 16, 2 * EDGE), 'blk', split_axis=0, c...  27.1 us
    optimization_barrier x2, other arithmetic, shards(): pieces, held = lax.optimization_barrier((pieces, held))  15.5 us
    all_to_all x1, starting transfers between devices, shards(): lax.all_to_all(pieces, 'blk', split_axis=0, concat_axis=0, tiled=True)  13.5 us
    concatenate x1, local copies, waits for them, and re-layouts, shards(): fields = jnp.concatenate([blank, low, fields, high, blank], axis=2)  12 us
    convert_element_type x1, other arithmetic, shards(): row_spreader = (row_slot[None, :] == jnp.arange(blocks * row_cap, dtype=j...  8.35 us
    ppermute x2, starting transfers between devices, exchanged(): lax.ppermute(lax.slice_in_dim(block, block.shape[dim] - width, None, axis...  7.53 us
    pallas_call x1, Pallas kernels, grid_update(): pl.pallas_call(grid_kernel, in_specs=[vmem] * 5, out_specs=[vmem] * 2, ou...  7.12 us
  transfers between devices with their start and end apart: 7, of which 3 were waited for; matrix products, arithmetic and copies ran while one was open for 30% of the time, Pallas kernels for 2%

commit v1 on v0

--- a/solution.py
+++ b/solution.py
@@ -53,7 +53,7 @@
         out_specs=pl.BlockSpec((64, GROUP, 2 * EDGE), lambda g: (0, g, 0)),
         out_shape=jax.ShapeDtypeStruct((64, tiles, 2 * EDGE), jnp.bfloat16),
         scratch_shapes=[pltpu.VMEM((2, 64 * GROUP, EDGE), jnp.float32)],
-        compiler_params=pltpu.CompilerParams(vmem_limit_bytes=32 * 1024 * 1024),
+        compiler_params=pltpu.CompilerParams(vmem_limit_bytes=60 * 1024 * 1024),
     )(remesh, strengths, left)
 
 
@@ -89,12 +89,176 @@
     )(index, remesh)
 
 
+def sums_kernel(quarter_ref, position_ref, arrived_ref, out_ref, picker):
+    quarter = quarter_ref[0]
+    rows = picker.shape[0]
+    row = lax.broadcasted_iota(jnp.int32, (rows, EDGE), 0)
+    block = row // 16
+    entry = row % 16
+    late = quarter >= 2
+    outer_block = jnp.where(late, block - 1, block + 1)
+    outer = outer_block * 12 + (entry - 12) * 4 + jnp.where(late, 3, 0)
+    usable = (outer_block >= 0) & (outer_block < 64) & (entry < 15)
+    wanted = jnp.where(entry < 12, block * 12 + entry, jnp.where(usable, outer, -1))
+    for chunk in range(picker.shape[1] // EDGE):
+        lanes = slice(chunk * EDGE, (chunk + 1) * EDGE)
+        picker[:, lanes] = (wanted == position_ref[:, lanes]).astype(jnp.bfloat16)
+    out_ref[...] = jnp.dot(
+        picker[...], arrived_ref[...], preferred_element_type=jnp.float32
+    ).astype(jnp.bfloat16)
+
+
+def tile_sums(quarter, position, arrived):
+    tiles = arrived.shape[0]
+    vmem = pl.BlockSpec(memory_space=pltpu.VMEM)
+    return pl.pallas_call(
+        sums_kernel,
+        in_specs=[pl.BlockSpec(memory_space=pltpu.SMEM), vmem, vmem],
+        out_specs=vmem,
+        out_shape=jax.ShapeDtypeStruct((1024, 2 * EDGE), jnp.bfloat16),
+        scratch_shapes=[pltpu.VMEM((1024, tiles), jnp.bfloat16)],
+        compiler_params=pltpu.CompilerParams(vmem_limit_bytes=40 * 1024 * 1024),
+    )(quarter, position, arrived)
+
+
+def widen_kernel(velocity_ref, stretch_ref, coupling_ref, low_ref, high_ref, ext_ref, last_ref, first_ref):
+    span = 32
+    wide = span + 2 * SIDE
+    source = [velocity_ref.at[c] for c in range(3)] + [stretch_ref.at[d] for d in range(3)]
+    source.append(coupling_ref)
+    for f in range(7):
+
+        def one(layer, carry, f=f):
+            ext_ref[f, layer, 0:SIDE, :] = jnp.zeros((SIDE, EDGE), jnp.float32)
+            ext_ref[f, layer, SIDE + span : wide, :] = jnp.zeros((SIDE, EDGE), jnp.float32)
+            ext_ref[f, layer, SIDE - REACH : SIDE, :] = low_ref[f, layer]
+            ext_ref[f, layer, SIDE + span : SIDE + span + REACH, :] = high_ref[f, layer]
+            ext_ref[f, layer, SIDE : SIDE + span, :] = source[f][layer]
+            return carry
+
+        lax.fori_loop(0, 16, one, 0)
+    for f in range(7):
+        depth = 3 if f < 3 else 2
+        at = 3 * f if f < 3 else 9 + 2 * (f - 3)
+        for k in range(depth):
+            last_ref[at + k] = ext_ref[f, 16 - depth + k, 4 : wide - 4, :]
+            first_ref[at + k] = ext_ref[f, k, 4 : wide - 4, :]
+
+
+def widened(velocity, stretch, coupling, low, high):
+    wide = 32 + 2 * SIDE
+    vmem = pl.BlockSpec(memory_space=pltpu.VMEM)
+    return pl.pallas_call(
+        widen_kernel,
+        in_specs=[vmem] * 5,
+        out_specs=[vmem] * 3,
+        out_shape=[
+            jax.ShapeDtypeStruct((7, 16, wide, EDGE), jnp.float32),
+            jax.ShapeDtypeStruct((17, wide - 8, EDGE), jnp.float32),
+            jax.ShapeDtypeStruct((17, wide - 8, EDGE), jnp.float32),
+        ],
+        compiler_params=pltpu.CompilerParams(vmem_limit_bytes=32 * 1024 * 1024),
+    )(velocity, stretch, coupling, low, high)
+
+
+def moved(value, direction):
+    wide = value.shape[0]
+    if direction == 1:
+        return pltpu.roll(value, wide - 1, 0), pltpu.roll(value, 1, 0)
+    lanes = lax.broadcasted_iota(jnp.int32, value.shape, 1)
+    ahead = jnp.where(lanes < EDGE - 1, pltpu.roll(value, EDGE - 1, 1), 0.0)
+    behind = jnp.where(lanes > 0, pltpu.roll(value, 1, 1), 0.0)
+    return ahead, behind
+
+
+def unforced(source, at, stretch, rate):
+    centre = [source[c, at] for c in range(3)]
+    squares = [(step_size * viscosity) * s * s for s in stretch]
+    carried = [(0.5 * step_size) * s * u for s, u in zip(stretch, centre)]
+    results = []
+    for c in range(3):
+        value = centre[c]
+        twice = 2.0 * value
+        change = value - rate * value
+        for d in range(3):
+            if d == 0:
+                ahead, behind = source[c, at + 1], source[c, at - 1]
+            else:
+                ahead, behind = moved(value, d)
+            change = change + squares[d] * (ahead + behind - twice)
+            change = change - carried[d] * (ahead - behind)
+        results.append(change)
+    return results
+
+
+def prepare_kernel(ext_ref, low_ref, high_ref, base_ref, stretch_ref, rate_ref, wide_velocity):
+    span = 32
+    wide = span + 2 * SIDE
+    blank = jnp.zeros((4, EDGE), jnp.float32)
+
+    def padded(slab):
+        return jnp.concatenate([blank, slab, blank], axis=0)
+
+    for c in range(3):
+        for k in range(3):
+            wide_velocity[c, k] = padded(low_ref[3 * c + k])
+            wide_velocity[c, 19 + k] = padded(high_ref[3 * c + k])
+    for d in range(3):
+        for k in range(2):
+            stretch_ref[d, k] = padded(low_ref[9 + 2 * d + k])
+            stretch_ref[d, 18 + k] = padded(high_ref[9 + 2 * d + k])
+    for k in range(2):
+        rate_ref[k] = padded(low_ref[15 + k])
+        rate_ref[18 + k] = padded(high_ref[15 + k])
+
+    def inner(layer, carry):
+        for c in range(3):
+            wide_velocity[c, layer + 3] = ext_ref[c, layer]
+            stretch_ref[c, layer + 2] = ext_ref[3 + c, layer]
+        rate_ref[layer + 2] = ext_ref[6, layer]
+        return carry
+
+    lax.fori_loop(0, 16, inner, 0)
+
+    def step(layer, carry):
+        results = unforced(
+            wide_velocity, layer + 1, [stretch_ref[d, layer] for d in range(3)], rate_ref[layer]
+        )
+        for c in range(3):
+            base_ref[c, layer] = results[c]
+        return carry
+
+    lax.fori_loop(0, 20, step, 0)
+
+
+def prepared(ext, low, high):
+    wide = 32 + 2 * SIDE
+    vmem = pl.BlockSpec(memory_space=pltpu.VMEM)
+    return pl.pallas_call(
+        prepare_kernel,
+        in_specs=[vmem] * 3,
+        out_specs=[vmem] * 3,
+        out_shape=[
+            jax.ShapeDtypeStruct((3, 20, wide, EDGE), jnp.float32),
+            jax.ShapeDtypeStruct((3, 20, wide, EDGE), jnp.float32),
+            jax.ShapeDtypeStruct((20, wide, EDGE), jnp.float32),
+        ],
+        scratch_shapes=[pltpu.VMEM((3, 22, wide, EDGE), jnp.float32)],
+        compiler_params=pltpu.CompilerParams(vmem_limit_bytes=32 * 1024 * 1024),
+        cost_estimate=pl.CostEstimate(
+            flops=30 * 1000 * 1000, bytes_accessed=8 * 1024 * 1024, transcendentals=0
+        ),
+    )(ext, low, high)
+
+
 def grid_kernel(
     sums_ref,
     low_ref,
     high_ref,
     right_ref,
-    fields_ref,
+    base_ref,
+    stretch_ref,
+    rate_ref,
     next_ref,
     rows_ref,
     centre_sums,
@@ -128,65 +292,34 @@
                 1, pl.ds(quarter * 32 + entry, 2, stride=16), :
             ]
 
-    lanes = lax.broadcasted_iota(jnp.int32, (wide, EDGE), 1)
-    not_last = lanes < EDGE - 1
-    not_first = lanes > 0
-
-    def after(value, direction):
-        if direction == 1:
-            return pltpu.roll(value, wide - 1, 0)
-        return jnp.where(not_last, pltpu.roll(value, EDGE - 1, 1), 0.0)
-
-    def before(value, direction):
-        if direction == 1:
-            return pltpu.roll(value, 1, 0)
-        return jnp.where(not_first, pltpu.roll(value, 1, 1), 0.0)
-
-    def advanced(source, at, layer, target_layer):
-        centre = [source[c, at] for c in range(3)]
-        stretch = [fields_ref[3 + d, layer] for d in range(3)]
-        rate = fields_ref[6, layer]
-        squares = [(step_size * viscosity) * s * s for s in stretch]
-        carried = [(0.5 * step_size) * s * u for s, u in zip(stretch, centre)]
-        results = []
+    def first_step(layer, carry):
+        rate = rate_ref[layer]
         for c in range(3):
-            value = centre[c]
-            twice = 2.0 * value
-            change = rate * (target[c, target_layer] - value)
-            for d in range(3):
-                if d == 0:
-                    ahead, behind = source[c, at + 1], source[c, at - 1]
-                else:
-                    ahead, behind = after(value, d), before(value, d)
-                change = change + squares[d] * (ahead + behind - twice)
-                change = change - carried[d] * (ahead - behind)
-            results.append(value + change)
-        return results
-
-    def first_step(layer, carry):
-        results = advanced(fields_ref, layer + 1, layer + 1, layer)
+            first[c, layer] = base_ref[c, layer] + rate * target[c, layer]
+        return carry
+
+    lax.fori_loop(0, 20, first_step, 0)
+
+    def second_step(layer, carry):
+        rate = rate_ref[layer + 1]
+        results = unforced(
+            first, layer + 1, [stretch_ref[d, layer + 1] for d in range(3)], rate
+        )
         for c in range(3):
-            first[c, layer] = results[c]
-        return carry
-
-    lax.fori_loop(0, 20, first_step, 0)
-
-    def second_step(layer, carry):
-        results = advanced(first, layer + 1, layer + 2, layer + 1)
-        for c in range(3):
-            second[c, layer] = results[c]
+            second[c, layer] = results[c] + rate * target[c, layer + 1]
         return carry
 
     lax.fori_loop(0, 18, second_step, 0)
 
     def curl(layer, carry):
         centre = [second[c, layer + 1] for c in range(3)]
-        half = [0.5 * fields_ref[3 + d, layer + 3] for d in range(3)]
+        half = [0.5 * stretch_ref[d, layer + 2] for d in range(3)]
 
         def slope(d, c):
             if d == 0:
                 return half[0] * (second[c, layer + 2] - second[c, layer])
-            return half[d] * (after(centre[c], d) - before(centre[c], d))
+            ahead, behind = moved(centre[c], d)
+            return half[d] * (ahead - behind)
 
         parts = (
             slope(1, 2) - slope(2, 1),
@@ -201,12 +334,12 @@
     lax.fori_loop(0, 16, curl, 0)
 
 
-def grid_update(sums, low, high, right, fields):
+def grid_update(sums, low, high, right, base, stretch, rate):
     wide = 32 + 2 * SIDE
     vmem = pl.BlockSpec(memory_space=pltpu.VMEM)
     return pl.pallas_call(
         grid_kernel,
-        in_specs=[vmem] * 5,
+        in_specs=[vmem] * 7,
         out_specs=[vmem] * 2,
         out_shape=[
             jax.ShapeDtypeStruct((3, 16, 32, EDGE), jnp.float32),
@@ -219,19 +352,13 @@
             pltpu.VMEM((3, 20, wide, EDGE), jnp.float32),
             pltpu.VMEM((3, 18, wide, EDGE), jnp.float32),
         ],
-        compiler_params=pltpu.CompilerParams(vmem_limit_bytes=40 * 1024 * 1024),
-    )(sums, low, high, right, fields)
-
-
-def exchanged(block, axis, dim, width):
-    count = lax.axis_size(axis)
+        compiler_params=pltpu.CompilerParams(vmem_limit_bytes=32 * 1024 * 1024),
+    )(sums, low, high, right, base, stretch, rate)
+
+
+def chain(count):
     forward = [(i, i + 1) for i in range(count - 1)]
-    backward = [(target, source) for source, target in forward]
-    low = lax.ppermute(
-        lax.slice_in_dim(block, block.shape[dim] - width, None, axis=dim), axis, forward
-    )
-    high = lax.ppermute(lax.slice_in_dim(block, 0, width, axis=dim), axis, backward)
-    return low, high
+    return forward, [(target, source) for source, target in forward]
 
 
 def slot_ranks(destination, block_count):
@@ -294,32 +421,34 @@
     arrived = lax.all_to_all(pieces, "blk", split_axis=0, concat_axis=0, tiled=True)
 
     def mine(values, count):
-        return lax.dynamic_index_in_dim(
-            values.reshape(blocks, spans, count), my_span, 1, keepdims=False
-        )
-
-    owners = mine(tile_owner, tile_count).reshape(-1)
-    places = mine(tile_place, tile_count).reshape(-1)
+        rows = values.reshape(blocks, spans * count // EDGE, EDGE)
+        if count >= EDGE:
+            part = lax.dynamic_slice_in_dim(
+                rows, my_span * (count // EDGE), count // EDGE, axis=1
+            )
+            return part.reshape(blocks, count)
+        whole = rows.reshape(blocks, spans, count)
+        return lax.dynamic_index_in_dim(whole, my_span, 1, keepdims=False)
+
+    owners = mine(tile_owner.T, tile_count).reshape(1, -1)
+    places = mine(tile_place, tile_count).reshape(1, -1)
     position = owners * 12 + places
-    entry = jnp.arange(16, dtype=jnp.int32)[None, :]
-    block = jnp.arange(blocks, dtype=jnp.int32)[:, None]
-    quarter = my_block // 16
-    outer = jnp.where(
-        quarter >= 2, (block - 1) * 12 + (entry - 12) * 4 + 3, (block + 1) * 12 + (entry - 12) * 4
-    )
-    outer_block = jnp.where(quarter >= 2, block - 1, block + 1)
-    outer = jnp.where((outer_block >= 0) & (outer_block < blocks) & (entry < 15), outer, -1)
-    wanted = jnp.where(entry < 12, block * 12 + entry, outer).reshape(-1)
-    tile_picker = (wanted[:, None] == position[None, :]).astype(jnp.bfloat16)
-
-    fields = jnp.concatenate([velocity, stretch, coupling[None]], axis=0)
-    low, high = exchanged(fields, "blk", 1, REACH)
-    fields = jnp.concatenate([low, fields, high], axis=1)
-    low, high = exchanged(fields, "span", 2, REACH)
-    blank = jnp.zeros(fields.shape[:2] + (SIDE - REACH, EDGE), fields.dtype)
-    fields = jnp.concatenate([blank, low, fields, high, blank], axis=2)
-
-    destinations = mine(row_dest, grid_count)
+    quarter = jnp.reshape(my_block // 16, (1,)).astype(jnp.int32)
+
+    forward, backward = chain(spans)
+    fields = (velocity, stretch, coupling[None])
+    low = lax.ppermute(
+        jnp.concatenate([f[:, :, -REACH:] for f in fields], axis=0), "span", forward
+    )
+    high = lax.ppermute(
+        jnp.concatenate([f[:, :, :REACH] for f in fields], axis=0), "span", backward
+    )
+    extended, last, opening = widened(velocity, stretch, coupling, low, high)
+    block_forward, block_backward = chain(blocks)
+    low = lax.ppermute(last, "blk", block_forward)
+    high = lax.ppermute(opening, "blk", block_backward)
+
+    destinations = mine(row_dest.T, grid_count)
     row_places = mine(row_place, grid_count)
     dest_mine = lax.dynamic_index_in_dim(destinations, my_block, 0, keepdims=False)
     row_slot = dest_mine * row_cap + slot_ranks(dest_mine, blocks)
@@ -329,18 +458,16 @@
     row_where = arrival_places(destinations, row_places, my_block, row_cap)
     remesh_rows = gathered_rows(row_where, remesh)
 
-    arrived, tile_picker, fields, row_spreader, remesh_rows = lax.optimization_barrier(
-        (arrived, tile_picker, fields, row_spreader, remesh_rows)
-    )
-    sums = jnp.dot(
-        tile_picker, arrived.reshape(-1, 2 * EDGE), preferred_element_type=jnp.float32
-    ).astype(jnp.bfloat16)
+    arrived, position, row_spreader, remesh_rows = lax.optimization_barrier(
+        (arrived, position, row_spreader, remesh_rows)
+    )
+    sums = tile_sums(quarter, position, arrived.reshape(-1, 2 * EDGE))
+    sums, extended, low, high = lax.optimization_barrier((sums, extended, low, high))
+    base, wide_stretch, rate = prepared(extended, low, high)
     sums = lax.all_to_all(
         sums.reshape(blocks, 16, 2 * EDGE), "blk", split_axis=0, concat_axis=0, tiled=True
     )
     split = sums.reshape(4, 16, 16, 2 * EDGE)
-    forward = [(i, i + 1) for i in range(spans - 1)]
-    backward = [(i + 1, i) for i in range(spans - 1)]
     low = lax.ppermute(split[:, 14:16, :, EDGE:], "span", forward)
     high = lax.ppermute(split[:, 0:2, :, :EDGE], "span", backward)
     current, vorticity = grid_update(
@@ -348,7 +475,9 @@
         low.reshape(-1, EDGE),
         high.reshape(-1, EDGE),
         green_right,
-        fields,
+        base,
+        wide_stretch,
+        rate,
     )
     outgoing = jnp.dot(
         row_spreader, vorticity.reshape(grid_count, EDGE), preferred_element_type=jnp.float32

time: 183 us -> 150 us (0.82)
  other arithmetic: 34.7 us -> 13.6 us
  local copies, waits for them, and re-layouts: 22 us -> 5.35 us
  Pallas kernels: 15.6 us -> 25.7 us
  blocking collectives: 57.1 us -> 53 us
  waiting for transfers between devices: 9.68 us -> 11.9 us
    optimization_barrier x2 -> x1, other arithmetic: 15.5 us -> 0.81 us  [shards(): pieces, held = lax.optimization_barrier((pieces, held))]
    concatenate x1 -> x0, local copies, waits for them, and re-layouts: 12 us -> none  [shards(): fields = jnp.concatenate([blank, low, fields, high, blank], axis=2)]
    all_to_all x1, waiting for transfers between devices: 0.01 us -> 11.9 us  [shards(): lax.all_to_all(pieces, 'blk', split_axis=0, concat_axis=0, tiled=True)]
    ppermute x4, waiting for transfers between devices: 8.68 us -> 0.01 us  [the longest x1 0.01 us: shards(): lax.ppermute(jnp.concatenate([f[:, :, -REACH:] for f in fields], axis=0),...]
    pallas_call x1 -> x4, Pallas kernels: 7.12 us -> 15.8 us  [the longest x1 5.13 us: grid_update(): pl.pallas_call(grid_kernel, in_specs=[vmem] * 7, out_specs=[vmem] * 2, ou...]
    dot_general x1 -> x0, matrix products: 6.45 us -> none  [shards(): jnp.dot(tile_picker, arrived.reshape(-1, 2 * EDGE), preferred_element_typ...]
    convert_element_type x1, other arithmetic: 5.54 us -> 0.01 us  [slot_ranks(): jnp.sum(before * one_hot.astype(jnp.float32), axis=1).astype(jnp.int32)]
    all_to_all x1, blocking collectives: 27.1 us -> 22.7 us  [shards(): lax.all_to_all(sums.reshape(blocks, 16, 2 * EDGE), 'blk', split_axis=0, c...]
  transfers between devices with their start and end apart: 7 -> 7, of which waited for: 3 -> 1; matrix products, arithmetic and copies ran while one was open for 30% -> 14% of each run, Pallas kernels for 2% -> 10%
where the time goes in v1:
time: 150 us; the launch traced here: 149 us
  blocking collectives  53 us (35%)
  starting transfers between devices  28 us (19%)
  Pallas kernels  25.7 us (17%)
  other arithmetic  13.6 us (9%)
  waiting for transfers between devices  11.9 us (8%)
  matrix products  10.3 us (7%)
  local copies, waits for them, and re-layouts  5.35 us (4%)
    all_to_all x1, blocking collectives, shards(): lax.all_to_all(outgoing.reshape(blocks, row_cap, EDGE), 'blk', split_axis...  30.3 us
    all_to_all x1, blocking collectives, shards(): lax.all_to_all(sums.reshape(blocks, 16, 2 * EDGE), 'blk', split_axis=0, c...  22.7 us
    all_to_all x1, starting transfers between devices, shards(): lax.all_to_all(pieces, 'blk', split_axis=0, concat_axis=0, tiled=True)  13.3 us
    all_to_all x1, waiting for transfers between devices, shards(): lax.all_to_all(pieces, 'blk', split_axis=0, concat_axis=0, tiled=True)  11.9 us
    convert_element_type x1, other arithmetic, shards(): row_spreader = (row_slot[None, :] == jnp.arange(blocks * row_cap, dtype=j...  8.32 us
    dot_general x1, matrix products, shards(): jnp.dot(row_spreader, vorticity.reshape(grid_count, EDGE), preferred_elem...  6.3 us
    pallas_call x1, Pallas kernels, tile_pieces(): pl.pallas_call(pieces_kernel, grid=(tiles // GROUP,), in_specs=[pl.BlockS...  5.55 us
    pallas_call x1, Pallas kernels, grid_update(): pl.pallas_call(grid_kernel, in_specs=[vmem] * 7, out_specs=[vmem] * 2, ou...  5.13 us
  transfers between devices with their start and end apart: 7, of which 1 were waited for; matrix products, arithmetic and copies ran while one was open for 14% of the time, Pallas kernels for 10%

profile of v1, /device:TPU:1, one launch (start us, length us, event | category | flops | bytes accessed | tf_op | source)
XLA Modules:
  0.0 149.0 jit_solution(13458231712951133085)
XLA Ops:
  0.6 5.5 %shard_map.122 = bf16[64,64,256]{2,1,0:T(8,128)(2,1)} custom-call(bf16[8192,128]{1,0:T(8,128)(2,1)} %remesh_ref.3, bf16[128,128]{1,0:T(8,128)(2,1)} %strengths_ref.1, bf16[128,128]{1,0:T(8,128)(2,1)} %left_ref.1), custom_call_target="tpu_custom_call" | custom-call | tf_op jit(solution)/shard_map/pallas_call | solution.py:45
  6.2 13.3 %all-to-all-start = ((bf16[64,64,256]{2,1,0:T(8,128)(2,1)}), bf16[64,64,256]{2,1,0:T(8,128)(2,1)}, u32[]{:S(2)}, u32[]{:S(2)}) async-start(bf16[64,64,256]{2,1,0:T(8,128)(2,1)} %shard_map.122), calls=%async_computation | async-start | bytes 4194304 | tf_op jit(solution)/shard_map/all_to_all | solution.py:421
  19.6 1.1 fusion.12
  20.7 0.7 pad_maximum_fusion
  21.5 3.1 %collective-permute-start = (f32[7,16,3,128]{3,2,1,0:T(4,128)}, f32[7,16,3,128]{3,2,1,0:T(4,128)S(1)}, u32[]{:S(2)}, u32[]{:S(2)}) collective-permute-start(f32[7,16,3,128]{3,2,1,0:T(4,128)} %pad_maximum_fusion), channel_id=1, source_target_pairs={{0,1},{1,2},{2,3},{4,5},{5,6},{6,7},{8,9},{9,10},{10,11},{12,13},{... | collective-permute-start | bytes 516104 | tf_op jit(solution)/shard_map/ppermute | solution.py:440
  24.6 0.8 pad_maximum_fusion.1
  25.3 1.3 collective-permute-start.1
  26.6 1.5 %constant_dynamic-slice_fusion = (s32[64,12,128]{2,1,0:T(8,128)S(1)}, s32[64,12,128]{2,1,0:T(8,128)S(1)}) fusion(s32[64,48,128]{2,1,0:T(8,128)} %bitcast.41, s32[]{:T(128)S(6)} %select_n.28, s32[64,48,128]{2,1,0:T(8,128)} %bitcast.42), kind=kLoop, calls=%fused_computation.27 | loop fusion | bytes 1572868 | tf_op jit(solution)/shard_map/dynamic_slice | solution.py:426
  28.1 0.1 copy.19
  28.3 1.0 fusion.6
  29.4 0.1 copy.18
  29.6 8.3 %fusion = bf16[3072,1536]{1,0:T(8,128)(2,1)} fusion(s32[1536]{0:T(1024)S(1)} %add_reduce_fusion.1), kind=kLoop, calls=%fused_computation.3 | loop fusion | flops 9437184 | bytes 9443328 | tf_op jit(solution)/shard_map/convert_element_type | solution.py:457
  37.9 2.0 %fusion.5 = s32[64,1536]{1,0:T(8,128)S(1)} fusion(s32[64,1536]{1,0:T(8,128)} %bitcast.40, s32[]{:T(128)S(6)} %axis_index.23), kind=kOutput, calls=%fused_computation.11 | convolution fusion | flops 304742400 | bytes 786436 | tf_op jit(solution)/shard_map/dot_general | solution.py:380
  39.9 2.7 %shard_map.125 = (f32[7,16,48,128]{3,2,1,0:T(8,128)S(1)}, f32[17,40,128]{2,1,0:T(8,128)}, f32[17,40,128]{2,1,0:T(8,128)}) custom-call(f32[3,16,32,128]{3,2,1,0:T(8,128)S(1)} %copy-done.3, f32[3,16,32,128]{3,2,1,0:T(8,128)S(1)} %copy-done.4, f32[16,32,128]{2,1,0:T(8,128)S(1)} %copy-done.5, f32[7,16,3,128]{3,2,1,0:T(4,128)S(1)} %collective-permute-done.low_ref, ...), custom_call_target="tpu_custom_call" | custom-call | tf_op jit(solution)/shard_map/pallas_call | solution.py:151
  42.6 1.5 %copy-done.1 = f32[7,16,48,128]{3,2,1,0:T(8,128)} copy-done((f32[7,16,48,128]{3,2,1,0:T(8,128)}, f32[7,16,48,128]{3,2,1,0:T(8,128)S(1)}, u32[]{:S(2)}) %copy-start.1) | copy-done | bytes 2752536
  44.1 3.8 %collective-permute-start.2 = (f32[17,40,128]{2,1,0:T(8,128)}, f32[17,40,128]{2,1,0:T(8,128)S(1)}, u32[]{:S(2)}, u32[]{:S(2)}) collective-permute-start(f32[17,40,128]{2,1,0:T(8,128)} %get-tuple-element.37), channel_id=1, source_target_pairs={{0,4},{4,8},{8,12},{12,16},{16,20},{20,24},{24,28},{28,32},{32,36}... | collective-permute-start | bytes 1044488 | tf_op jit(solution)/shard_map/ppermute | solution.py:448
  47.9 2.1 %collective-permute-start.3 = (f32[17,40,128]{2,1,0:T(8,128)}, f32[17,40,128]{2,1,0:T(8,128)}, u32[]{:S(2)}, u32[]{:S(2)}) collective-permute-start(f32[17,40,128]{2,1,0:T(8,128)} %get-tuple-element.38), channel_id=1, source_target_pairs={{4,0},{8,4},{12,8},{16,12},{20,16},{24,20},{28,24},{32,28},{36,32}... | collective-permute-start | bytes 1044488 | tf_op jit(solution)/shard_map/ppermute | solution.py:449
  50.0 2.8 %select_reduce_fusion = s32[64,48]{1,0:T(8,128)S(1)} fusion(s32[64,1536]{1,0:T(8,128)S(1)} %bitcast.36, s32[64,1536]{1,0:T(8,128)S(1)} %fusion.5), kind=kLoop, calls=%fused_computation | loop fusion | flops 14152704 | bytes 798720 | tf_op jit(solution)/shard_map/reduce_sum | solution.py:385
  52.9 4.3 %shard_map.123 = bf16[3072,128]{1,0:T(8,128)(2,1)S(1)} custom-call(s32[3072]{0:T(1024)S(1)} %reshape.89.index_ref, bf16[8192,128]{1,0:T(8,128)(2,1)S(1)} %copy-done), custom_call_target="tpu_custom_call" | custom-call | bytes 16777216 | tf_op jit(solution)/shard_map/pallas_call | solution.py:75
  57.3 0.5 broadcast.26
  57.8 0.8 reduce.11
  58.8 0.1 add_reduce_fusion
  59.1 11.9 %all-to-all-done = bf16[64,64,256]{2,1,0:T(8,128)(2,1)} async-done(((bf16[64,64,256]{2,1,0:T(8,128)(2,1)}), bf16[64,64,256]{2,1,0:T(8,128)(2,1)}, u32[]{:S(2)}, u32[]{:S(2)}) %all-to-all-start) | async-done | bytes 2097184 | tf_op jit(solution)/shard_map/all_to_all | solution.py:421
  70.9 4.5 %shard_map.124 = bf16[1024,256]{1,0:T(8,128)(2,1)S(1)} custom-call(s32[1]{0:T(128)} %bitcast.quarter_ref, s32[1,4096]{1,0:T(1,128)S(1)} %add.38.position_ref, bf16[4096,256]{1,0:T(8,128)(2,1)} %bitcast.3.arrived_ref), custom_call_target="tpu_custom_call" | custom-call | tf_op jit(solution)/shard_map/pallas_call | solution.py:114
  75.5 22.7 %all_to_all.15 = bf16[64,16,256]{2,1,0:T(8,128)(2,1)S(1)} all-to-all(bf16[64,16,256]{2,1,0:T(8,128)(2,1)S(1)} %bitcast.28), channel_id=1, replica_groups=mesh['blk'=64,'span'=4] {'blk'}, dimensions={0} | all-to-all | bytes 1048576 | tf_op jit(solution)/shard_map/all_to_all | solution.py:467
  98.2 3.1 %collective-permute-start.4 = (bf16[4,2,16,128]{3,2,1,0:T(8,128)(2,1)S(1)}, bf16[4,2,16,128]{3,2,1,0:T(8,128)(2,1)S(1)}, u32[]{:S(2)}, u32[]{:S(2)}) collective-permute-start(bf16[4,2,16,128]{3,2,1,0:T(8,128)(2,1)S(1)} %get-tuple-element.55), channel_id=1, source_target_pairs={{0,1},{1,2},{2,3},{4,5},{5,6},{6,7},{8,9},{9,10},{10,11},{12,13},{... | collective-permute-start | bytes 98312 | tf_op jit(solution)/shard_map/ppermute | solution.py:471
  101.3 1.3 collective-permute-start.5
  102.6 3.5 %shard_map.126 = (f32[3,20,48,128]{3,2,1,0:T(8,128)S(1)}, f32[3,20,48,128]{3,2,1,0:T(8,128)S(1)}, f32[20,48,128]{2,1,0:T(8,128)S(1)}) custom-call(f32[7,16,48,128]{3,2,1,0:T(8,128)S(1)} %copy-done.2, f32[17,40,128]{2,1,0:T(8,128)S(1)} %collective-permute-done.2.low_ref, f32[17,40,128]{2,1,0:T(8,128)} %collective-permute-done.3.high_ref), custom_call_target="tpu_custom_call" | custom-call | flops 30000000 | bytes 8388608 | tf_op jit(solution)/shard_map/pallas_call | solution.py:237
  106.1 5.1 %shard_map.127 = (f32[3,16,32,128]{3,2,1,0:T(8,128)}, bf16[3,16,32,128]{3,2,1,0:T(8,128)(2,1)S(1)}) custom-call(bf16[1024,256]{1,0:T(8,128)(2,1)S(1)} %bitcast.27, bf16[128,128]{1,0:T(8,128)(2,1)S(1)} %bitcast.30, bf16[128,128]{1,0:T(8,128)(2,1)S(1)} %bitcast.31, bf16[128,128]{1,0:T(8,128)(2,1)S(1)} %copy-done.6, ...), custom_call_target="tpu_custom_call" | custom-call | tf_op jit(solution)/shard_map/pallas_call | solution.py:340
  111.3 6.3 %convolution_convert_fusion = bf16[3072,128]{1,0:T(8,128)(2,1)S(1)} fusion(bf16[3072,1536]{1,0:T(8,128)(2,1)} %fusion, bf16[1536,128]{1,0:T(8,128)(2,1)S(1)} %bitcast.32), kind=kOutput, calls=%fused_computation.8 | convolution fusion | flops 1208352768 | bytes 10616832 | tf_op jit(solution)/shard_map/dot_general | solution.py:482
  117.6 30.3 %all_to_all.16 = bf16[64,48,128]{2,1,0:T(8,128)(2,1)S(1)} all-to-all(bf16[64,48,128]{2,1,0:T(8,128)(2,1)S(1)} %bitcast.37), channel_id=1, replica_groups=mesh['blk'=64,'span'=4] {'blk'}, dimensions={0} | all-to-all | bytes 1572864 | tf_op jit(solution)/shard_map/all_to_all | solution.py:485
  147.9 1.1 fusion.7
  (36 shorter events, 0.5 us)
Async XLA Ops:
  0.6 19.0 %copy-start.3 = (f32[3,16,32,128]{3,2,1,0:T(8,128)S(1)}, f32[3,16,32,128]{3,2,1,0:T(8,128)}, u32[]{:S(2)}) copy-start(f32[3,16,32,128]{3,2,1,0:T(8,128)} %velocity_ref) | copy-start | bytes 2359300
  0.6 18.9 %copy-start.5 = (f32[16,32,128]{2,1,0:T(8,128)S(1)}, f32[16,32,128]{2,1,0:T(8,128)}, u32[]{:S(2)}) copy-start(f32[16,32,128]{2,1,0:T(8,128)} %coupling_ref) | copy-start | bytes 786436
  6.2 64.7 %all-to-all-start = ((bf16[64,64,256]{2,1,0:T(8,128)(2,1)}), bf16[64,64,256]{2,1,0:T(8,128)(2,1)}, u32[]{:S(2)}, u32[]{:S(2)}) async-start(bf16[64,64,256]{2,1,0:T(8,128)(2,1)} %shard_map.122), calls=%async_computation | async-start | bytes 4194304 | tf_op jit(solution)/shard_map/all_to_all | solution.py:421
  21.5 18.4 %collective-permute-start = (f32[7,16,3,128]{3,2,1,0:T(4,128)}, f32[7,16,3,128]{3,2,1,0:T(4,128)S(1)}, u32[]{:S(2)}, u32[]{:S(2)}) collective-permute-start(f32[7,16,3,128]{3,2,1,0:T(4,128)} %pad_maximum_fusion), channel_id=1, source_target_pairs={{0,1},{1,2},{2,3},{4,5},{5,6},{6,7},{8,9},{9,10},{10,11},{12,13},{... | collective-permute-start | bytes 516104 | tf_op jit(solution)/shard_map/ppermute | solution.py:440
  25.3 14.5 %collective-permute-start.1 = (f32[7,16,3,128]{3,2,1,0:T(4,128)}, f32[7,16,3,128]{3,2,1,0:T(4,128)}, u32[]{:S(2)}, u32[]{:S(2)}) collective-permute-start(f32[7,16,3,128]{3,2,1,0:T(4,128)} %pad_maximum_fusion.1), channel_id=1, source_target_pairs={{1,0},{2,1},{3,2},{5,4},{6,5},{7,6},{9,8},{10,9},{11,10},{13,12},{... | collective-permute-start | bytes 516104 | tf_op jit(solution)/shard_map/ppermute | solution.py:443
  28.3 1.3 copy-start.7
  29.5 10.3 %copy-start.4 = (f32[3,16,32,128]{3,2,1,0:T(8,128)S(1)}, f32[3,16,32,128]{3,2,1,0:T(8,128)}, u32[]{:S(2)}) copy-start(f32[3,16,32,128]{3,2,1,0:T(8,128)} %stretch_ref) | copy-start | bytes 2359300
  37.9 15.0 %copy-start = (bf16[8192,128]{1,0:T(8,128)(2,1)S(1)}, bf16[8192,128]{1,0:T(8,128)(2,1)}, u32[]{:S(2)}) copy-start(bf16[8192,128]{1,0:T(8,128)(2,1)} %remesh_ref.3) | copy-start | bytes 6291460
  37.9 19.9 %copy-start.10 = (s32[16384,1]{0,1:T(1,128)S(1)}, s32[16384,1]{0,1:T(1,128)}, u32[]{:S(2)}) copy-start(s32[16384,1]{0,1:T(1,128)} %param.18) | copy-start | bytes 196612
  37.9 20.8 %copy-start.9 = (s32[16384]{0:T(1024)S(1)}, s32[16384]{0:T(1024)}, u32[]{:S(2)}) copy-start(s32[16384]{0:T(1024)} %param.19) | copy-start | bytes 196612
  42.6 1.5 %copy-start.1 = (f32[7,16,48,128]{3,2,1,0:T(8,128)}, f32[7,16,48,128]{3,2,1,0:T(8,128)S(1)}, u32[]{:S(2)}) copy-start(f32[7,16,48,128]{3,2,1,0:T(8,128)S(1)} %get-tuple-element.40.ext_ref) | copy-start | bytes 8257540
  44.1 31.4 %collective-permute-start.2 = (f32[17,40,128]{2,1,0:T(8,128)}, f32[17,40,128]{2,1,0:T(8,128)S(1)}, u32[]{:S(2)}, u32[]{:S(2)}) collective-permute-start(f32[17,40,128]{2,1,0:T(8,128)} %get-tuple-element.37), channel_id=1, source_target_pairs={{0,4},{4,8},{8,12},{12,16},{16,20},{20,24},{24,28},{28,32},{32,36}... | collective-permute-start | bytes 1044488 | tf_op jit(solution)/shard_map/ppermute | solution.py:448
  47.9 27.6 %collective-permute-start.3 = (f32[17,40,128]{2,1,0:T(8,128)}, f32[17,40,128]{2,1,0:T(8,128)}, u32[]{:S(2)}, u32[]{:S(2)}) collective-permute-start(f32[17,40,128]{2,1,0:T(8,128)} %get-tuple-element.38), channel_id=1, source_target_pairs={{4,0},{8,4},{12,8},{16,12},{20,16},{24,20},{28,24},{32,28},{36,32}... | collective-permute-start | bytes 1044488 | tf_op jit(solution)/shard_map/ppermute | solution.py:449
  57.2 48.9 %copy-start.6 = (bf16[128,128]{1,0:T(8,128)(2,1)S(1)}, bf16[128,128]{1,0:T(8,128)(2,1)}, u32[]{:S(2)}) copy-start(bf16[128,128]{1,0:T(8,128)(2,1)} %right_ref.1) | copy-start | bytes 98308
  70.9 31.7 %copy-start.2 = (f32[7,16,48,128]{3,2,1,0:T(8,128)S(1)}, f32[7,16,48,128]{3,2,1,0:T(8,128)}, u32[]{:S(2)}) copy-start(f32[7,16,48,128]{3,2,1,0:T(8,128)} %copy-done.1) | copy-start | bytes 8257540
  98.2 7.9 %collective-permute-start.4 = (bf16[4,2,16,128]{3,2,1,0:T(8,128)(2,1)S(1)}, bf16[4,2,16,128]{3,2,1,0:T(8,128)(2,1)S(1)}, u32[]{:S(2)}, u32[]{:S(2)}) collective-permute-start(bf16[4,2,16,128]{3,2,1,0:T(8,128)(2,1)S(1)} %get-tuple-element.55), channel_id=1, source_target_pairs={{0,1},{1,2},{2,3},{4,5},{5,6},{6,7},{8,9},{9,10},{10,11},{12,13},{... | collective-permute-start | bytes 98312 | tf_op jit(solution)/shard_map/ppermute | solution.py:471
  101.3 4.8 %collective-permute-start.5 = (bf16[4,2,16,128]{3,2,1,0:T(8,128)(2,1)S(1)}, bf16[4,2,16,128]{3,2,1,0:T(8,128)(2,1)S(1)}, u32[]{:S(2)}, u32[]{:S(2)}) collective-permute-start(bf16[4,2,16,128]{3,2,1,0:T(8,128)(2,1)S(1)} %get-tuple-element.54), channel_id=1, source_target_pairs={{1,0},{2,1},{3,2},{5,4},{6,5},{7,6},{9,8},{10,9},{11,10},{13,12},{... | collective-permute-start | bytes 98312 | tf_op jit(solution)/shard_map/ppermute | solution.py:472
  111.3 36.6 %copy-start.8 = (bf16[128,128]{1,0:T(8,128)(2,1)S(1)}, bf16[128,128]{1,0:T(8,128)(2,1)}, u32[]{:S(2)}) copy-start(bf16[128,128]{1,0:T(8,128)(2,1)} %strengths_ref.1) | copy-start | bytes 98308

commit v2 on v1

v2 whole, which is shorter than its diff:
```python
import jax
import jax.numpy as jnp
from jax import lax
from jax.experimental import pallas as pl
from jax.experimental.pallas import tpu as pltpu
from jax.sharding import PartitionSpec as P

step_size = 0.05
viscosity = 0.4
blend = 0.5

EDGE = 128
REACH = 3
FRONT = 9
WIDE = 48
SPAN = 32
GROUP = 32
PITCH = GROUP + 1
ROW_PITCH = 17


def twice_diagonal(block):
    blank = jnp.zeros_like(block)
    return jnp.concatenate(
        [jnp.concatenate([block, blank], axis=1), jnp.concatenate([blank, block], axis=1)], axis=0
    )


def pieces_kernel(remesh_ref, strengths_ref, left_ref, out_ref, scratch):
    left = left_ref[...]
    strengths = twice_diagonal(strengths_ref[...])
    for pair in range(GROUP // 2):
        first = remesh_ref[(2 * pair) * EDGE : (2 * pair + 1) * EDGE, :]
        second = remesh_ref[(2 * pair + 1) * EDGE : (2 * pair + 2) * EDGE, :]
        vortex = jnp.dot(
            jnp.concatenate([first, second], axis=1), strengths, preferred_element_type=jnp.float32
        ).astype(jnp.bfloat16)
        both = jnp.dot(left, vortex, preferred_element_type=jnp.float32)
        for half in range(2):
            tile = 2 * pair + half
            for quarter in range(4):
                for side in range(2):
                    start = quarter * 32 + side * 16
                    scratch[
                        side, pl.ds(quarter * 16 * PITCH + tile, 16, stride=PITCH), :
                    ] = both[start : start + 16, half * EDGE : (half + 1) * EDGE]
    for side in range(2):
        for piece in range(64):
            out_ref[piece, :, side * EDGE : (side + 1) * EDGE] = scratch[
                side, piece * PITCH : piece * PITCH + GROUP, :
            ].astype(jnp.bfloat16)


def tile_pieces(remesh, strengths, left):
    tiles = remesh.shape[0] // EDGE
    return pl.pallas_call(
        pieces_kernel,
        grid=(tiles // GROUP,),
        in_specs=[
            pl.BlockSpec((GROUP * EDGE, EDGE), lambda g: (g, 0)),
            pl.BlockSpec((EDGE, EDGE), lambda g: (0, 0)),
            pl.BlockSpec((EDGE, EDGE), lambda g: (0, 0)),
        ],
        out_specs=pl.BlockSpec((64, GROUP, 2 * EDGE), lambda g: (0, g, 0)),
        out_shape=jax.ShapeDtypeStruct((64, tiles, 2 * EDGE), jnp.bfloat16),
        scratch_shapes=[pltpu.VMEM((2, 64 * PITCH, EDGE), jnp.float32)],
        compiler_params=pltpu.CompilerParams(vmem_limit_bytes=60 * 1024 * 1024),
    )(remesh, strengths, left)


def gather_kernel(index_ref, remesh_ref, out_ref, wide, picked):
    wide[...] = remesh_ref[...].astype(jnp.float32)

    def some(step, carry):
        for k in range(16):
            slot = step * 16 + k
            picked[pl.ds(slot, 1), :] = wide[pl.ds(index_ref[slot], 1), :]
        return carry

    lax.fori_loop(0, out_ref.shape[0] // 16, some, 0)
    out_ref[...] = picked[...].astype(jnp.bfloat16)


def gathered_rows(index, remesh):
    slots = index.shape[0]
    return pl.pallas_call(
        gather_kernel,
        in_specs=[
            pl.BlockSpec(memory_space=pltpu.SMEM),
            pl.BlockSpec(memory_space=pltpu.VMEM),
        ],
        out_specs=pl.BlockSpec(memory_space=pltpu.VMEM),
        out_shape=jax.ShapeDtypeStruct((slots, EDGE), jnp.bfloat16),
        scratch_shapes=[
            pltpu.VMEM(remesh.shape, jnp.float32),
            pltpu.VMEM((slots, EDGE), jnp.float32),
        ],
        compiler_params=pltpu.CompilerParams(vmem_limit_bytes=16 * 1024 * 1024),
        cost_estimate=pl.CostEstimate(flops=0, bytes_accessed=16 * 1024 * 1024, transcendentals=0),
    )(index, remesh)


def sums_kernel(quarter_ref, position_ref, arrived_ref, out_ref):
    depth = 1024
    late = quarter_ref[0] >= 2
    row = lax.broadcasted_iota(jnp.int32, (out_ref.shape[0], EDGE), 0)
    block = row // 16
    entry = row % 16
    outer_block = jnp.where(late, block - 1, block + 1)
    outer = outer_block * 12 + (entry - 12) * 4 + jnp.where(late, 3, 0)
    usable = (outer_block >= 0) & (outer_block < 64) & (entry < 15)
    wanted = jnp.where(entry < 12, block * 12 + entry, jnp.where(usable, outer, -1))
    total = None
    for first in range(0, arrived_ref.shape[0], depth):
        picker = jnp.concatenate(
            [
                (wanted == position_ref[:, start : start + EDGE]).astype(jnp.bfloat16)
                for start in range(first, first + depth, EDGE)
            ],
            axis=1,
        )
        part = jnp.dot(
            picker, arrived_ref[first : first + depth, :], preferred_element_type=jnp.float32
        )
        total = part if total is None else total + part
    out_ref[...] = total.astype(jnp.bfloat16)


def tile_sums(quarter, position, arrived):
    vmem = pl.BlockSpec(memory_space=pltpu.VMEM)
    return pl.pallas_call(
        sums_kernel,
        in_specs=[pl.BlockSpec(memory_space=pltpu.SMEM), vmem, vmem],
        out_specs=vmem,
        out_shape=jax.ShapeDtypeStruct((1024, 2 * EDGE), jnp.bfloat16),
        compiler_params=pltpu.CompilerParams(vmem_limit_bytes=16 * 1024 * 1024),
    )(quarter, position, arrived)


def widen_kernel(velocity_ref, stretch_ref, coupling_ref, low_ref, high_ref, ext_ref, last_ref, first_ref):
    back = FRONT + SPAN
    source = [velocity_ref.at[c] for c in range(3)] + [stretch_ref.at[d] for d in range(3)]
    source.append(coupling_ref)
    for f in range(7):

        def one(layer, carry, f=f):
            ext_ref[f, layer, 0:8, :] = jnp.zeros((8, EDGE), jnp.float32)
            ext_ref[f, layer, WIDE - 8 : WIDE, :] = jnp.zeros((8, EDGE), jnp.float32)
            ext_ref[f, layer, FRONT - REACH : FRONT, :] = low_ref[f, layer]
            ext_ref[f, layer, back : back + REACH, :] = high_ref[f, layer]
            ext_ref[f, layer, FRONT:back, :] = source[f][layer]
            return carry

        lax.fori_loop(0, 16, one, 0)
    for f in range(7):
        depth = 3 if f < 3 else 2
        at = 3 * f if f < 3 else 9 + 2 * (f - 3)
        for k in range(depth):
            last_ref[at + k] = ext_ref[f, 16 - depth + k, 4 : WIDE - 4, :]
            first_ref[at + k] = ext_ref[f, k, 4 : WIDE - 4, :]


def widened(velocity, stretch, coupling, low, high):
    vmem = pl.BlockSpec(memory_space=pltpu.VMEM)
    return pl.pallas_call(
        widen_kernel,
        in_specs=[vmem] * 5,
        out_specs=[vmem] * 3,
        out_shape=[
            jax.ShapeDtypeStruct((7, 16, WIDE, EDGE), jnp.float32),
            jax.ShapeDtypeStruct((17, WIDE - 8, EDGE), jnp.float32),
            jax.ShapeDtypeStruct((17, WIDE - 8, EDGE), jnp.float32),
        ],
        compiler_params=pltpu.CompilerParams(vmem_limit_bytes=16 * 1024 * 1024),
    )(velocity, stretch, coupling, low, high)


def unforced(source, at, squares, halves, keep, lanes, low):
    whole = [source[c, at] for c in range(3)]
    centre = [value[low:] for value in whole]
    carried = [h * u for h, u in zip(halves, centre)]
    ahead_weight = [s - a for s, a in zip(squares, carried)]
    behind_weight = [s + a for s, a in zip(squares, carried)]
    ahead_weight[2] = jnp.where(lanes < EDGE - 1, ahead_weight[2], 0.0)
    behind_weight[2] = jnp.where(lanes > 0, behind_weight[2], 0.0)
    results = []
    for c in range(3):
        total = keep * centre[c]
        total = total + ahead_weight[0] * source[c, at + 1, low:, :]
        total = total + behind_weight[0] * source[c, at - 1, low:, :]
        total = total + ahead_weight[1] * pltpu.roll(whole[c], WIDE - 1, 0)[low:]
        total = total + behind_weight[1] * pltpu.roll(whole[c], 1, 0)[low:]
        total = total + ahead_weight[2] * pltpu.roll(centre[c], EDGE - 1, 1)
        total = total + behind_weight[2] * pltpu.roll(centre[c], 1, 1)
        results.append(total)
    return results


def entry_of(component, layer):
    chord = layer - 2
    entry = component * 4 + chord // 4 if 0 <= chord < 16 else 12 + component
    return chord % 4, entry


def front_kernel(
    sums_ref,
    right_ref,
    ext_ref,
    low_ref,
    high_ref,
    target_ref,
    base_ref,
    squares_ref,
    halves_ref,
    keep_ref,
    rate_ref,
    velocity,
    spread,
):
    blank = jnp.zeros((8, EDGE), jnp.float32)
    lanes = lax.broadcasted_iota(jnp.int32, (WIDE, EDGE), 1)
    product = jnp.dot(
        sums_ref[...], twice_diagonal(right_ref[...]), preferred_element_type=jnp.float32
    )
    for side in range(2):
        for piece in range(64):
            spread[side, piece * ROW_PITCH : piece * ROW_PITCH + 16, :] = product[
                piece * 16 : piece * 16 + 16, side * EDGE : (side + 1) * EDGE
            ]

    def padded(slab):
        return jnp.concatenate([blank[:4], slab, blank[:4]], axis=0)

    for c in range(3):
        for k in range(3):
            velocity[c, k] = padded(low_ref[3 * c + k])
            velocity[c, 19 + k] = padded(high_ref[3 * c + k])
        for layer in range(16):
            velocity[c, layer + 3] = ext_ref[c, layer]

    for layer in range(20):
        inner = layer - 2
        if 0 <= inner < 16:
            stretch = [ext_ref[3 + d, inner] for d in range(3)]
            rate = ext_ref[6, inner]
        else:
            slab, k = (low_ref, layer) if inner < 0 else (high_ref, inner - 16)
            stretch = [padded(slab[9 + 2 * d + k]) for d in range(3)]
            rate = padded(slab[15 + k])
        squares = [(step_size * viscosity) * s * s for s in stretch]
        halves = [(0.5 * step_size) * s for s in stretch]
        keep = 1.0 - rate - 2.0 * (squares[0] + squares[1] + squares[2])
        results = unforced(velocity, layer + 1, squares, halves, keep, lanes, 0)
        for d in range(3):
            squares_ref[d, layer] = squares[d]
            halves_ref[d, layer] = halves[d]
            base_ref[d, layer] = results[d]
        keep_ref[layer] = keep
        rate_ref[layer] = rate
        for component in range(3):
            quarter, entry = entry_of(component, layer)
            target_ref[component, layer, 0:8, :] = blank
            target_ref[component, layer, WIDE - 8 : WIDE, :] = blank
            for side in range(2):
                start = FRONT + 16 * side
                target_ref[component, layer, start : start + 16, :] = spread[
                    side, pl.ds(quarter * 16 * ROW_PITCH + entry, 16, stride=ROW_PITCH), :
                ]
            target_ref[component, layer, 8:FRONT, :] = blank[: FRONT - 8]


def fronted(sums, right, ext, low, high):
    vmem = pl.BlockSpec(memory_space=pltpu.VMEM)
    return pl.pallas_call(
        front_kernel,
        in_specs=[vmem] * 5,
        out_specs=[vmem] * 6,
        out_shape=[jax.ShapeDtypeStruct((3, 20, WIDE, EDGE), jnp.float32)] * 4
        + [jax.ShapeDtypeStruct((20, WIDE, EDGE), jnp.float32)] * 2,
        scratch_shapes=[
            pltpu.VMEM((3, 22, WIDE, EDGE), jnp.float32),
            pltpu.VMEM((2, 64 * ROW_PITCH, EDGE), jnp.float32),
        ],
        compiler_params=pltpu.CompilerParams(vmem_limit_bytes=16 * 1024 * 1024),
        cost_estimate=pl.CostEstimate(
            flops=164 * 1000 * 1000, bytes_accessed=8 * 1024 * 1024, transcendentals=0
        ),
    )(sums, right, ext, low, high)


def grid_kernel(
    target_ref,
    low_ref,
    high_ref,
    right_ref,
    base_ref,
    squares_ref,
    halves_ref,
    keep_ref,
    rate_ref,
    slot_ref,
    next_ref,
    out_ref,
    side_sums,
    forced,
    first,
    second,
    rows,
    slots,
    done,
    sems,
):
    right = right_ref[...]
    back = FRONT + SPAN
    lanes = lax.broadcasted_iota(jnp.int32, (WIDE - 8, EDGE), 1)
    side_sums[0] = jnp.dot(low_ref[...], right, preferred_element_type=jnp.float32)
    side_sums[1] = jnp.dot(high_ref[...], right, preferred_element_type=jnp.float32)
    slots[...] = jnp.zeros_like(slots)
    for c in range(3):
        for layer in range(20):
            quarter, entry = entry_of(c, layer)
            forced[c, layer] = target_ref[c, layer]
            forced[c, layer, FRONT - 2 : FRONT, :] = side_sums[
                0, pl.ds(quarter * 32 + entry, 2, stride=16), :
            ]
            forced[c, layer, back : back + 2, :] = side_sums[
                1, pl.ds(quarter * 32 + entry, 2, stride=16), :
            ]
    for layer in range(20):
        rate = rate_ref[layer]
        for c in range(3):
            pull = rate * forced[c, layer]
            forced[c, layer] = pull
            first[c, layer] = base_ref[c, layer] + pull

    def second_step(layer):
        results = unforced(
            first,
            layer + 1,
            [squares_ref[d, layer + 1, 8:, :] for d in range(3)],
            [halves_ref[d, layer + 1, 8:, :] for d in range(3)],
            keep_ref[layer + 1, 8:, :],
            lanes,
            8,
        )
        for c in range(3):
            second[c, layer] = results[c] + forced[c, layer + 1, 8:, :]

    def curl(layer):
        whole = [second[c, layer + 1] for c in range(3)]
        half = [halves_ref[d, layer + 2, 8:, :] for d in range(3)]

        def slope(d, c):
            if d == 0:
                return half[0] * (second[c, layer + 2] - second[c, layer])
            if d == 1:
                ahead = pltpu.roll(whole[c], WIDE - 9, 0)
                behind = pltpu.roll(whole[c], 1, 0)
            else:
                ahead = jnp.where(lanes < EDGE - 1, pltpu.roll(whole[c], EDGE - 1, 1), 0.0)
                behind = jnp.where(lanes > 0, pltpu.roll(whole[c], 1, 1), 0.0)
            return half[d] * (ahead - behind)

        parts = (
            slope(1, 2) - slope(2, 1),
            slope(2, 0) - slope(0, 2),
            slope(0, 1) - slope(1, 0),
        )
        for c in range(3):
            start = (c * 16 + layer) * SPAN
            rows[start : start + SPAN, :] = (1.0 / step_size) * parts[c][1 : 1 + SPAN]
            done[c, layer] = whole[c][1 : 1 + SPAN]

    def scatter(layer):
        for c in range(3):
            start = (c * 16 + layer) * SPAN
            for row in range(start, start + SPAN):
                slots[pl.ds(slot_ref[row], 1), :] = rows[row : row + 1, :]

    copies = []
    for layer in range(18):
        second_step(layer)
        if layer >= 2:
            curl(layer - 2)
            scatter(layer - 2)
        if layer in (9, 17):
            part = len(copies)
            copies.append(
                pltpu.make_async_copy(
                    done.at[:, pl.ds(8 * part, 8)], next_ref.at[:, pl.ds(8 * part, 8)], sems.at[part]
                )
            )
            copies[part].start()
    out_ref[...] = slots[...].astype(jnp.bfloat16)
    for copy in copies:
        copy.wait()


def grid_update(target, low, high, right, base, squares, halves, keep, rate, slot):
    vmem = pl.BlockSpec(memory_space=pltpu.VMEM)
    return pl.pallas_call(
        grid_kernel,
        in_specs=[vmem] * 9 + [pl.BlockSpec(memory_space=pltpu.SMEM)],
        out_specs=[pl.BlockSpec(memory_space=pl.ANY), vmem],
        out_shape=[
            jax.ShapeDtypeStruct((3, 16, SPAN, EDGE), jnp.float32),
            jax.ShapeDtypeStruct((2 * slot.shape[0], EDGE), jnp.bfloat16),
        ],
        scratch_shapes=[
            pltpu.VMEM((2, 128, EDGE), jnp.float32),
            pltpu.VMEM((3, 20, WIDE, EDGE), jnp.float32),
            pltpu.VMEM((3, 20, WIDE, EDGE), jnp.float32),
            pltpu.VMEM((3, 18, WIDE - 8, EDGE), jnp.float32),
            pltpu.VMEM((slot.shape[0], EDGE), jnp.float32),
            pltpu.VMEM((2 * slot.shape[0], EDGE), jnp.float32),
            pltpu.VMEM((3, 16, SPAN, EDGE), jnp.float32),
            pltpu.SemaphoreType.DMA((2,)),
        ],
        compiler_params=pltpu.CompilerParams(vmem_limit_bytes=24 * 1024 * 1024),
    )(target, low, high, right, base, squares, halves, keep, rate, slot)


def chain(count):
    forward = [(i, i + 1) for i in range(count - 1)]
    return forward, [(target, source) for source, target in forward]


def slot_ranks(destination, block_count):
    count = destination.shape[0]
    one_hot = (destination[:, None] == jnp.arange(block_count, dtype=jnp.int32)[None, :]).astype(
        jnp.bfloat16
    )
    positions = jnp.arange(count, dtype=jnp.int32)
    lower = (positions[:, None] > positions[None, :]).astype(jnp.bfloat16)
    before = jnp.dot(lower, one_hot, preferred_element_type=jnp.float32)
    return jnp.sum(before * one_hot.astype(jnp.float32), axis=1).astype(jnp.int32)


def arrival_places(destination, places, receiver, capacity):
    count = destination.shape[1]
    to_me = destination == receiver
    positions = jnp.arange(count, dtype=jnp.int32)
    upper = (positions[:, None] < positions[None, :]).astype(jnp.bfloat16)
    rank = jnp.dot(
        to_me.astype(jnp.bfloat16), upper, preferred_element_type=jnp.float32
    ).astype(jnp.int32)
    rank = jnp.where(to_me, rank, -1)
    matches = rank[:, None, :] == jnp.arange(capacity, dtype=jnp.int32)[None, :, None]
    return jnp.sum(jnp.where(matches, places[:, None, :], 0), axis=2).reshape(-1)


def shards(
    velocity,
    stretch,
    coupling,
    strengths,
    remesh,
    green_left,
    green_right,
    tile_owner,
    tile_place,
    row_dest,
    row_place,
):
    blocks = lax.axis_size("blk")
    spans = lax.axis_size("span")
    my_block = lax.axis_index("blk")
    my_span = lax.axis_index("span")
    tile_count = remesh.shape[0] // EDGE
    grid_count = velocity.shape[0] * velocity.shape[1] * velocity.shape[2]
    row_cap = 2 * grid_count // blocks

    pieces = tile_pieces(remesh, strengths, green_left)
    held = (
        velocity,
        stretch,
        coupling,
        tile_owner,
        tile_place,
        row_dest,
        row_place,
    )
    pieces, held = lax.optimization_barrier((pieces, held))
    velocity, stretch, coupling, tile_owner, tile_place, row_dest, row_place = held
    arrived = lax.all_to_all(pieces, "blk", split_axis=0, concat_axis=0, tiled=True)

    def mine(values, count):
        rows = values.reshape(blocks, spans * count // EDGE, EDGE)
        if count >= EDGE:
            part = lax.dynamic_slice_in_dim(
                rows, my_span * (count // EDGE), count // EDGE, axis=1
            )
            return part.reshape(blocks, count)
        whole = rows.reshape(blocks, spans, count)
        return lax.dynamic_index_in_dim(whole, my_span, 1, keepdims=False)

    owners = mine(tile_owner.T, tile_count).reshape(1, -1)
    places = mine(tile_place, tile_count).reshape(1, -1)
    position = owners * 12 + places
    quarter = jnp.reshape(my_block // 16, (1,)).astype(jnp.int32)

    forward, backward = chain(spans)
    fields = (velocity, stretch, coupling[None])
    low = lax.ppermute(
        jnp.concatenate([f[:, :, -REACH:] for f in fields], axis=0), "span", forward
    )
    high = lax.ppermute(
        jnp.concatenate([f[:, :, :REACH] for f in fields], axis=0), "span", backward
    )
    extended, last, opening = widened(velocity, stretch, coupling, low, high)
    block_forward, block_backward = chain(blocks)
    low = lax.ppermute(last, "blk", block_forward)
    high = lax.ppermute(opening, "blk", block_backward)

    destinations = mine(row_dest.T, grid_count)
    row_places = mine(row_place, grid_count)
    dest_mine = lax.dynamic_index_in_dim(destinations, my_block, 0, keepdims=False)
    row_slot = dest_mine * row_cap + slot_ranks(dest_mine, blocks)
    row_where = arrival_places(destinations, row_places, my_block, row_cap)
    remesh_rows = gathered_rows(row_where, remesh)

    arrived, position, row_slot, remesh_rows = lax.optimization_barrier(
        (arrived, position, row_slot, remesh_rows)
    )
    sums = tile_sums(quarter, position, arrived.reshape(-1, 2 * EDGE))
    sums, extended, low, high = lax.optimization_barrier((sums, extended, low, high))
    sums = lax.all_to_all(
        sums.reshape(blocks, 16, 2 * EDGE), "blk", split_axis=0, concat_axis=0, tiled=True
    )
    split = sums.reshape(4, 16, 16, 2 * EDGE)
    target, base, squares, halves, keep, rate = fronted(
        sums.reshape(-1, 2 * EDGE), green_right, extended, low, high
    )
    low = lax.ppermute(split[:, 14:16, :, EDGE:], "span", forward)
    high = lax.ppermute(split[:, 0:2, :, :EDGE], "span", backward)
    current, outgoing = grid_update(
        target,
        low.reshape(-1, EDGE),
        high.reshape(-1, EDGE),
        green_right,
        base,
        squares,
        halves,
        keep,
        rate,
        row_slot,
    )
    incoming = lax.all_to_all(
        outgoing.reshape(blocks, row_cap, EDGE), "blk", split_axis=0, concat_axis=0, tiled=True
    )
    spread = lax.dot_general(
        remesh_rows,
        incoming.reshape(-1, EDGE),
        (((0,), (0,)), ((), ())),
        preferred_element_type=jnp.float32,
    )
    return current, (1.0 - blend) * strengths.astype(jnp.float32) + blend * spread


def solution(mesh):
    placed = (
        P(None, "blk", "span", None),
        P(None, "blk", "span", None),
        P("blk", "span", None),
        P(("blk", "span"), None),
        P(("blk", "span"), None),
        P(),
        P(),
        P(),
        P(),
        P(),
        P(),
    )
    return jax.shard_map(
        shards,
        mesh=mesh,
        in_specs=placed,
        out_specs=(P(None, "blk", "span", None), P(("blk", "span"), None)),
        check_vma=False,
    )
```

time: 150 us -> 140 us (0.933)
  other arithmetic: 13.6 us -> 5.2 us
  matrix products: 10.3 us -> 4.05 us
  Pallas kernels: 25.7 us -> 19.7 us
  local copies, waits for them, and re-layouts: 5.35 us -> 11.1 us
  waiting for transfers between devices: 11.9 us -> 15.5 us
  starting transfers between devices: 28 us -> 30 us
    convert_element_type x2 -> x0, other arithmetic: 8.33 us -> none  [the longest x1 8.32 us: shards(): row_spreader = (row_slot[None, :] == jnp.arange(blocks * row_cap, dtype=j...]
    dot_general x1 -> x0, matrix products: 6.3 us -> none  [shards(): jnp.dot(row_spreader, vorticity.reshape(grid_count, EDGE), preferred_elem...]
    unnamed x24 -> x22, local copies, waits for them, and re-layouts: 1.79 us -> 6.59 us
    all_to_all x1, waiting for transfers between devices: 11.9 us -> 15.5 us  [shards(): lax.all_to_all(pieces, 'blk', split_axis=0, concat_axis=0, tiled=True)]
    pallas_call x2, Pallas kernels: 8.6 us -> 5.1 us  [the longest x1 3.53 us: grid_update(): pl.pallas_call(grid_kernel, in_specs=[vmem] * 9 + [pl.BlockSpec(memory_sp...]
    ppermute x1, starting transfers between devices: 3.1 us -> 4.67 us  [shards(): lax.ppermute(jnp.concatenate([f[:, :, -REACH:] for f in fields], axis=0),...]
  transfers between devices with their start and end apart: 7 -> 7, of which waited for: 1 -> 1; matrix products, arithmetic and copies ran while one was open for 14% -> 10% of each run, Pallas kernels for 10% -> 8%
where the time goes in v2:
time: 140 us
  blocking collectives  53 us (38%)
  starting transfers between devices  30 us (21%)
  Pallas kernels  19.7 us (14%)
  waiting for transfers between devices  15.5 us (11%)
  local copies, waits for them, and re-layouts  11.1 us (8%)
  other arithmetic  5.2 us (4%)
  matrix products  4.05 us (3%)
    all_to_all x1, blocking collectives, shards(): lax.all_to_all(outgoing.reshape(blocks, row_cap, EDGE), 'blk', split_axis...  30.3 us
    all_to_all x1, blocking collectives, shards(): lax.all_to_all(sums.reshape(blocks, 16, 2 * EDGE), 'blk', split_axis=0, c...  22.7 us
    all_to_all x1, waiting for transfers between devices, shards(): lax.all_to_all(pieces, 'blk', split_axis=0, concat_axis=0, tiled=True)  15.5 us
    all_to_all x1, starting transfers between devices, shards(): lax.all_to_all(pieces, 'blk', split_axis=0, concat_axis=0, tiled=True)  13.5 us
    unnamed x22, local copies, waits for them, and re-layouts  6.59 us
    ppermute x1, starting transfers between devices, shards(): lax.ppermute(jnp.concatenate([f[:, :, -REACH:] for f in fields], axis=0),...  4.67 us
    pallas_call x1, Pallas kernels, tile_pieces(): pl.pallas_call(pieces_kernel, grid=(tiles // GROUP,), in_specs=[pl.BlockS...  4.53 us
    pallas_call x1, Pallas kernels, gathered_rows(): pl.pallas_call(gather_kernel, in_specs=[pl.BlockSpec(memory_space=pltpu.S...  4.32 us
  transfers between devices with their start and end apart: 7, of which 1 were waited for; matrix products, arithmetic and copies ran while one was open for 10% of the time, Pallas kernels for 8%

profile of v2, /device:TPU:1, one launch (start us, length us, event | category | flops | bytes accessed | tf_op | source)
XLA Modules:
  0.0 139.6 jit_solution(6898114599561345030)
XLA Ops:
  0.6 4.5 %shard_map.122 = bf16[64,64,256]{2,1,0:T(8,128)(2,1)} custom-call(bf16[8192,128]{1,0:T(8,128)(2,1)} %remesh_ref.3, bf16[128,128]{1,0:T(8,128)(2,1)} %strengths_ref.1, bf16[128,128]{1,0:T(8,128)(2,1)} %left_ref.1), custom_call_target="tpu_custom_call" | custom-call | tf_op jit(solution)/shard_map/pallas_call | solution.py:56
  5.2 13.5 %all-to-all-start = ((bf16[64,64,256]{2,1,0:T(8,128)(2,1)}), bf16[64,64,256]{2,1,0:T(8,128)(2,1)}, u32[]{:S(2)}, u32[]{:S(2)}) async-start(bf16[64,64,256]{2,1,0:T(8,128)(2,1)} %shard_map.122), calls=%async_computation | async-start | bytes 4194304 | tf_op jit(solution)/shard_map/all_to_all | solution.py:485
  18.7 1.3 fusion.11
  20.0 0.7 pad_maximum_fusion.1
  20.7 1.3 collective-permute-start.1
  22.0 0.7 pad_maximum_fusion
  22.8 4.7 %collective-permute-start = (f32[7,16,3,128]{3,2,1,0:T(4,128)}, f32[7,16,3,128]{3,2,1,0:T(4,128)}, u32[]{:S(2)}, u32[]{:S(2)}) collective-permute-start(f32[7,16,3,128]{3,2,1,0:T(4,128)} %pad_maximum_fusion), channel_id=1, source_target_pairs={{0,1},{1,2},{2,3},{4,5},{5,6},{6,7},{8,9},{9,10},{10,11},{12,13},{... | collective-permute-start | bytes 516104 | tf_op jit(solution)/shard_map/ppermute | solution.py:504
  27.4 1.5 %constant_dynamic-slice_fusion = (s32[64,12,128]{2,1,0:T(8,128)S(1)}, s32[64,12,128]{2,1,0:T(8,128)S(1)}) fusion(s32[64,48,128]{2,1,0:T(8,128)} %bitcast.36, s32[]{:T(128)S(6)} %select_n.28, s32[64,48,128]{2,1,0:T(8,128)} %bitcast.37), kind=kLoop, calls=%fused_computation.24 | loop fusion | bytes 1572868 | tf_op jit(solution)/shard_map/dynamic_slice | solution.py:490
  28.9 0.9 copy.19
  29.9 2.0 %fusion.4 = s32[64,1536]{1,0:T(8,128)S(1)} fusion(s32[64,1536]{1,0:T(8,128)} %bitcast.34, s32[]{:T(128)S(6)} %axis_index.23), kind=kOutput, calls=%fused_computation.8 | convolution fusion | flops 304742400 | bytes 786436 | tf_op jit(solution)/shard_map/dot_general | solution.py:444
  31.9 2.8 %select_reduce_fusion = s32[64,48]{1,0:T(8,128)S(1)} fusion(s32[64,1536]{1,0:T(8,128)S(1)} %bitcast.33, s32[64,1536]{1,0:T(8,128)S(1)} %fusion.4), kind=kLoop, calls=%fused_computation | loop fusion | flops 14152704 | bytes 798720 | tf_op jit(solution)/shard_map/reduce_sum | solution.py:449
  34.8 4.3 %shard_map.123 = bf16[3072,128]{1,0:T(8,128)(2,1)S(1)} custom-call(s32[3072]{0:T(1024)S(1)} %reshape.78.index_ref, bf16[8192,128]{1,0:T(8,128)(2,1)S(1)} %copy-done), custom_call_target="tpu_custom_call" | custom-call | bytes 16777216 | tf_op jit(solution)/shard_map/pallas_call | solution.py:86
  39.1 0.5 broadcast.24
  39.6 0.8 reduce.9
  40.9 0.8 dynamic-slice_reduce_fusion
  41.8 1.1 copy-done.3
  42.9 1.1 copy-done.4
  44.0 1.8 %shard_map.125 = (f32[7,16,48,128]{3,2,1,0:T(8,128)S(1)}, f32[17,40,128]{2,1,0:T(8,128)S(1)}, f32[17,40,128]{2,1,0:T(8,128)S(1)}) custom-call(f32[3,16,32,128]{3,2,1,0:T(8,128)S(1)} %copy-done.3, f32[3,16,32,128]{3,2,1,0:T(8,128)S(1)} %copy-done.4, f32[16,32,128]{2,1,0:T(8,128)S(1)} %copy-done.5, f32[7,16,3,128]{3,2,1,0:T(4,128)} %collective-permute-done.low_ref, ...), custom_call_target="tpu_custom_call" | custom-call | tf_op jit(solution)/shard_map/pallas_call | solution.py:165
  45.9 1.5 %copy-done.1 = f32[7,16,48,128]{3,2,1,0:T(8,128)} copy-done((f32[7,16,48,128]{3,2,1,0:T(8,128)}, f32[7,16,48,128]{3,2,1,0:T(8,128)S(1)}, u32[]{:S(2)}) %copy-start.1) | copy-done | bytes 2752536
  47.4 4.1 %collective-permute-start.2 = (f32[17,40,128]{2,1,0:T(8,128)S(1)}, f32[17,40,128]{2,1,0:T(8,128)S(1)}, u32[]{:S(2)}, u32[]{:S(2)}) collective-permute-start(f32[17,40,128]{2,1,0:T(8,128)S(1)} %get-tuple-element.40), channel_id=1, source_target_pairs={{0,4},{4,8},{8,12},{12,16},{16,20},{20,24},{24,28},{28,32},{32,36}... | collective-permute-start | bytes 1044488 | tf_op jit(solution)/shard_map/ppermute | solution.py:512
  51.5 1.9 %collective-permute-start.3 = (f32[17,40,128]{2,1,0:T(8,128)S(1)}, f32[17,40,128]{2,1,0:T(8,128)S(1)}, u32[]{:S(2)}, u32[]{:S(2)}) collective-permute-start(f32[17,40,128]{2,1,0:T(8,128)S(1)} %get-tuple-element.41), channel_id=1, source_target_pairs={{4,0},{8,4},{12,8},{16,12},{20,16},{24,20},{28,24},{32,28},{36,32}... | collective-permute-start | bytes 1044488 | tf_op jit(solution)/shard_map/ppermute | solution.py:513
  53.4 1.0 fusion.5
  54.5 15.5 %all-to-all-done = bf16[64,64,256]{2,1,0:T(8,128)(2,1)} async-done(((bf16[64,64,256]{2,1,0:T(8,128)(2,1)}), bf16[64,64,256]{2,1,0:T(8,128)(2,1)}, u32[]{:S(2)}, u32[]{:S(2)}) %all-to-all-start) | async-done | bytes 2097184 | tf_op jit(solution)/shard_map/all_to_all | solution.py:485
  70.0 3.9 %shard_map.124 = bf16[1024,256]{1,0:T(8,128)(2,1)S(1)} custom-call(s32[1]{0:T(128)} %bitcast.quarter_ref, s32[1,4096]{1,0:T(1,128)S(1)} %add.37.position_ref, bf16[4096,256]{1,0:T(8,128)(2,1)} %bitcast.3.arrived_ref), custom_call_target="tpu_custom_call" | custom-call | tf_op jit(solution)/shard_map/pallas_call | solution.py:131
  74.0 22.7 %all_to_all.15 = bf16[64,16,256]{2,1,0:T(8,128)(2,1)S(1)} all-to-all(bf16[64,16,256]{2,1,0:T(8,128)(2,1)S(1)} %bitcast.25), channel_id=1, replica_groups=mesh['blk'=64,'span'=4] {'blk'}, dimensions={0} | all-to-all | bytes 1048576 | tf_op jit(solution)/shard_map/all_to_all | solution.py:527
  96.7 3.1 %collective-permute-start.4 = (bf16[4,2,16,128]{3,2,1,0:T(8,128)(2,1)S(1)}, bf16[4,2,16,128]{3,2,1,0:T(8,128)(2,1)S(1)}, u32[]{:S(2)}, u32[]{:S(2)}) collective-permute-start(bf16[4,2,16,128]{3,2,1,0:T(8,128)(2,1)S(1)} %get-tuple-element.61), channel_id=1, source_target_pairs={{0,1},{1,2},{2,3},{4,5},{5,6},{6,7},{8,9},{9,10},{10,11},{12,13},{... | collective-permute-start | bytes 98312 | tf_op jit(solution)/shard_map/ppermute | solution.py:534
  99.8 1.5 %collective-permute-start.5 = (bf16[4,2,16,128]{3,2,1,0:T(8,128)(2,1)S(1)}, bf16[4,2,16,128]{3,2,1,0:T(8,128)(2,1)S(1)}, u32[]{:S(2)}, u32[]{:S(2)}) collective-permute-start(bf16[4,2,16,128]{3,2,1,0:T(8,128)(2,1)S(1)} %get-tuple-element.60), channel_id=1, source_target_pairs={{1,0},{2,1},{3,2},{5,4},{6,5},{7,6},{9,8},{10,9},{11,10},{13,12},{... | collective-permute-start | bytes 98312 | tf_op jit(solution)/shard_map/ppermute | solution.py:535
  101.3 1.8 %copy-done.2 = f32[7,16,48,128]{3,2,1,0:T(8,128)S(1)} copy-done((f32[7,16,48,128]{3,2,1,0:T(8,128)S(1)}, f32[7,16,48,128]{3,2,1,0:T(8,128)}, u32[]{:S(2)}) %copy-start.2) | copy-done | bytes 2752536
  103.1 1.6 %shard_map.126 = (f32[3,20,48,128]{3,2,1,0:T(8,128)S(1)}, f32[3,20,48,128]{3,2,1,0:T(8,128)S(1)}, f32[3,20,48,128]{3,2,1,0:T(8,128)S(1)}, f32[3,20,48,128]{3,2,1...) custom-call(bf16[1024,256]{1,0:T(8,128)(2,1)S(1)} %bitcast.24, bf16[128,128]{1,0:T(8,128)(2,1)S(1)} %copy-done.6, ...), custom_call_target="tpu_custom_call" | custom-call | flops 164000000 | bytes 8388608 | tf_op jit(solution)/shard_map/pallas_call | solution.py:274
  104.7 3.5 %shard_map.127 = (f32[3,16,32,128]{3,2,1,0:T(8,128)}, bf16[3072,128]{1,0:T(8,128)(2,1)S(1)}) custom-call(f32[3,20,48,128]{3,2,1,0:T(8,128)S(1)} %get-tuple-element.46.target_ref, bf16[128,128]{1,0:T(8,128)(2,1)S(1)} %bitcast.28, bf16[128,128]{1,0:T(8,128)(2,1)S(1)} %bitcast.29, bf16[128,128]{1,0:T(8,128)(2,1)S(1)} %copy-done.6, ...), custom_call_target="tpu_custom_call" | custom-call | tf_op jit(solution)/shard_map/pallas_call | solution.py:401
  108.3 30.3 %all_to_all.16 = bf16[64,48,128]{2,1,0:T(8,128)(2,1)S(1)} all-to-all(bf16[64,48,128]{2,1,0:T(8,128)(2,1)S(1)} %bitcast.26), channel_id=1, replica_groups=mesh['blk'=64,'span'=4] {'blk'}, dimensions={0} | all-to-all | bytes 1572864 | tf_op jit(solution)/shard_map/all_to_all | solution.py:548
  138.5 1.1 fusion.6
  (31 shorter events, 0.7 us)
Async XLA Ops:
  5.2 13.5 %copy-start.5 = (f32[16,32,128]{2,1,0:T(8,128)S(1)}, f32[16,32,128]{2,1,0:T(8,128)}, u32[]{:S(2)}) copy-start(f32[16,32,128]{2,1,0:T(8,128)} %coupling_ref) | copy-start | bytes 786436
  5.2 64.9 %all-to-all-start = ((bf16[64,64,256]{2,1,0:T(8,128)(2,1)}), bf16[64,64,256]{2,1,0:T(8,128)(2,1)}, u32[]{:S(2)}, u32[]{:S(2)}) async-start(bf16[64,64,256]{2,1,0:T(8,128)(2,1)} %shard_map.122), calls=%async_computation | async-start | bytes 4194304 | tf_op jit(solution)/shard_map/all_to_all | solution.py:485
  20.7 21.0 %collective-permute-start.1 = (f32[7,16,3,128]{3,2,1,0:T(4,128)}, f32[7,16,3,128]{3,2,1,0:T(4,128)S(1)}, u32[]{:S(2)}, u32[]{:S(2)}) collective-permute-start(f32[7,16,3,128]{3,2,1,0:T(4,128)} %pad_maximum_fusion.1), channel_id=1, source_target_pairs={{1,0},{2,1},{3,2},{5,4},{6,5},{7,6},{9,8},{10,9},{11,10},{13,12},{... | collective-permute-start | bytes 516104 | tf_op jit(solution)/shard_map/ppermute | solution.py:507
  22.8 19.0 %collective-permute-start = (f32[7,16,3,128]{3,2,1,0:T(4,128)}, f32[7,16,3,128]{3,2,1,0:T(4,128)}, u32[]{:S(2)}, u32[]{:S(2)}) collective-permute-start(f32[7,16,3,128]{3,2,1,0:T(4,128)} %pad_maximum_fusion), channel_id=1, source_target_pairs={{0,1},{1,2},{2,3},{4,5},{5,6},{6,7},{8,9},{9,10},{10,11},{12,13},{... | collective-permute-start | bytes 516104 | tf_op jit(solution)/shard_map/ppermute | solution.py:504
  29.9 4.9 %copy-start = (bf16[8192,128]{1,0:T(8,128)(2,1)S(1)}, bf16[8192,128]{1,0:T(8,128)(2,1)}, u32[]{:S(2)}) copy-start(bf16[8192,128]{1,0:T(8,128)(2,1)} %remesh_ref.3) | copy-start | bytes 6291460
  31.9 7.7 %copy-start.9 = (s32[16384,1]{0,1:T(1,128)S(1)}, s32[16384,1]{0,1:T(1,128)}, u32[]{:S(2)}) copy-start(s32[16384,1]{0,1:T(1,128)} %param.18) | copy-start | bytes 196612
  31.9 8.6 %copy-start.8 = (s32[16384]{0:T(1024)S(1)}, s32[16384]{0:T(1024)}, u32[]{:S(2)}) copy-start(s32[16384]{0:T(1024)} %param.19) | copy-start | bytes 196612
  41.8 1.1 copy-start.3
  42.9 1.1 copy-start.4
  45.9 1.5 %copy-start.1 = (f32[7,16,48,128]{3,2,1,0:T(8,128)}, f32[7,16,48,128]{3,2,1,0:T(8,128)S(1)}, u32[]{:S(2)}) copy-start(f32[7,16,48,128]{3,2,1,0:T(8,128)S(1)} %get-tuple-element.43.ext_ref) | copy-start | bytes 8257540
  47.4 26.5 %collective-permute-start.2 = (f32[17,40,128]{2,1,0:T(8,128)S(1)}, f32[17,40,128]{2,1,0:T(8,128)S(1)}, u32[]{:S(2)}, u32[]{:S(2)}) collective-permute-start(f32[17,40,128]{2,1,0:T(8,128)S(1)} %get-tuple-element.40), channel_id=1, source_target_pairs={{0,4},{4,8},{8,12},{12,16},{16,20},{20,24},{24,28},{28,32},{32,36}... | collective-permute-start | bytes 1044488 | tf_op jit(solution)/shard_map/ppermute | solution.py:512
  51.5 22.5 %collective-permute-start.3 = (f32[17,40,128]{2,1,0:T(8,128)S(1)}, f32[17,40,128]{2,1,0:T(8,128)S(1)}, u32[]{:S(2)}, u32[]{:S(2)}) collective-permute-start(f32[17,40,128]{2,1,0:T(8,128)S(1)} %get-tuple-element.41), channel_id=1, source_target_pairs={{4,0},{8,4},{12,8},{16,12},{20,16},{24,20},{28,24},{32,28},{36,32}... | collective-permute-start | bytes 1044488 | tf_op jit(solution)/shard_map/ppermute | solution.py:513
  54.5 46.8 %copy-start.6 = (bf16[128,128]{1,0:T(8,128)(2,1)S(1)}, bf16[128,128]{1,0:T(8,128)(2,1)}, u32[]{:S(2)}) copy-start(bf16[128,128]{1,0:T(8,128)(2,1)} %right_ref.3) | copy-start | bytes 98308
  96.7 8.0 %collective-permute-start.4 = (bf16[4,2,16,128]{3,2,1,0:T(8,128)(2,1)S(1)}, bf16[4,2,16,128]{3,2,1,0:T(8,128)(2,1)S(1)}, u32[]{:S(2)}, u32[]{:S(2)}) collective-permute-start(bf16[4,2,16,128]{3,2,1,0:T(8,128)(2,1)S(1)} %get-tuple-element.61), channel_id=1, source_target_pairs={{0,1},{1,2},{2,3},{4,5},{5,6},{6,7},{8,9},{9,10},{10,11},{12,13},{... | collective-permute-start | bytes 98312 | tf_op jit(solution)/shard_map/ppermute | solution.py:534
  99.8 4.9 %collective-permute-start.5 = (bf16[4,2,16,128]{3,2,1,0:T(8,128)(2,1)S(1)}, bf16[4,2,16,128]{3,2,1,0:T(8,128)(2,1)S(1)}, u32[]{:S(2)}, u32[]{:S(2)}) collective-permute-start(bf16[4,2,16,128]{3,2,1,0:T(8,128)(2,1)S(1)} %get-tuple-element.60), channel_id=1, source_target_pairs={{1,0},{2,1},{3,2},{5,4},{6,5},{7,6},{9,8},{10,9},{11,10},{13,12},{... | collective-permute-start | bytes 98312 | tf_op jit(solution)/shard_map/ppermute | solution.py:535
  101.3 1.8 %copy-start.2 = (f32[7,16,48,128]{3,2,1,0:T(8,128)S(1)}, f32[7,16,48,128]{3,2,1,0:T(8,128)}, u32[]{:S(2)}) copy-start(f32[7,16,48,128]{3,2,1,0:T(8,128)} %copy-done.1) | copy-start | bytes 8257540
  104.7 33.8 %copy-start.7 = (bf16[128,128]{1,0:T(8,128)(2,1)S(1)}, bf16[128,128]{1,0:T(8,128)(2,1)}, u32[]{:S(2)}) copy-start(bf16[128,128]{1,0:T(8,128)(2,1)} %strengths_ref.1) | copy-start | bytes 98308

commit v3 on v2

--- a/solution.py
+++ b/solution.py
@@ -11,8 +11,8 @@
 
 EDGE = 128
 REACH = 3
-FRONT = 9
-WIDE = 48
+FRONT = 4
+WIDE = 40
 SPAN = 32
 GROUP = 32
 PITCH = GROUP + 1
@@ -29,13 +29,20 @@
 def pieces_kernel(remesh_ref, strengths_ref, left_ref, out_ref, scratch):
     left = left_ref[...]
     strengths = twice_diagonal(strengths_ref[...])
+    paired = jnp.concatenate(
+        [
+            jnp.concatenate(
+                [remesh_ref[at : at + EDGE, :], remesh_ref[at + EDGE : at + 2 * EDGE, :]], axis=1
+            )
+            for at in range(0, GROUP * EDGE, 2 * EDGE)
+        ],
+        axis=0,
+    )
+    vortex = jnp.dot(paired, strengths, preferred_element_type=jnp.float32).astype(jnp.bfloat16)
     for pair in range(GROUP // 2):
-        first = remesh_ref[(2 * pair) * EDGE : (2 * pair + 1) * EDGE, :]
-        second = remesh_ref[(2 * pair + 1) * EDGE : (2 * pair + 2) * EDGE, :]
-        vortex = jnp.dot(
-            jnp.concatenate([first, second], axis=1), strengths, preferred_element_type=jnp.float32
-        ).astype(jnp.bfloat16)
-        both = jnp.dot(left, vortex, preferred_element_type=jnp.float32)
+        both = jnp.dot(
+            left, vortex[pair * EDGE : (pair + 1) * EDGE], preferred_element_type=jnp.float32
+        )
         for half in range(2):
             tile = 2 * pair + half
             for quarter in range(4):
@@ -100,16 +107,11 @@
     )(index, remesh)
 
 
-def sums_kernel(quarter_ref, position_ref, arrived_ref, out_ref):
+def sums_kernel(quarter_ref, position_ref, arrived_ref, out_ref, spread):
     depth = 1024
-    late = quarter_ref[0] >= 2
-    row = lax.broadcasted_iota(jnp.int32, (out_ref.shape[0], EDGE), 0)
-    block = row // 16
-    entry = row % 16
-    outer_block = jnp.where(late, block - 1, block + 1)
-    outer = outer_block * 12 + (entry - 12) * 4 + jnp.where(late, 3, 0)
-    usable = (outer_block >= 0) & (outer_block < 64) & (entry < 15)
-    wanted = jnp.where(entry < 12, block * 12 + entry, jnp.where(usable, outer, -1))
+    blocks = 64
+    row = lax.broadcasted_iota(jnp.int32, (12 * blocks, EDGE), 0)
+    wanted = (row % blocks) * 12 + row // blocks
     total = None
     for first in range(0, arrived_ref.shape[0], depth):
         picker = jnp.concatenate(
@@ -123,7 +125,28 @@
             picker, arrived_ref[first : first + depth, :], preferred_element_type=jnp.float32
         )
         total = part if total is None else total + part
-    out_ref[...] = total.astype(jnp.bfloat16)
+    late = quarter_ref[0] >= 2
+    block = lax.broadcasted_iota(jnp.int32, (blocks, EDGE), 0)
+    for side in range(2):
+        lanes = slice(side * EDGE, (side + 1) * EDGE)
+        places = [total[p * blocks : (p + 1) * blocks, lanes] for p in range(12)]
+        for component in range(3):
+            before = pltpu.roll(places[component * 4 + 3], 1, 0)
+            after = pltpu.roll(places[component * 4], blocks - 1, 0)
+            places.append(
+                jnp.where(
+                    late,
+                    jnp.where(block > 0, before, 0.0),
+                    jnp.where(block < blocks - 1, after, 0.0),
+                )
+            )
+        places.append(jnp.zeros((blocks, EDGE), jnp.float32))
+        for entry, value in enumerate(places):
+            spread[side, pl.ds(entry, blocks, stride=ROW_PITCH), :] = value
+        for k in range(blocks):
+            out_ref[16 * k : 16 * k + 16, lanes] = spread[
+                side, ROW_PITCH * k : ROW_PITCH * k + 16, :
+            ].astype(jnp.bfloat16)
 
 
 def tile_sums(quarter, position, arrived):
@@ -133,22 +156,24 @@
         in_specs=[pl.BlockSpec(memory_space=pltpu.SMEM), vmem, vmem],
         out_specs=vmem,
         out_shape=jax.ShapeDtypeStruct((1024, 2 * EDGE), jnp.bfloat16),
+        scratch_shapes=[pltpu.VMEM((2, 64 * ROW_PITCH, EDGE), jnp.float32)],
         compiler_params=pltpu.CompilerParams(vmem_limit_bytes=16 * 1024 * 1024),
     )(quarter, position, arrived)
 
 
-def widen_kernel(velocity_ref, stretch_ref, coupling_ref, low_ref, high_ref, ext_ref, last_ref, first_ref):
+def widen_kernel(velocity_ref, stretch_ref, coupling_ref, low_ref, high_ref, wide_u, wide_s, wide_r, last_ref, first_ref):
     back = FRONT + SPAN
     source = [velocity_ref.at[c] for c in range(3)] + [stretch_ref.at[d] for d in range(3)]
     source.append(coupling_ref)
+    wide = [wide_u.at[c] for c in range(3)] + [wide_s.at[d] for d in range(3)] + [wide_r]
     for f in range(7):
 
         def one(layer, carry, f=f):
-            ext_ref[f, layer, 0:8, :] = jnp.zeros((8, EDGE), jnp.float32)
-            ext_ref[f, layer, WIDE - 8 : WIDE, :] = jnp.zeros((8, EDGE), jnp.float32)
-            ext_ref[f, layer, FRONT - REACH : FRONT, :] = low_ref[f, layer]
-            ext_ref[f, layer, back : back + REACH, :] = high_ref[f, layer]
-            ext_ref[f, layer, FRONT:back, :] = source[f][layer]
+            wide[f][layer, 0:8, :] = jnp.zeros((8, EDGE), jnp.float32)
+            wide[f][layer, WIDE - 8 : WIDE, :] = jnp.zeros((8, EDGE), jnp.float32)
+            wide[f][layer, FRONT - REACH : FRONT, :] = low_ref[f, layer]
+            wide[f][layer, back : back + REACH, :] = high_ref[f, layer]
+            wide[f][layer, FRONT:back, :] = source[f][layer]
             return carry
 
         lax.fori_loop(0, 16, one, 0)
@@ -156,8 +181,8 @@
         depth = 3 if f < 3 else 2
         at = 3 * f if f < 3 else 9 + 2 * (f - 3)
         for k in range(depth):
-            last_ref[at + k] = ext_ref[f, 16 - depth + k, 4 : WIDE - 4, :]
-            first_ref[at + k] = ext_ref[f, k, 4 : WIDE - 4, :]
+            last_ref[at + k] = wide[f][16 - depth + k]
+            first_ref[at + k] = wide[f][k]
 
 
 def widened(velocity, stretch, coupling, low, high):
@@ -165,19 +190,20 @@
     return pl.pallas_call(
         widen_kernel,
         in_specs=[vmem] * 5,
-        out_specs=[vmem] * 3,
+        out_specs=[vmem] * 5,
         out_shape=[
-            jax.ShapeDtypeStruct((7, 16, WIDE, EDGE), jnp.float32),
-            jax.ShapeDtypeStruct((17, WIDE - 8, EDGE), jnp.float32),
-            jax.ShapeDtypeStruct((17, WIDE - 8, EDGE), jnp.float32),
+            jax.ShapeDtypeStruct((3, 16, WIDE, EDGE), jnp.float32),
+            jax.ShapeDtypeStruct((3, 16, WIDE, EDGE), jnp.float32),
+            jax.ShapeDtypeStruct((16, WIDE, EDGE), jnp.float32),
+            jax.ShapeDtypeStruct((17, WIDE, EDGE), jnp.float32),
+            jax.ShapeDtypeStruct((17, WIDE, EDGE), jnp.float32),
         ],
         compiler_params=pltpu.CompilerParams(vmem_limit_bytes=16 * 1024 * 1024),
     )(velocity, stretch, coupling, low, high)
 
 
-def unforced(source, at, squares, halves, keep, lanes, low):
-    whole = [source[c, at] for c in range(3)]
-    centre = [value[low:] for value in whole]
+def unforced(source, at, squares, halves, keep, lanes):
+    centre = [source[c, at] for c in range(3)]
     carried = [h * u for h, u in zip(halves, centre)]
     ahead_weight = [s - a for s, a in zip(squares, carried)]
     behind_weight = [s + a for s, a in zip(squares, carried)]
@@ -186,10 +212,10 @@
     results = []
     for c in range(3):
         total = keep * centre[c]
-        total = total + ahead_weight[0] * source[c, at + 1, low:, :]
-        total = total + behind_weight[0] * source[c, at - 1, low:, :]
-        total = total + ahead_weight[1] * pltpu.roll(whole[c], WIDE - 1, 0)[low:]
-        total = total + behind_weight[1] * pltpu.roll(whole[c], 1, 0)[low:]
+        total = total + ahead_weight[0] * source[c, at + 1]
+        total = total + behind_weight[0] * source[c, at - 1]
+        total = total + ahead_weight[1] * pltpu.roll(centre[c], WIDE - 1, 0)
+        total = total + behind_weight[1] * pltpu.roll(centre[c], 1, 0)
         total = total + ahead_weight[2] * pltpu.roll(centre[c], EDGE - 1, 1)
         total = total + behind_weight[2] * pltpu.roll(centre[c], 1, 1)
         results.append(total)
@@ -205,7 +231,9 @@
 def front_kernel(
     sums_ref,
     right_ref,
-    ext_ref,
+    wide_u,
+    wide_s,
+    wide_r,
     low_ref,
     high_ref,
     target_ref,
@@ -228,29 +256,26 @@
                 piece * 16 : piece * 16 + 16, side * EDGE : (side + 1) * EDGE
             ]
 
-    def padded(slab):
-        return jnp.concatenate([blank[:4], slab, blank[:4]], axis=0)
-
     for c in range(3):
         for k in range(3):
-            velocity[c, k] = padded(low_ref[3 * c + k])
-            velocity[c, 19 + k] = padded(high_ref[3 * c + k])
+            velocity[c, k] = low_ref[3 * c + k]
+            velocity[c, 19 + k] = high_ref[3 * c + k]
         for layer in range(16):
-            velocity[c, layer + 3] = ext_ref[c, layer]
+            velocity[c, layer + 3] = wide_u[c, layer]
 
     for layer in range(20):
         inner = layer - 2
         if 0 <= inner < 16:
-            stretch = [ext_ref[3 + d, inner] for d in range(3)]
-            rate = ext_ref[6, inner]
+            stretch = [wide_s[d, inner] for d in range(3)]
+            rate = wide_r[inner]
         else:
             slab, k = (low_ref, layer) if inner < 0 else (high_ref, inner - 16)
-            stretch = [padded(slab[9 + 2 * d + k]) for d in range(3)]
-            rate = padded(slab[15 + k])
+            stretch = [slab[9 + 2 * d + k] for d in range(3)]
+            rate = slab[15 + k]
         squares = [(step_size * viscosity) * s * s for s in stretch]
         halves = [(0.5 * step_size) * s for s in stretch]
         keep = 1.0 - rate - 2.0 * (squares[0] + squares[1] + squares[2])
-        results = unforced(velocity, layer + 1, squares, halves, keep, lanes, 0)
+        results = unforced(velocity, layer + 1, squares, halves, keep, lanes)
         for d in range(3):
             squares_ref[d, layer] = squares[d]
             halves_ref[d, layer] = halves[d]
@@ -266,14 +291,13 @@
                 target_ref[component, layer, start : start + 16, :] = spread[
                     side, pl.ds(quarter * 16 * ROW_PITCH + entry, 16, stride=ROW_PITCH), :
                 ]
-            target_ref[component, layer, 8:FRONT, :] = blank[: FRONT - 8]
-
-
-def fronted(sums, right, ext, low, high):
+
+
+def fronted(sums, right, fields, low, high):
     vmem = pl.BlockSpec(memory_space=pltpu.VMEM)
     return pl.pallas_call(
         front_kernel,
-        in_specs=[vmem] * 5,
+        in_specs=[vmem] * 7,
         out_specs=[vmem] * 6,
         out_shape=[jax.ShapeDtypeStruct((3, 20, WIDE, EDGE), jnp.float32)] * 4
         + [jax.ShapeDtypeStruct((20, WIDE, EDGE), jnp.float32)] * 2,
@@ -285,7 +309,7 @@
         cost_estimate=pl.CostEstimate(
             flops=164 * 1000 * 1000, bytes_accessed=8 * 1024 * 1024, transcendentals=0
         ),
-    )(sums, right, ext, low, high)
+    )(sums, right, *fields, low, high)
 
 
 def grid_kernel(
@@ -312,7 +336,7 @@
 ):
     right = right_ref[...]
     back = FRONT + SPAN
-    lanes = lax.broadcasted_iota(jnp.int32, (WIDE - 8, EDGE), 1)
+    lanes = lax.broadcasted_iota(jnp.int32, (WIDE, EDGE), 1)
     side_sums[0] = jnp.dot(low_ref[...], right, preferred_element_type=jnp.float32)
     side_sums[1] = jnp.dot(high_ref[...], right, preferred_element_type=jnp.float32)
     slots[...] = jnp.zeros_like(slots)
@@ -337,24 +361,23 @@
         results = unforced(
             first,
             layer + 1,
-            [squares_ref[d, layer + 1, 8:, :] for d in range(3)],
-            [halves_ref[d, layer + 1, 8:, :] for d in range(3)],
-            keep_ref[layer + 1, 8:, :],
+            [squares_ref[d, layer + 1] for d in range(3)],
+            [halves_ref[d, layer + 1] for d in range(3)],
+            keep_ref[layer + 1],
             lanes,
-            8,
         )
         for c in range(3):
-            second[c, layer] = results[c] + forced[c, layer + 1, 8:, :]
+            second[c, layer] = results[c] + forced[c, layer + 1]
 
     def curl(layer):
         whole = [second[c, layer + 1] for c in range(3)]
-        half = [halves_ref[d, layer + 2, 8:, :] for d in range(3)]
+        half = [halves_ref[d, layer + 2] for d in range(3)]
 
         def slope(d, c):
             if d == 0:
                 return half[0] * (second[c, layer + 2] - second[c, layer])
             if d == 1:
-                ahead = pltpu.roll(whole[c], WIDE - 9, 0)
+                ahead = pltpu.roll(whole[c], WIDE - 1, 0)
                 behind = pltpu.roll(whole[c], 1, 0)
             else:
                 ahead = jnp.where(lanes < EDGE - 1, pltpu.roll(whole[c], EDGE - 1, 1), 0.0)
@@ -368,8 +391,8 @@
         )
         for c in range(3):
             start = (c * 16 + layer) * SPAN
-            rows[start : start + SPAN, :] = (1.0 / step_size) * parts[c][1 : 1 + SPAN]
-            done[c, layer] = whole[c][1 : 1 + SPAN]
+            rows[start : start + SPAN, :] = (1.0 / step_size) * parts[c][FRONT:back]
+            done[c, layer] = whole[c][FRONT:back]
 
     def scatter(layer):
         for c in range(3):
@@ -410,7 +433,7 @@
             pltpu.VMEM((2, 128, EDGE), jnp.float32),
             pltpu.VMEM((3, 20, WIDE, EDGE), jnp.float32),
             pltpu.VMEM((3, 20, WIDE, EDGE), jnp.float32),
-            pltpu.VMEM((3, 18, WIDE - 8, EDGE), jnp.float32),
+            pltpu.VMEM((3, 18, WIDE, EDGE), jnp.float32),
             pltpu.VMEM((slot.shape[0], EDGE), jnp.float32),
             pltpu.VMEM((2 * slot.shape[0], EDGE), jnp.float32),
             pltpu.VMEM((3, 16, SPAN, EDGE), jnp.float32),
@@ -418,6 +441,25 @@
         ],
         compiler_params=pltpu.CompilerParams(vmem_limit_bytes=24 * 1024 * 1024),
     )(target, low, high, right, base, squares, halves, keep, rate, slot)
+
+
+def edges_kernel(sums_ref, left_ref, right_ref):
+    for quarter in range(4):
+        for k in range(2):
+            row = 32 * quarter + 16 * k
+            left_ref[row : row + 16, :] = sums_ref[16 * quarter + k, :, :EDGE]
+            right_ref[row : row + 16, :] = sums_ref[16 * quarter + 14 + k, :, EDGE:]
+
+
+def edges(sums):
+    vmem = pl.BlockSpec(memory_space=pltpu.VMEM)
+    return pl.pallas_call(
+        edges_kernel,
+        in_specs=[vmem],
+        out_specs=[vmem] * 2,
+        out_shape=[jax.ShapeDtypeStruct((128, EDGE), jnp.bfloat16)] * 2,
+        compiler_params=pltpu.CompilerParams(vmem_limit_bytes=16 * 1024 * 1024),
+    )(sums)
 
 
 def chain(count):
@@ -507,10 +549,6 @@
     high = lax.ppermute(
         jnp.concatenate([f[:, :, :REACH] for f in fields], axis=0), "span", backward
     )
-    extended, last, opening = widened(velocity, stretch, coupling, low, high)
-    block_forward, block_backward = chain(blocks)
-    low = lax.ppermute(last, "blk", block_forward)
-    high = lax.ppermute(opening, "blk", block_backward)
 
     destinations = mine(row_dest.T, grid_count)
     row_places = mine(row_place, grid_count)
@@ -518,6 +556,13 @@
     row_slot = dest_mine * row_cap + slot_ranks(dest_mine, blocks)
     row_where = arrival_places(destinations, row_places, my_block, row_cap)
     remesh_rows = gathered_rows(row_where, remesh)
+    low, high, position, row_slot, remesh_rows = lax.optimization_barrier(
+        (low, high, position, row_slot, remesh_rows)
+    )
+    *extended, last, opening = widened(velocity, stretch, coupling, low, high)
+    block_forward, block_backward = chain(blocks)
+    low = lax.ppermute(last, "blk", block_forward)
+    high = lax.ppermute(opening, "blk", block_backward)
 
     arrived, position, row_slot, remesh_rows = lax.optimization_barrier(
         (arrived, position, row_slot, remesh_rows)
@@ -527,16 +572,16 @@
     sums = lax.all_to_all(
         sums.reshape(blocks, 16, 2 * EDGE), "blk", split_axis=0, concat_axis=0, tiled=True
     )
-    split = sums.reshape(4, 16, 16, 2 * EDGE)
+    left_edge, right_edge = edges(sums)
     target, base, squares, halves, keep, rate = fronted(
         sums.reshape(-1, 2 * EDGE), green_right, extended, low, high
     )
-    low = lax.ppermute(split[:, 14:16, :, EDGE:], "span", forward)
-    high = lax.ppermute(split[:, 0:2, :, :EDGE], "span", backward)
+    low = lax.ppermute(right_edge, "span", forward)
+    high = lax.ppermute(left_edge, "span", backward)
     current, outgoing = grid_update(
         target,
-        low.reshape(-1, EDGE),
-        high.reshape(-1, EDGE),
+        low,
+        high,
         green_right,
         base,
         squares,

time: 140 us -> 140 us (level)
  local copies, waits for them, and re-layouts: 11.1 us -> 6.57 us
  waiting for transfers between devices: 15.5 us -> 18.3 us
    unnamed x22, local copies, waits for them, and re-layouts: 6.59 us -> 2.05 us
    all_to_all x1, waiting for transfers between devices: 15.5 us -> 17.4 us  [shards(): lax.all_to_all(pieces, 'blk', split_axis=0, concat_axis=0, tiled=True)]
    pallas_call x2 -> x3, Pallas kernels: 3.4 us -> 4.99 us  [the longest x1 2.68 us: widened(): pl.pallas_call(widen_kernel, in_specs=[vmem] * 5, out_specs=[vmem] * 5, o...]
  transfers between devices with their start and end apart: 7 -> 7, of which waited for: 1 -> 2; matrix products, arithmetic and copies ran while one was open for 10% -> 10% of each run, Pallas kernels for 8% -> 9%
where the time goes in v3:
time: 140 us; the launch traced here: 139 us
  blocking collectives  53.2 us (38%)
  starting transfers between devices  30 us (21%)
  Pallas kernels  20.5 us (15%)
  waiting for transfers between devices  18.3 us (13%)
  local copies, waits for them, and re-layouts  6.57 us (5%)
  other arithmetic  5.24 us (4%)
  matrix products  4.05 us (3%)
    all_to_all x1, blocking collectives, shards(): lax.all_to_all(outgoing.reshape(blocks, row_cap, EDGE), 'blk', split_axis...  30.5 us
    all_to_all x1, blocking collectives, shards(): lax.all_to_all(sums.reshape(blocks, 16, 2 * EDGE), 'blk', split_axis=0, c...  22.7 us
    all_to_all x1, waiting for transfers between devices, shards(): lax.all_to_all(pieces, 'blk', split_axis=0, concat_axis=0, tiled=True)  17.4 us
    all_to_all x1, starting transfers between devices, shards(): lax.all_to_all(pieces, 'blk', split_axis=0, concat_axis=0, tiled=True)  13.5 us
    ppermute x1, starting transfers between devices, shards(): lax.ppermute(jnp.concatenate([f[:, :, -REACH:] for f in fields], axis=0),...  4.69 us
    pallas_call x1, Pallas kernels, gathered_rows(): pl.pallas_call(gather_kernel, in_specs=[pl.BlockSpec(memory_space=pltpu.S...  4.32 us
    pallas_call x1, Pallas kernels, tile_pieces(): pl.pallas_call(pieces_kernel, grid=(tiles // GROUP,), in_specs=[pl.BlockS...  4.22 us
    ppermute x1, starting transfers between devices, shards(): low = lax.ppermute(last, 'blk', block_forward)  4.09 us
  transfers between devices with their start and end apart: 7, of which 2 were waited for; matrix products, arithmetic and copies ran while one was open for 10% of the time, Pallas kernels for 9%

profile of v3, /device:TPU:1, one launch (start us, length us, event | category | flops | bytes accessed | tf_op | source)
XLA Modules:
  0.0 138.8 jit_solution(6473732988700278767)
XLA Ops:
  0.6 4.2 %shard_map.122 = bf16[64,64,256]{2,1,0:T(8,128)(2,1)} custom-call(bf16[8192,128]{1,0:T(8,128)(2,1)} %remesh_ref.3, bf16[128,128]{1,0:T(8,128)(2,1)} %strengths_ref.1, bf16[128,128]{1,0:T(8,128)(2,1)} %left_ref.1), custom_call_target="tpu_custom_call" | custom-call | tf_op jit(solution)/shard_map/pallas_call | solution.py:63
  4.9 13.5 %all-to-all-start = ((bf16[64,64,256]{2,1,0:T(8,128)(2,1)}), bf16[64,64,256]{2,1,0:T(8,128)(2,1)}, u32[]{:S(2)}, u32[]{:S(2)}) async-start(bf16[64,64,256]{2,1,0:T(8,128)(2,1)} %shard_map.122), calls=%async_computation | async-start | bytes 4194304 | tf_op jit(solution)/shard_map/all_to_all | solution.py:527
  18.4 1.3 fusion.11
  19.7 0.8 pad_maximum_fusion.1
  20.4 1.3 collective-permute-start.1
  21.7 0.7 pad_maximum_fusion
  22.5 4.7 %collective-permute-start = (f32[7,16,3,128]{3,2,1,0:T(4,128)}, f32[7,16,3,128]{3,2,1,0:T(4,128)}, u32[]{:S(2)}, u32[]{:S(2)}) collective-permute-start(f32[7,16,3,128]{3,2,1,0:T(4,128)} %pad_maximum_fusion), channel_id=1, source_target_pairs={{0,1},{1,2},{2,3},{4,5},{5,6},{6,7},{8,9},{9,10},{10,11},{12,13},{... | collective-permute-start | bytes 516104 | tf_op jit(solution)/shard_map/ppermute | solution.py:546
  27.2 1.5 %constant_dynamic-slice_fusion = (s32[64,12,128]{2,1,0:T(8,128)S(1)}, s32[64,12,128]{2,1,0:T(8,128)S(1)}) fusion(s32[64,48,128]{2,1,0:T(8,128)} %bitcast.30, s32[]{:T(128)S(6)} %select_n.28, s32[64,48,128]{2,1,0:T(8,128)} %bitcast.31), kind=kLoop, calls=%fused_computation.24 | loop fusion | bytes 1572868 | tf_op jit(solution)/shard_map/dynamic_slice | solution.py:532
  28.7 0.9 copy.19
  29.7 2.0 %fusion.4 = s32[64,1536]{1,0:T(8,128)S(1)} fusion(s32[64,1536]{1,0:T(8,128)} %bitcast.28, s32[]{:T(128)S(6)} %axis_index.23), kind=kOutput, calls=%fused_computation.8 | convolution fusion | flops 304742400 | bytes 786436 | tf_op jit(solution)/shard_map/dot_general | solution.py:486
  31.7 2.8 %select_reduce_fusion = s32[64,48]{1,0:T(8,128)S(1)} fusion(s32[64,1536]{1,0:T(8,128)S(1)} %bitcast.27, s32[64,1536]{1,0:T(8,128)S(1)} %fusion.4), kind=kLoop, calls=%fused_computation | loop fusion | flops 14152704 | bytes 798720 | tf_op jit(solution)/shard_map/reduce_sum | solution.py:491
  34.5 4.3 %shard_map.123 = bf16[3072,128]{1,0:T(8,128)(2,1)S(1)} custom-call(s32[3072]{0:T(1024)S(1)} %reshape.69.index_ref, bf16[8192,128]{1,0:T(8,128)(2,1)S(1)} %copy-done), custom_call_target="tpu_custom_call" | custom-call | bytes 16777216 | tf_op jit(solution)/shard_map/pallas_call | solution.py:93
  38.8 0.5 broadcast.24
  39.4 0.8 reduce.9
  40.4 0.1 add_reduce_fusion
  40.6 0.8 dynamic-slice_reduce_fusion
  41.5 1.0 fusion.5
  42.6 0.2 copy-done.2
  42.9 2.7 %shard_map.125 = (f32[3,16,40,128]{3,2,1,0:T(8,128)S(1)}, f32[3,16,40,128]{3,2,1,0:T(8,128)S(1)}, f32[16,40,128]{2,1,0:T(8,128)S(1)}, f32[17,40,128]{2,1,0:T(8,128)}, f32[17,40,128]{2,1,0:T(8,128)}) custom-call(f32[3,16,32,128]{3,2,1,0:T(8,128)S(1)} %copy-done.1, f32[3,16,32,128]{3,2,1,0:T(8,128)S(1)} %copy-done.2, f32[16,32,128]{2,1,0:T(8,128)S(1)} %copy-done.3, ...), custom_call_target="tpu_custom_call" | custom-call | tf_op jit(solution)/shard_map/pallas_call | solution.py:190
  45.5 0.7 copy-done.4
  46.3 4.1 %collective-permute-start.2 = (f32[17,40,128]{2,1,0:T(8,128)}, f32[17,40,128]{2,1,0:T(8,128)S(1)}, u32[]{:S(2)}, u32[]{:S(2)}) collective-permute-start(f32[17,40,128]{2,1,0:T(8,128)} %get-tuple-element.58), channel_id=1, source_target_pairs={{0,4},{4,8},{8,12},{12,16},{16,20},{20,24},{24,28},{28,32},{32,36}... | collective-permute-start | bytes 1044488 | tf_op jit(solution)/shard_map/ppermute | solution.py:564
  50.4 1.9 %collective-permute-start.3 = (f32[17,40,128]{2,1,0:T(8,128)}, f32[17,40,128]{2,1,0:T(8,128)}, u32[]{:S(2)}, u32[]{:S(2)}) collective-permute-start(f32[17,40,128]{2,1,0:T(8,128)} %get-tuple-element.59), channel_id=1, source_target_pairs={{4,0},{8,4},{12,8},{16,12},{20,16},{24,20},{28,24},{32,28},{36,32}... | collective-permute-start | bytes 1044488 | tf_op jit(solution)/shard_map/ppermute | solution.py:565
  52.3 17.4 %all-to-all-done = bf16[64,64,256]{2,1,0:T(8,128)(2,1)} async-done(((bf16[64,64,256]{2,1,0:T(8,128)(2,1)}), bf16[64,64,256]{2,1,0:T(8,128)(2,1)}, u32[]{:S(2)}, u32[]{:S(2)}) %all-to-all-start) | async-done | bytes 2097184 | tf_op jit(solution)/shard_map/all_to_all | solution.py:527
  69.7 3.5 %shard_map.124 = bf16[1024,256]{1,0:T(8,128)(2,1)S(1)} custom-call(s32[1]{0:T(128)} %bitcast.quarter_ref, s32[1,4096]{1,0:T(1,128)S(1)} %add.37.position_ref, bf16[4096,256]{1,0:T(8,128)(2,1)} %bitcast.4.arrived_ref), custom_call_target="tpu_custom_call" | custom-call | tf_op jit(solution)/shard_map/pallas_call | solution.py:154
  73.2 22.7 %all_to_all.15.sums_ref = bf16[64,16,256]{2,1,0:T(8,128)(2,1)S(1)} all-to-all(bf16[64,16,256]{2,1,0:T(8,128)(2,1)S(1)} %bitcast.21), channel_id=1, replica_groups=mesh['blk'=64,'span'=4] {'blk'}, dimensions={0} | all-to-all | bytes 1048576 | tf_op jit(solution)/shard_map/all_to_all | solution.py:572
  95.9 3.1 %collective-permute-start.4 = (bf16[128,128]{1,0:T(8,128)(2,1)S(1)}, bf16[128,128]{1,0:T(8,128)(2,1)S(1)}, u32[]{:S(2)}, u32[]{:S(2)}) collective-permute-start(bf16[128,128]{1,0:T(8,128)(2,1)S(1)} %get-tuple-element.67), channel_id=1, source_target_pairs={{0,1},{1,2},{2,3},{4,5},{5,6},{6,7},{8,9},{9,10},{10,11},{12,13},{... | collective-permute-start | bytes 98312 | tf_op jit(solution)/shard_map/ppermute | solution.py:579
  99.1 1.5 %collective-permute-start.5 = (bf16[128,128]{1,0:T(8,128)(2,1)S(1)}, bf16[128,128]{1,0:T(8,128)(2,1)S(1)}, u32[]{:S(2)}, u32[]{:S(2)}) collective-permute-start(bf16[128,128]{1,0:T(8,128)(2,1)S(1)} %get-tuple-element.68), channel_id=1, source_target_pairs={{1,0},{2,1},{3,2},{5,4},{6,5},{7,6},{9,8},{10,9},{11,10},{13,12},{... | collective-permute-start | bytes 98312 | tf_op jit(solution)/shard_map/ppermute | solution.py:580
  100.6 2.3 %shard_map.126 = (f32[3,20,40,128]{3,2,1,0:T(8,128)S(1)}, f32[3,20,40,128]{3,2,1,0:T(8,128)S(1)}, f32[3,20,40,128]{3,2,1,0:T(8,128)S(1)}, f32[3,20,40,128]{3,2,1...) custom-call(bf16[1024,256]{1,0:T(8,128)(2,1)S(1)} %bitcast.20, bf16[128,128]{1,0:T(8,128)(2,1)S(1)} %copy-done.6, ...), custom_call_target="tpu_custom_call" | custom-call | flops 164000000 | bytes 8388608 | tf_op jit(solution)/shard_map/pallas_call | solution.py:298
  102.9 0.8 collective-permute-done.5.high_ref
  103.7 3.5 %shard_map.128 = (f32[3,16,32,128]{3,2,1,0:T(8,128)}, bf16[3072,128]{1,0:T(8,128)(2,1)S(1)}) custom-call(f32[3,20,40,128]{3,2,1,0:T(8,128)S(1)} %get-tuple-element.66.target_ref, bf16[128,128]{1,0:T(8,128)(2,1)S(1)} %collective-permute-done.4.low_ref, bf16[128,128]{1,0:T(8,128)(2,1)S(1)} %collective-permute-done.5.high_ref, bf16[128,128]{1,0:T(8,128)(2,1)S(1)} %copy-done.6, ...), custom_call_target="tpu_custom_call" | custom-call | tf_op jit(solution)/shard_map/pallas_call | solution.py:424
  107.3 30.5 %all_to_all.16 = bf16[64,48,128]{2,1,0:T(8,128)(2,1)S(1)} all-to-all(bf16[64,48,128]{2,1,0:T(8,128)(2,1)S(1)} %bitcast.22), channel_id=1, replica_groups=mesh['blk'=64,'span'=4] {'blk'}, dimensions={0} | all-to-all | bytes 1572864 | tf_op jit(solution)/shard_map/all_to_all | solution.py:593
  137.8 1.1 fusion.6
  (31 shorter events, 0.6 us)
Async XLA Ops:
  4.8 13.5 %copy-start.3 = (f32[16,32,128]{2,1,0:T(8,128)S(1)}, f32[16,32,128]{2,1,0:T(8,128)}, u32[]{:S(2)}) copy-start(f32[16,32,128]{2,1,0:T(8,128)} %coupling_ref) | copy-start | bytes 786436
  4.9 64.9 %all-to-all-start = ((bf16[64,64,256]{2,1,0:T(8,128)(2,1)}), bf16[64,64,256]{2,1,0:T(8,128)(2,1)}, u32[]{:S(2)}, u32[]{:S(2)}) async-start(bf16[64,64,256]{2,1,0:T(8,128)(2,1)} %shard_map.122), calls=%async_computation | async-start | bytes 4194304 | tf_op jit(solution)/shard_map/all_to_all | solution.py:527
  20.4 22.1 %collective-permute-start.1 = (f32[7,16,3,128]{3,2,1,0:T(4,128)}, f32[7,16,3,128]{3,2,1,0:T(4,128)S(1)}, u32[]{:S(2)}, u32[]{:S(2)}) collective-permute-start(f32[7,16,3,128]{3,2,1,0:T(4,128)} %pad_maximum_fusion.1), channel_id=1, source_target_pairs={{1,0},{2,1},{3,2},{5,4},{6,5},{7,6},{9,8},{10,9},{11,10},{13,12},{... | collective-permute-start | bytes 516104 | tf_op jit(solution)/shard_map/ppermute | solution.py:549
  22.5 20.1 %collective-permute-start = (f32[7,16,3,128]{3,2,1,0:T(4,128)}, f32[7,16,3,128]{3,2,1,0:T(4,128)}, u32[]{:S(2)}, u32[]{:S(2)}) collective-permute-start(f32[7,16,3,128]{3,2,1,0:T(4,128)} %pad_maximum_fusion), channel_id=1, source_target_pairs={{0,1},{1,2},{2,3},{4,5},{5,6},{6,7},{8,9},{9,10},{10,11},{12,13},{... | collective-permute-start | bytes 516104 | tf_op jit(solution)/shard_map/ppermute | solution.py:546
  29.6 4.9 %copy-start = (bf16[8192,128]{1,0:T(8,128)(2,1)S(1)}, bf16[8192,128]{1,0:T(8,128)(2,1)}, u32[]{:S(2)}) copy-start(bf16[8192,128]{1,0:T(8,128)(2,1)} %remesh_ref.3) | copy-start | bytes 6291460
  31.6 7.7 %copy-start.9 = (s32[16384,1]{0,1:T(1,128)S(1)}, s32[16384,1]{0,1:T(1,128)}, u32[]{:S(2)}) copy-start(s32[16384,1]{0,1:T(1,128)} %param.18) | copy-start | bytes 196612
  31.6 8.6 %copy-start.8 = (s32[16384]{0:T(1024)S(1)}, s32[16384]{0:T(1024)}, u32[]{:S(2)}) copy-start(s32[16384]{0:T(1024)} %param.19) | copy-start | bytes 196612
  41.5 1.1 copy-start.1
  41.5 1.4 copy-start.2
  45.5 0.7 copy-start.4
  46.3 26.9 %collective-permute-start.2 = (f32[17,40,128]{2,1,0:T(8,128)}, f32[17,40,128]{2,1,0:T(8,128)S(1)}, u32[]{:S(2)}, u32[]{:S(2)}) collective-permute-start(f32[17,40,128]{2,1,0:T(8,128)} %get-tuple-element.58), channel_id=1, source_target_pairs={{0,4},{4,8},{8,12},{12,16},{16,20},{20,24},{24,28},{28,32},{32,36}... | collective-permute-start | bytes 1044488 | tf_op jit(solution)/shard_map/ppermute | solution.py:564
  50.4 22.9 %collective-permute-start.3 = (f32[17,40,128]{2,1,0:T(8,128)}, f32[17,40,128]{2,1,0:T(8,128)}, u32[]{:S(2)}, u32[]{:S(2)}) collective-permute-start(f32[17,40,128]{2,1,0:T(8,128)} %get-tuple-element.59), channel_id=1, source_target_pairs={{4,0},{8,4},{12,8},{16,12},{20,16},{24,20},{28,24},{32,28},{36,32}... | collective-permute-start | bytes 1044488 | tf_op jit(solution)/shard_map/ppermute | solution.py:565
  69.7 30.8 %copy-start.5 = (f32[16,40,128]{2,1,0:T(8,128)S(1)}, f32[16,40,128]{2,1,0:T(8,128)}, u32[]{:S(2)}) copy-start(f32[16,40,128]{2,1,0:T(8,128)} %copy-done.4) | copy-start | bytes 983044
  69.7 30.8 %copy-start.6 = (bf16[128,128]{1,0:T(8,128)(2,1)S(1)}, bf16[128,128]{1,0:T(8,128)(2,1)}, u32[]{:S(2)}) copy-start(bf16[128,128]{1,0:T(8,128)(2,1)} %right_ref.3) | copy-start | bytes 98308
  95.9 6.9 %collective-permute-start.4 = (bf16[128,128]{1,0:T(8,128)(2,1)S(1)}, bf16[128,128]{1,0:T(8,128)(2,1)S(1)}, u32[]{:S(2)}, u32[]{:S(2)}) collective-permute-start(bf16[128,128]{1,0:T(8,128)(2,1)S(1)} %get-tuple-element.67), channel_id=1, source_target_pairs={{0,1},{1,2},{2,3},{4,5},{5,6},{6,7},{8,9},{9,10},{10,11},{12,13},{... | collective-permute-start | bytes 98312 | tf_op jit(solution)/shard_map/ppermute | solution.py:579
  99.1 4.7 %collective-permute-start.5 = (bf16[128,128]{1,0:T(8,128)(2,1)S(1)}, bf16[128,128]{1,0:T(8,128)(2,1)S(1)}, u32[]{:S(2)}, u32[]{:S(2)}) collective-permute-start(bf16[128,128]{1,0:T(8,128)(2,1)S(1)} %get-tuple-element.68), channel_id=1, source_target_pairs={{1,0},{2,1},{3,2},{5,4},{6,5},{7,6},{9,8},{10,9},{11,10},{13,12},{... | collective-permute-start | bytes 98312 | tf_op jit(solution)/shard_map/ppermute | solution.py:580
  103.7 34.0 %copy-start.7 = (bf16[128,128]{1,0:T(8,128)(2,1)S(1)}, bf16[128,128]{1,0:T(8,128)(2,1)}, u32[]{:S(2)}) copy-start(bf16[128,128]{1,0:T(8,128)(2,1)} %strengths_ref.1) | copy-start | bytes 98308

commit v4 on v3

--- a/solution.py
+++ b/solution.py
@@ -13,6 +13,7 @@
 REACH = 3
 FRONT = 4
 WIDE = 40
+SLAB = 48
 SPAN = 32
 GROUP = 32
 PITCH = GROUP + 1
@@ -102,7 +103,7 @@
             pltpu.VMEM(remesh.shape, jnp.float32),
             pltpu.VMEM((slots, EDGE), jnp.float32),
         ],
-        compiler_params=pltpu.CompilerParams(vmem_limit_bytes=16 * 1024 * 1024),
+        compiler_params=pltpu.CompilerParams(vmem_limit_bytes=60 * 1024 * 1024),
         cost_estimate=pl.CostEstimate(flops=0, bytes_accessed=16 * 1024 * 1024, transcendentals=0),
     )(index, remesh)
 
@@ -161,43 +162,43 @@
     )(quarter, position, arrived)
 
 
-def widen_kernel(velocity_ref, stretch_ref, coupling_ref, low_ref, high_ref, wide_u, wide_s, wide_r, last_ref, first_ref):
-    back = FRONT + SPAN
-    source = [velocity_ref.at[c] for c in range(3)] + [stretch_ref.at[d] for d in range(3)]
-    source.append(coupling_ref)
-    wide = [wide_u.at[c] for c in range(3)] + [wide_s.at[d] for d in range(3)] + [wide_r]
+def widen(out_ref, centre, low, high):
+    out_ref[0:8, :] = jnp.zeros((8, EDGE), jnp.float32)
+    out_ref[WIDE - 8 : WIDE, :] = jnp.zeros((8, EDGE), jnp.float32)
+    out_ref[FRONT - REACH : FRONT, :] = low
+    out_ref[FRONT + SPAN : FRONT + SPAN + REACH, :] = high
+    out_ref[FRONT : FRONT + SPAN, :] = centre
+
+
+def field_of(velocity_ref, stretch_ref, coupling_ref, f):
+    if f < 3:
+        return velocity_ref.at[f]
+    return stretch_ref.at[f - 3] if f < 6 else coupling_ref
+
+
+def slabs_kernel(
+    velocity_ref, stretch_ref, coupling_ref, low_ref, high_ref, last_ref, first_ref, held
+):
+    blank = jnp.zeros((SLAB - WIDE, EDGE), jnp.float32)
     for f in range(7):
-
-        def one(layer, carry, f=f):
-            wide[f][layer, 0:8, :] = jnp.zeros((8, EDGE), jnp.float32)
-            wide[f][layer, WIDE - 8 : WIDE, :] = jnp.zeros((8, EDGE), jnp.float32)
-            wide[f][layer, FRONT - REACH : FRONT, :] = low_ref[f, layer]
-            wide[f][layer, back : back + REACH, :] = high_ref[f, layer]
-            wide[f][layer, FRONT:back, :] = source[f][layer]
-            return carry
-
-        lax.fori_loop(0, 16, one, 0)
-    for f in range(7):
+        field = field_of(velocity_ref, stretch_ref, coupling_ref, f)
         depth = 3 if f < 3 else 2
         at = 3 * f if f < 3 else 9 + 2 * (f - 3)
         for k in range(depth):
-            last_ref[at + k] = wide[f][16 - depth + k]
-            first_ref[at + k] = wide[f][k]
-
-
-def widened(velocity, stretch, coupling, low, high):
+            for out_ref, layer in ((last_ref, 16 - depth + k), (first_ref, k)):
+                one = held.at[0 if out_ref is last_ref else 1, at + k]
+                widen(one, field[layer], low_ref[f, layer], high_ref[f, layer])
+                out_ref[at + k] = jnp.concatenate([one[...], blank], axis=0).astype(jnp.bfloat16)
+
+
+def slabs(velocity, stretch, coupling, low, high):
     vmem = pl.BlockSpec(memory_space=pltpu.VMEM)
     return pl.pallas_call(
-        widen_kernel,
+        slabs_kernel,
         in_specs=[vmem] * 5,
-        out_specs=[vmem] * 5,
-        out_shape=[
-            jax.ShapeDtypeStruct((3, 16, WIDE, EDGE), jnp.float32),
-            jax.ShapeDtypeStruct((3, 16, WIDE, EDGE), jnp.float32),
-            jax.ShapeDtypeStruct((16, WIDE, EDGE), jnp.float32),
-            jax.ShapeDtypeStruct((17, WIDE, EDGE), jnp.float32),
-            jax.ShapeDtypeStruct((17, WIDE, EDGE), jnp.float32),
-        ],
+        out_specs=[vmem] * 2,
+        out_shape=[jax.ShapeDtypeStruct((17, SLAB, EDGE), jnp.bfloat16)] * 2,
+        scratch_shapes=[pltpu.VMEM((2, 17, WIDE, EDGE), jnp.float32)],
         compiler_params=pltpu.CompilerParams(vmem_limit_bytes=16 * 1024 * 1024),
     )(velocity, stretch, coupling, low, high)
 
@@ -228,12 +229,18 @@
     return chord % 4, entry
 
 
+def slab_layer(ref, k):
+    return ref[k].astype(jnp.float32)[:WIDE]
+
+
 def front_kernel(
     sums_ref,
     right_ref,
-    wide_u,
-    wide_s,
-    wide_r,
+    velocity_ref,
+    stretch_ref,
+    coupling_ref,
+    span_low,
+    span_high,
     low_ref,
     high_ref,
     target_ref,
@@ -243,6 +250,7 @@
     keep_ref,
     rate_ref,
     velocity,
+    metric,
     spread,
 ):
     blank = jnp.zeros((8, EDGE), jnp.float32)
@@ -258,20 +266,27 @@
 
     for c in range(3):
         for k in range(3):
-            velocity[c, k] = low_ref[3 * c + k]
-            velocity[c, 19 + k] = high_ref[3 * c + k]
+            velocity[c, k] = slab_layer(low_ref, 3 * c + k)
+            velocity[c, 19 + k] = slab_layer(high_ref, 3 * c + k)
+    for f in range(7):
+        field = field_of(velocity_ref, stretch_ref, coupling_ref, f)
         for layer in range(16):
-            velocity[c, layer + 3] = wide_u[c, layer]
+            widen(
+                velocity.at[f, layer + 3] if f < 3 else metric.at[f - 3, layer],
+                field[layer],
+                span_low[f, layer],
+                span_high[f, layer],
+            )
 
     for layer in range(20):
         inner = layer - 2
         if 0 <= inner < 16:
-            stretch = [wide_s[d, inner] for d in range(3)]
-            rate = wide_r[inner]
+            stretch = [metric[d, inner] for d in range(3)]
+            rate = metric[3, inner]
         else:
             slab, k = (low_ref, layer) if inner < 0 else (high_ref, inner - 16)
-            stretch = [slab[9 + 2 * d + k] for d in range(3)]
-            rate = slab[15 + k]
+            stretch = [slab_layer(slab, 9 + 2 * d + k) for d in range(3)]
+            rate = slab_layer(slab, 15 + k)
         squares = [(step_size * viscosity) * s * s for s in stretch]
         halves = [(0.5 * step_size) * s for s in stretch]
         keep = 1.0 - rate - 2.0 * (squares[0] + squares[1] + squares[2])
@@ -297,12 +312,13 @@
     vmem = pl.BlockSpec(memory_space=pltpu.VMEM)
     return pl.pallas_call(
         front_kernel,
-        in_specs=[vmem] * 7,
+        in_specs=[vmem] * 9,
         out_specs=[vmem] * 6,
         out_shape=[jax.ShapeDtypeStruct((3, 20, WIDE, EDGE), jnp.float32)] * 4
         + [jax.ShapeDtypeStruct((20, WIDE, EDGE), jnp.float32)] * 2,
         scratch_shapes=[
             pltpu.VMEM((3, 22, WIDE, EDGE), jnp.float32),
+            pltpu.VMEM((4, 16, WIDE, EDGE), jnp.float32),
             pltpu.VMEM((2, 64 * ROW_PITCH, EDGE), jnp.float32),
         ],
         compiler_params=pltpu.CompilerParams(vmem_limit_bytes=16 * 1024 * 1024),
@@ -550,19 +566,18 @@
         jnp.concatenate([f[:, :, :REACH] for f in fields], axis=0), "span", backward
     )
 
+    last, opening = slabs(velocity, stretch, coupling, low, high)
+    extended = (velocity, stretch, coupling, low, high)
+    block_forward, block_backward = chain(blocks)
+    low = lax.ppermute(last, "blk", block_forward)
+    high = lax.ppermute(opening, "blk", block_backward)
+
     destinations = mine(row_dest.T, grid_count)
     row_places = mine(row_place, grid_count)
     dest_mine = lax.dynamic_index_in_dim(destinations, my_block, 0, keepdims=False)
     row_slot = dest_mine * row_cap + slot_ranks(dest_mine, blocks)
     row_where = arrival_places(destinations, row_places, my_block, row_cap)
     remesh_rows = gathered_rows(row_where, remesh)
-    low, high, position, row_slot, remesh_rows = lax.optimization_barrier(
-        (low, high, position, row_slot, remesh_rows)
-    )
-    *extended, last, opening = widened(velocity, stretch, coupling, low, high)
-    block_forward, block_backward = chain(blocks)
-    low = lax.ppermute(last, "blk", block_forward)
-    high = lax.ppermute(opening, "blk", block_backward)
 
     arrived, position, row_slot, remesh_rows = lax.optimization_barrier(
         (arrived, position, row_slot, remesh_rows)

time: 140 us -> 138 us (0.986)
  starting transfers between devices: 30 us -> 28 us
    pallas_call x1, Pallas kernels: 4.32 us -> 6.16 us  [gathered_rows(): pl.pallas_call(gather_kernel, in_specs=[pl.BlockSpec(memory_space=pltpu.S...]
    pallas_call x1, Pallas kernels: 3.46 us -> 1.82 us  [tile_sums(): pl.pallas_call(sums_kernel, in_specs=[pl.BlockSpec(memory_space=pltpu.SME...]
    ppermute x1, starting transfers between devices: 4.69 us -> 3.12 us  [shards(): lax.ppermute(jnp.concatenate([f[:, :, -REACH:] for f in fields], axis=0),...]
    another operation x2, local copies, waits for them, and re-layouts: 0.22 us -> 1.72 us  [mine(): whole = rows.reshape(blocks, spans, count)]
  transfers between devices with their start and end apart: 7 -> 7, of which waited for: 2 -> 2; matrix products, arithmetic and copies ran while one was open for 10% -> 11% of each run, Pallas kernels for 9% -> 9%
where the time goes in v4:
time: 138 us; the launch traced here: 137 us
  blocking collectives  53.3 us (39%)
  starting transfers between devices  28 us (20%)
  Pallas kernels  20.2 us (15%)
  waiting for transfers between devices  18.3 us (13%)
  local copies, waits for them, and re-layouts  7.51 us (5%)
  other arithmetic  6.11 us (4%)
  matrix products  2.79 us (2%)
    all_to_all x1, blocking collectives, shards(): lax.all_to_all(outgoing.reshape(blocks, row_cap, EDGE), 'blk', split_axis...  30.5 us
    all_to_all x1, blocking collectives, shards(): lax.all_to_all(sums.reshape(blocks, 16, 2 * EDGE), 'blk', split_axis=0, c...  22.8 us
    all_to_all x1, waiting for transfers between devices, shards(): lax.all_to_all(pieces, 'blk', split_axis=0, concat_axis=0, tiled=True)  17.9 us
    all_to_all x1, starting transfers between devices, shards(): lax.all_to_all(pieces, 'blk', split_axis=0, concat_axis=0, tiled=True)  13.3 us
    pallas_call x1, Pallas kernels, gathered_rows(): pl.pallas_call(gather_kernel, in_specs=[pl.BlockSpec(memory_space=pltpu.S...  6.16 us
    pallas_call x1, Pallas kernels, tile_pieces(): pl.pallas_call(pieces_kernel, grid=(tiles // GROUP,), in_specs=[pl.BlockS...  4.22 us
    ppermute x1, starting transfers between devices, shards(): low = lax.ppermute(last, 'blk', block_forward)  3.81 us
    pallas_call x1, Pallas kernels, grid_update(): pl.pallas_call(grid_kernel, in_specs=[vmem] * 9 + [pl.BlockSpec(memory_sp...  3.51 us
  transfers between devices with their start and end apart: 7, of which 2 were waited for; matrix products, arithmetic and copies ran while one was open for 11% of the time, Pallas kernels for 9%

profile of v4, /device:TPU:1, one launch (start us, length us, event | category | flops | bytes accessed | tf_op | source)
XLA Modules:
  0.0 137.2 jit_solution(14497185926336991745)
XLA Ops:
  0.6 4.2 %shard_map.122 = bf16[64,64,256]{2,1,0:T(8,128)(2,1)} custom-call(bf16[8192,128]{1,0:T(8,128)(2,1)} %remesh_ref.3, bf16[128,128]{1,0:T(8,128)(2,1)} %strengths_ref.1, bf16[128,128]{1,0:T(8,128)(2,1)} %left_ref.1), custom_call_target="tpu_custom_call" | custom-call | tf_op jit(solution)/shard_map/pallas_call | solution.py:64
  4.9 13.3 %all-to-all-start = ((bf16[64,64,256]{2,1,0:T(8,128)(2,1)}), bf16[64,64,256]{2,1,0:T(8,128)(2,1)S(1)}, u32[]{:S(2)}, u32[]{:S(2)}) async-start(bf16[64,64,256]{2,1,0:T(8,128)(2,1)} %shard_map.122), calls=%async_computation | async-start | bytes 4194304 | tf_op jit(solution)/shard_map/all_to_all | solution.py:543
  18.2 1.1 fusion.11
  19.3 0.7 pad_maximum_fusion
  20.1 3.1 %collective-permute-start = (f32[7,16,3,128]{3,2,1,0:T(4,128)}, f32[7,16,3,128]{3,2,1,0:T(4,128)S(1)}, u32[]{:S(2)}, u32[]{:S(2)}) collective-permute-start(f32[7,16,3,128]{3,2,1,0:T(4,128)} %pad_maximum_fusion), channel_id=1, source_target_pairs={{0,1},{1,2},{2,3},{4,5},{5,6},{6,7},{8,9},{9,10},{10,11},{12,13},{... | collective-permute-start | bytes 516104 | tf_op jit(solution)/shard_map/ppermute | solution.py:562
  23.2 0.7 pad_maximum_fusion.1
  23.9 1.3 collective-permute-start.1
  25.2 0.5 broadcast.24
  25.7 0.8 reduce.9
  26.5 0.8 reshape_reshape_transpose.3
  27.3 0.9 reshape_reshape.3
  28.3 1.0 add_reduce_fusion
  29.4 1.5 %constant_dynamic-slice_fusion = (s32[64,12,128]{2,1,0:T(8,128)S(1)}, s32[64,12,128]{2,1,0:T(8,128)S(1)}) fusion(s32[64,48,128]{2,1,0:T(8,128)} %bitcast.31, s32[]{:T(128)S(6)} %select_n.28, s32[64,48,128]{2,1,0:T(8,128)} %bitcast.32), kind=kLoop, calls=%fused_computation.24 | loop fusion | bytes 1572868 | tf_op jit(solution)/shard_map/dynamic_slice | solution.py:548
  31.2 0.7 copy-done.6
  31.9 0.7 fusion.4
  32.6 2.8 %select_reduce_fusion = s32[64,48]{1,0:T(8,128)S(1)} fusion(s32[64,1536]{1,0:T(8,128)S(1)} %bitcast.28, s32[64,1536]{1,0:T(8,128)S(1)} %fusion.4), kind=kLoop, calls=%fused_computation | loop fusion | flops 14152704 | bytes 798720 | tf_op jit(solution)/shard_map/reduce_sum | solution.py:507
  35.4 0.7 reshape.69.index_ref
  36.1 6.2 %shard_map.123 = bf16[3072,128]{1,0:T(8,128)(2,1)} custom-call(s32[3072]{0:T(1024)} %reshape.69.index_ref, bf16[8192,128]{1,0:T(8,128)(2,1)} %remesh_ref.3), custom_call_target="tpu_custom_call" | custom-call | bytes 16777216 | tf_op jit(solution)/shard_map/pallas_call | solution.py:94
  42.3 0.8 dynamic-slice_reduce_fusion
  43.1 1.0 fusion.5
  44.2 1.8 %shard_map.125 = (bf16[17,48,128]{2,1,0:T(8,128)(2,1)}, bf16[17,48,128]{2,1,0:T(8,128)(2,1)}) custom-call(f32[3,16,32,128]{3,2,1,0:T(8,128)S(1)} %copy-done, f32[3,16,32,128]{3,2,1,0:T(8,128)S(1)} %copy-done.1, f32[16,32,128]{2,1,0:T(8,128)S(1)} %copy-done.3, f32[7,16,3,128]{3,2,1,0:T(4,128)S(1)} %collective-permute-done.low_ref.span_low, ...), custom_call_target="tpu_custom_call" | custom-call | tf_op jit(solution)/shard_map/pallas_call | solution.py:196
  46.0 3.8 %collective-permute-start.2 = (bf16[17,48,128]{2,1,0:T(8,128)(2,1)}, bf16[17,48,128]{2,1,0:T(8,128)(2,1)}, u32[]{:S(2)}, u32[]{:S(2)}) collective-permute-start(bf16[17,48,128]{2,1,0:T(8,128)(2,1)} %get-tuple-element.44), channel_id=1, source_target_pairs={{0,4},{4,8},{8,12},{12,16},{16,20},{20,24},{24,28},{28,32},{32,36}... | collective-permute-start | bytes 626696 | tf_op jit(solution)/shard_map/ppermute | solution.py:572
  49.8 1.9 %collective-permute-start.3 = (bf16[17,48,128]{2,1,0:T(8,128)(2,1)}, bf16[17,48,128]{2,1,0:T(8,128)(2,1)}, u32[]{:S(2)}, u32[]{:S(2)}) collective-permute-start(bf16[17,48,128]{2,1,0:T(8,128)(2,1)} %get-tuple-element.45), channel_id=1, source_target_pairs={{4,0},{8,4},{12,8},{16,12},{20,16},{24,20},{28,24},{32,28},{36,32}... | collective-permute-start | bytes 626696 | tf_op jit(solution)/shard_map/ppermute | solution.py:573
  51.8 17.9 %all-to-all-done = bf16[64,64,256]{2,1,0:T(8,128)(2,1)S(1)} async-done(((bf16[64,64,256]{2,1,0:T(8,128)(2,1)}), bf16[64,64,256]{2,1,0:T(8,128)(2,1)S(1)}, u32[]{:S(2)}, u32[]{:S(2)}) %all-to-all-start) | async-done | bytes 2097184 | tf_op jit(solution)/shard_map/all_to_all | solution.py:543
  69.6 1.8 %shard_map.124 = bf16[1024,256]{1,0:T(8,128)(2,1)S(1)} custom-call(s32[1]{0:T(128)} %bitcast.quarter_ref, s32[1,4096]{1,0:T(1,128)S(1)} %add.37.position_ref, bf16[4096,256]{1,0:T(8,128)(2,1)S(1)} %bitcast.20), custom_call_target="tpu_custom_call" | custom-call | tf_op jit(solution)/shard_map/pallas_call | solution.py:155
  71.5 22.8 %all_to_all.15.sums_ref = bf16[64,16,256]{2,1,0:T(8,128)(2,1)S(1)} all-to-all(bf16[64,16,256]{2,1,0:T(8,128)(2,1)S(1)} %bitcast.22), channel_id=1, replica_groups=mesh['blk'=64,'span'=4] {'blk'}, dimensions={0} | all-to-all | bytes 1048576 | tf_op jit(solution)/shard_map/all_to_all | solution.py:587
  94.3 3.1 %collective-permute-start.4 = (bf16[128,128]{1,0:T(8,128)(2,1)S(1)}, bf16[128,128]{1,0:T(8,128)(2,1)S(1)}, u32[]{:S(2)}, u32[]{:S(2)}) collective-permute-start(bf16[128,128]{1,0:T(8,128)(2,1)S(1)} %get-tuple-element.55), channel_id=1, source_target_pairs={{0,1},{1,2},{2,3},{4,5},{5,6},{6,7},{8,9},{9,10},{10,11},{12,13},{... | collective-permute-start | bytes 98312 | tf_op jit(solution)/shard_map/ppermute | solution.py:594
  97.4 1.5 %collective-permute-start.5 = (bf16[128,128]{1,0:T(8,128)(2,1)S(1)}, bf16[128,128]{1,0:T(8,128)(2,1)S(1)}, u32[]{:S(2)}, u32[]{:S(2)}) collective-permute-start(bf16[128,128]{1,0:T(8,128)(2,1)S(1)} %get-tuple-element.56), channel_id=1, source_target_pairs={{1,0},{2,1},{3,2},{5,4},{6,5},{7,6},{9,8},{10,9},{11,10},{13,12},{... | collective-permute-start | bytes 98312 | tf_op jit(solution)/shard_map/ppermute | solution.py:595
  98.9 2.7 %shard_map.126 = (f32[3,20,40,128]{3,2,1,0:T(8,128)S(1)}, f32[3,20,40,128]{3,2,1,0:T(8,128)S(1)}, f32[3,20,40,128]{3,2,1,0:T(8,128)S(1)}, f32[3,20,40,128]{3,2,1...) custom-call(bf16[1024,256]{1,0:T(8,128)(2,1)S(1)} %bitcast.21, bf16[128,128]{1,0:T(8,128)(2,1)S(1)} %copy-done.4, ...), custom_call_target="tpu_custom_call" | custom-call | flops 164000000 | bytes 8388608 | tf_op jit(solution)/shard_map/pallas_call | solution.py:313
  102.1 3.5 %shard_map.128 = (f32[3,16,32,128]{3,2,1,0:T(8,128)}, bf16[3072,128]{1,0:T(8,128)(2,1)S(1)}) custom-call(f32[3,20,40,128]{3,2,1,0:T(8,128)S(1)} %get-tuple-element.54.target_ref, bf16[128,128]{1,0:T(8,128)(2,1)S(1)} %collective-permute-done.4.low_ref, bf16[128,128]{1,0:T(8,128)(2,1)S(1)} %collective-permute-done.5.high_ref, bf16[128,128]{1,0:T(8,128)(2,1)S(1)} %copy-done.4, ...), custom_call_target="tpu_custom_call" | custom-call | tf_op jit(solution)/shard_map/pallas_call | solution.py:440
  105.6 30.5 %all_to_all.16 = bf16[64,48,128]{2,1,0:T(8,128)(2,1)S(1)} all-to-all(bf16[64,48,128]{2,1,0:T(8,128)(2,1)S(1)} %bitcast.24), channel_id=1, replica_groups=mesh['blk'=64,'span'=4] {'blk'}, dimensions={0} | all-to-all | bytes 1572864 | tf_op jit(solution)/shard_map/all_to_all | solution.py:608
  136.1 1.0 fusion.6
  (29 shorter events, 0.9 us)
Async XLA Ops:
  4.8 13.3 %copy-start.3 = (f32[16,32,128]{2,1,0:T(8,128)S(1)}, f32[16,32,128]{2,1,0:T(8,128)}, u32[]{:S(2)}) copy-start(f32[16,32,128]{2,1,0:T(8,128)} %coupling_ref.1) | copy-start | bytes 786436
  4.9 13.3 %copy-start = (f32[3,16,32,128]{3,2,1,0:T(8,128)S(1)}, f32[3,16,32,128]{3,2,1,0:T(8,128)}, u32[]{:S(2)}) copy-start(f32[3,16,32,128]{3,2,1,0:T(8,128)} %velocity_ref.1) | copy-start | bytes 2359300
  4.9 20.9 %copy-start.8 = (s32[16384,1]{0,1:T(1,128)S(1)}, s32[16384,1]{0,1:T(1,128)}, u32[]{:S(2)}) copy-start(s32[16384,1]{0,1:T(1,128)} %param.18) | copy-start | bytes 196612
  4.9 64.8 %all-to-all-start = ((bf16[64,64,256]{2,1,0:T(8,128)(2,1)}), bf16[64,64,256]{2,1,0:T(8,128)(2,1)S(1)}, u32[]{:S(2)}, u32[]{:S(2)}) async-start(bf16[64,64,256]{2,1,0:T(8,128)(2,1)} %shard_map.122), calls=%async_computation | async-start | bytes 4194304 | tf_op jit(solution)/shard_map/all_to_all | solution.py:543
  20.1 24.1 %collective-permute-start = (f32[7,16,3,128]{3,2,1,0:T(4,128)}, f32[7,16,3,128]{3,2,1,0:T(4,128)S(1)}, u32[]{:S(2)}, u32[]{:S(2)}) collective-permute-start(f32[7,16,3,128]{3,2,1,0:T(4,128)} %pad_maximum_fusion), channel_id=1, source_target_pairs={{0,1},{1,2},{2,3},{4,5},{5,6},{6,7},{8,9},{9,10},{10,11},{12,13},{... | collective-permute-start | bytes 516104 | tf_op jit(solution)/shard_map/ppermute | solution.py:562
  23.9 20.2 %collective-permute-start.1 = (f32[7,16,3,128]{3,2,1,0:T(4,128)}, f32[7,16,3,128]{3,2,1,0:T(4,128)}, u32[]{:S(2)}, u32[]{:S(2)}) collective-permute-start(f32[7,16,3,128]{3,2,1,0:T(4,128)} %pad_maximum_fusion.1), channel_id=1, source_target_pairs={{1,0},{2,1},{3,2},{5,4},{6,5},{7,6},{9,8},{10,9},{11,10},{13,12},{... | collective-permute-start | bytes 516104 | tf_op jit(solution)/shard_map/ppermute | solution.py:565
  31.2 0.7 copy-start.6
  43.1 1.1 copy-start.1
  46.0 25.5 %collective-permute-start.2 = (bf16[17,48,128]{2,1,0:T(8,128)(2,1)}, bf16[17,48,128]{2,1,0:T(8,128)(2,1)}, u32[]{:S(2)}, u32[]{:S(2)}) collective-permute-start(bf16[17,48,128]{2,1,0:T(8,128)(2,1)} %get-tuple-element.44), channel_id=1, source_target_pairs={{0,4},{4,8},{8,12},{12,16},{16,20},{20,24},{24,28},{28,32},{32,36}... | collective-permute-start | bytes 626696 | tf_op jit(solution)/shard_map/ppermute | solution.py:572
  49.8 21.6 %collective-permute-start.3 = (bf16[17,48,128]{2,1,0:T(8,128)(2,1)}, bf16[17,48,128]{2,1,0:T(8,128)(2,1)}, u32[]{:S(2)}, u32[]{:S(2)}) collective-permute-start(bf16[17,48,128]{2,1,0:T(8,128)(2,1)} %get-tuple-element.45), channel_id=1, source_target_pairs={{4,0},{8,4},{12,8},{16,12},{20,16},{24,20},{28,24},{32,28},{36,32}... | collective-permute-start | bytes 626696 | tf_op jit(solution)/shard_map/ppermute | solution.py:573
  69.6 29.3 %copy-start.2 = (f32[3,16,32,128]{3,2,1,0:T(8,128)S(1)}, f32[3,16,32,128]{3,2,1,0:T(8,128)}, u32[]{:S(2)}) copy-start(f32[3,16,32,128]{3,2,1,0:T(8,128)} %stretch_ref.1) | copy-start | bytes 2359300
  69.6 29.3 %copy-start.4 = (bf16[128,128]{1,0:T(8,128)(2,1)S(1)}, bf16[128,128]{1,0:T(8,128)(2,1)}, u32[]{:S(2)}) copy-start(bf16[128,128]{1,0:T(8,128)(2,1)} %right_ref.3) | copy-start | bytes 98308
  94.3 7.3 %collective-permute-start.4 = (bf16[128,128]{1,0:T(8,128)(2,1)S(1)}, bf16[128,128]{1,0:T(8,128)(2,1)S(1)}, u32[]{:S(2)}, u32[]{:S(2)}) collective-permute-start(bf16[128,128]{1,0:T(8,128)(2,1)S(1)} %get-tuple-element.55), channel_id=1, source_target_pairs={{0,1},{1,2},{2,3},{4,5},{5,6},{6,7},{8,9},{9,10},{10,11},{12,13},{... | collective-permute-start | bytes 98312 | tf_op jit(solution)/shard_map/ppermute | solution.py:594
  97.4 4.7 %collective-permute-start.5 = (bf16[128,128]{1,0:T(8,128)(2,1)S(1)}, bf16[128,128]{1,0:T(8,128)(2,1)S(1)}, u32[]{:S(2)}, u32[]{:S(2)}) collective-permute-start(bf16[128,128]{1,0:T(8,128)(2,1)S(1)} %get-tuple-element.56), channel_id=1, source_target_pairs={{1,0},{2,1},{3,2},{5,4},{6,5},{7,6},{9,8},{10,9},{11,10},{13,12},{... | collective-permute-start | bytes 98312 | tf_op jit(solution)/shard_map/ppermute | solution.py:595
  102.1 34.0 %copy-start.5 = (bf16[3072,128]{1,0:T(8,128)(2,1)S(1)}, bf16[3072,128]{1,0:T(8,128)(2,1)}, u32[]{:S(2)}) copy-start(bf16[3072,128]{1,0:T(8,128)(2,1)} %shard_map.123) | copy-start | bytes 2359300
  102.1 34.0 %copy-start.7 = (bf16[128,128]{1,0:T(8,128)(2,1)S(1)}, bf16[128,128]{1,0:T(8,128)(2,1)}, u32[]{:S(2)}) copy-start(bf16[128,128]{1,0:T(8,128)(2,1)} %strengths_ref.1) | copy-start | bytes 98308

commit v5 on v4

--- a/solution.py
+++ b/solution.py
@@ -71,7 +71,7 @@
         ],
         out_specs=pl.BlockSpec((64, GROUP, 2 * EDGE), lambda g: (0, g, 0)),
         out_shape=jax.ShapeDtypeStruct((64, tiles, 2 * EDGE), jnp.bfloat16),
-        scratch_shapes=[pltpu.VMEM((2, 64 * PITCH, EDGE), jnp.float32)],
+        scratch_shapes=[pltpu.VMEM((2, 65 * PITCH, EDGE), jnp.float32)],
         compiler_params=pltpu.CompilerParams(vmem_limit_bytes=60 * 1024 * 1024),
     )(remesh, strengths, left)
 
@@ -157,7 +157,7 @@
         in_specs=[pl.BlockSpec(memory_space=pltpu.SMEM), vmem, vmem],
         out_specs=vmem,
         out_shape=jax.ShapeDtypeStruct((1024, 2 * EDGE), jnp.bfloat16),
-        scratch_shapes=[pltpu.VMEM((2, 64 * ROW_PITCH, EDGE), jnp.float32)],
+        scratch_shapes=[pltpu.VMEM((2, 65 * ROW_PITCH, EDGE), jnp.float32)],
         compiler_params=pltpu.CompilerParams(vmem_limit_bytes=16 * 1024 * 1024),
     )(quarter, position, arrived)
 
@@ -319,7 +319,7 @@
         scratch_shapes=[
             pltpu.VMEM((3, 22, WIDE, EDGE), jnp.float32),
             pltpu.VMEM((4, 16, WIDE, EDGE), jnp.float32),
-            pltpu.VMEM((2, 64 * ROW_PITCH, EDGE), jnp.float32),
+            pltpu.VMEM((2, 65 * ROW_PITCH, EDGE), jnp.float32),
         ],
         compiler_params=pltpu.CompilerParams(vmem_limit_bytes=16 * 1024 * 1024),
         cost_estimate=pl.CostEstimate(
@@ -353,8 +353,8 @@
     right = right_ref[...]
     back = FRONT + SPAN
     lanes = lax.broadcasted_iota(jnp.int32, (WIDE, EDGE), 1)
-    side_sums[0] = jnp.dot(low_ref[...], right, preferred_element_type=jnp.float32)
-    side_sums[1] = jnp.dot(high_ref[...], right, preferred_element_type=jnp.float32)
+    for side, ref in enumerate((low_ref, high_ref)):
+        side_sums[side, 0:128, :] = jnp.dot(ref[...], right, preferred_element_type=jnp.float32)
     slots[...] = jnp.zeros_like(slots)
     for c in range(3):
         for layer in range(20):
@@ -446,7 +446,7 @@
             jax.ShapeDtypeStruct((2 * slot.shape[0], EDGE), jnp.bfloat16),
         ],
         scratch_shapes=[
-            pltpu.VMEM((2, 128, EDGE), jnp.float32),
+            pltpu.VMEM((2, 144, EDGE), jnp.float32),
             pltpu.VMEM((3, 20, WIDE, EDGE), jnp.float32),
             pltpu.VMEM((3, 20, WIDE, EDGE), jnp.float32),
             pltpu.VMEM((3, 18, WIDE, EDGE), jnp.float32),

time: 138 us -> 138 us (level)
  no operation moved by 1% of the time
where the time goes in v5:
time: 138 us; the launch traced here: 137 us
  blocking collectives  53.3 us (39%)
  starting transfers between devices  28 us (20%)
  Pallas kernels  20.2 us (15%)
  waiting for transfers between devices  18.3 us (13%)
  local copies, waits for them, and re-layouts  7.51 us (5%)
  other arithmetic  6.11 us (4%)
  matrix products  2.78 us (2%)
    all_to_all x1, blocking collectives, shards(): lax.all_to_all(outgoing.reshape(blocks, row_cap, EDGE), 'blk', split_axis...  30.5 us
    all_to_all x1, blocking collectives, shards(): lax.all_to_all(sums.reshape(blocks, 16, 2 * EDGE), 'blk', split_axis=0, c...  22.8 us
    all_to_all x1, waiting for transfers between devices, shards(): lax.all_to_all(pieces, 'blk', split_axis=0, concat_axis=0, tiled=True)  17.9 us
    all_to_all x1, starting transfers between devices, shards(): lax.all_to_all(pieces, 'blk', split_axis=0, concat_axis=0, tiled=True)  13.3 us
    pallas_call x1, Pallas kernels, gathered_rows(): pl.pallas_call(gather_kernel, in_specs=[pl.BlockSpec(memory_space=pltpu.S...  6.16 us
    pallas_call x1, Pallas kernels, tile_pieces(): pl.pallas_call(pieces_kernel, grid=(tiles // GROUP,), in_specs=[pl.BlockS...  4.25 us
    ppermute x1, starting transfers between devices, shards(): low = lax.ppermute(last, 'blk', block_forward)  3.81 us
    pallas_call x1, Pallas kernels, grid_update(): pl.pallas_call(grid_kernel, in_specs=[vmem] * 9 + [pl.BlockSpec(memory_sp...  3.51 us
  transfers between devices with their start and end apart: 7, of which 2 were waited for; matrix products, arithmetic and copies ran while one was open for 11% of the time, Pallas kernels for 9%

profile of v5, /device:TPU:1, one launch (start us, length us, event | category | flops | bytes accessed | tf_op | source)
XLA Modules:
  0.0 137.2 jit_solution(7388795829066343913)
XLA Ops:
  0.6 4.3 %shard_map.122 = bf16[64,64,256]{2,1,0:T(8,128)(2,1)} custom-call(bf16[8192,128]{1,0:T(8,128)(2,1)} %remesh_ref.3, bf16[128,128]{1,0:T(8,128)(2,1)} %strengths_ref.1, bf16[128,128]{1,0:T(8,128)(2,1)} %left_ref.1), custom_call_target="tpu_custom_call" | custom-call | tf_op jit(solution)/shard_map/pallas_call | solution.py:64
  4.9 13.3 %all-to-all-start = ((bf16[64,64,256]{2,1,0:T(8,128)(2,1)}), bf16[64,64,256]{2,1,0:T(8,128)(2,1)S(1)}, u32[]{:S(2)}, u32[]{:S(2)}) async-start(bf16[64,64,256]{2,1,0:T(8,128)(2,1)} %shard_map.122), calls=%async_computation | async-start | bytes 4194304 | tf_op jit(solution)/shard_map/all_to_all | solution.py:543
  18.2 1.1 fusion.11
  19.3 0.7 pad_maximum_fusion
  20.1 3.1 %collective-permute-start = (f32[7,16,3,128]{3,2,1,0:T(4,128)}, f32[7,16,3,128]{3,2,1,0:T(4,128)S(1)}, u32[]{:S(2)}, u32[]{:S(2)}) collective-permute-start(f32[7,16,3,128]{3,2,1,0:T(4,128)} %pad_maximum_fusion), channel_id=1, source_target_pairs={{0,1},{1,2},{2,3},{4,5},{5,6},{6,7},{8,9},{9,10},{10,11},{12,13},{... | collective-permute-start | bytes 516104 | tf_op jit(solution)/shard_map/ppermute | solution.py:562
  23.2 0.7 pad_maximum_fusion.1
  23.9 1.3 collective-permute-start.1
  25.2 0.5 broadcast.24
  25.8 0.8 reduce.9
  26.6 0.8 reshape_reshape_transpose.3
  27.3 0.9 reshape_reshape.3
  28.3 1.0 add_reduce_fusion
  29.4 1.5 %constant_dynamic-slice_fusion = (s32[64,12,128]{2,1,0:T(8,128)S(1)}, s32[64,12,128]{2,1,0:T(8,128)S(1)}) fusion(s32[64,48,128]{2,1,0:T(8,128)} %bitcast.31, s32[]{:T(128)S(6)} %select_n.28, s32[64,48,128]{2,1,0:T(8,128)} %bitcast.32), kind=kLoop, calls=%fused_computation.24 | loop fusion | bytes 1572868 | tf_op jit(solution)/shard_map/dynamic_slice | solution.py:548
  31.2 0.7 copy-done.6
  32.0 0.7 fusion.4
  32.7 2.8 %select_reduce_fusion = s32[64,48]{1,0:T(8,128)S(1)} fusion(s32[64,1536]{1,0:T(8,128)S(1)} %bitcast.28, s32[64,1536]{1,0:T(8,128)S(1)} %fusion.4), kind=kLoop, calls=%fused_computation | loop fusion | flops 14152704 | bytes 798720 | tf_op jit(solution)/shard_map/reduce_sum | solution.py:507
  35.4 0.7 reshape.69.index_ref
  36.1 6.2 %shard_map.123 = bf16[3072,128]{1,0:T(8,128)(2,1)} custom-call(s32[3072]{0:T(1024)} %reshape.69.index_ref, bf16[8192,128]{1,0:T(8,128)(2,1)} %remesh_ref.3), custom_call_target="tpu_custom_call" | custom-call | bytes 16777216 | tf_op jit(solution)/shard_map/pallas_call | solution.py:94
  42.3 0.8 dynamic-slice_reduce_fusion
  43.1 1.0 fusion.5
  44.2 1.8 %shard_map.125 = (bf16[17,48,128]{2,1,0:T(8,128)(2,1)}, bf16[17,48,128]{2,1,0:T(8,128)(2,1)}) custom-call(f32[3,16,32,128]{3,2,1,0:T(8,128)S(1)} %copy-done, f32[3,16,32,128]{3,2,1,0:T(8,128)S(1)} %copy-done.1, f32[16,32,128]{2,1,0:T(8,128)S(1)} %copy-done.3, f32[7,16,3,128]{3,2,1,0:T(4,128)S(1)} %collective-permute-done.low_ref.span_low, ...), custom_call_target="tpu_custom_call" | custom-call | tf_op jit(solution)/shard_map/pallas_call | solution.py:196
  46.1 3.8 %collective-permute-start.2 = (bf16[17,48,128]{2,1,0:T(8,128)(2,1)}, bf16[17,48,128]{2,1,0:T(8,128)(2,1)}, u32[]{:S(2)}, u32[]{:S(2)}) collective-permute-start(bf16[17,48,128]{2,1,0:T(8,128)(2,1)} %get-tuple-element.44), channel_id=1, source_target_pairs={{0,4},{4,8},{8,12},{12,16},{16,20},{20,24},{24,28},{28,32},{32,36}... | collective-permute-start | bytes 626696 | tf_op jit(solution)/shard_map/ppermute | solution.py:572
  49.9 1.9 %collective-permute-start.3 = (bf16[17,48,128]{2,1,0:T(8,128)(2,1)}, bf16[17,48,128]{2,1,0:T(8,128)(2,1)}, u32[]{:S(2)}, u32[]{:S(2)}) collective-permute-start(bf16[17,48,128]{2,1,0:T(8,128)(2,1)} %get-tuple-element.45), channel_id=1, source_target_pairs={{4,0},{8,4},{12,8},{16,12},{20,16},{24,20},{28,24},{32,28},{36,32}... | collective-permute-start | bytes 626696 | tf_op jit(solution)/shard_map/ppermute | solution.py:573
  51.8 17.9 %all-to-all-done = bf16[64,64,256]{2,1,0:T(8,128)(2,1)S(1)} async-done(((bf16[64,64,256]{2,1,0:T(8,128)(2,1)}), bf16[64,64,256]{2,1,0:T(8,128)(2,1)S(1)}, u32[]{:S(2)}, u32[]{:S(2)}) %all-to-all-start) | async-done | bytes 2097184 | tf_op jit(solution)/shard_map/all_to_all | solution.py:543
  69.7 1.8 %shard_map.124 = bf16[1024,256]{1,0:T(8,128)(2,1)S(1)} custom-call(s32[1]{0:T(128)} %bitcast.quarter_ref, s32[1,4096]{1,0:T(1,128)S(1)} %add.37.position_ref, bf16[4096,256]{1,0:T(8,128)(2,1)S(1)} %bitcast.20), custom_call_target="tpu_custom_call" | custom-call | tf_op jit(solution)/shard_map/pallas_call | solution.py:155
  71.5 22.8 %all_to_all.15.sums_ref = bf16[64,16,256]{2,1,0:T(8,128)(2,1)S(1)} all-to-all(bf16[64,16,256]{2,1,0:T(8,128)(2,1)S(1)} %bitcast.22), channel_id=1, replica_groups=mesh['blk'=64,'span'=4] {'blk'}, dimensions={0} | all-to-all | bytes 1048576 | tf_op jit(solution)/shard_map/all_to_all | solution.py:587
  94.3 3.1 %collective-permute-start.4 = (bf16[128,128]{1,0:T(8,128)(2,1)S(1)}, bf16[128,128]{1,0:T(8,128)(2,1)S(1)}, u32[]{:S(2)}, u32[]{:S(2)}) collective-permute-start(bf16[128,128]{1,0:T(8,128)(2,1)S(1)} %get-tuple-element.55), channel_id=1, source_target_pairs={{0,1},{1,2},{2,3},{4,5},{5,6},{6,7},{8,9},{9,10},{10,11},{12,13},{... | collective-permute-start | bytes 98312 | tf_op jit(solution)/shard_map/ppermute | solution.py:594
  97.5 1.5 %collective-permute-start.5 = (bf16[128,128]{1,0:T(8,128)(2,1)S(1)}, bf16[128,128]{1,0:T(8,128)(2,1)S(1)}, u32[]{:S(2)}, u32[]{:S(2)}) collective-permute-start(bf16[128,128]{1,0:T(8,128)(2,1)S(1)} %get-tuple-element.56), channel_id=1, source_target_pairs={{1,0},{2,1},{3,2},{5,4},{6,5},{7,6},{9,8},{10,9},{11,10},{13,12},{... | collective-permute-start | bytes 98312 | tf_op jit(solution)/shard_map/ppermute | solution.py:595
  99.0 2.7 %shard_map.126 = (f32[3,20,40,128]{3,2,1,0:T(8,128)S(1)}, f32[3,20,40,128]{3,2,1,0:T(8,128)S(1)}, f32[3,20,40,128]{3,2,1,0:T(8,128)S(1)}, f32[3,20,40,128]{3,2,1...) custom-call(bf16[1024,256]{1,0:T(8,128)(2,1)S(1)} %bitcast.21, bf16[128,128]{1,0:T(8,128)(2,1)S(1)} %copy-done.4, ...), custom_call_target="tpu_custom_call" | custom-call | flops 164000000 | bytes 8388608 | tf_op jit(solution)/shard_map/pallas_call | solution.py:313
  102.1 3.5 %shard_map.128 = (f32[3,16,32,128]{3,2,1,0:T(8,128)}, bf16[3072,128]{1,0:T(8,128)(2,1)S(1)}) custom-call(f32[3,20,40,128]{3,2,1,0:T(8,128)S(1)} %get-tuple-element.54.target_ref, bf16[128,128]{1,0:T(8,128)(2,1)S(1)} %collective-permute-done.4.low_ref, bf16[128,128]{1,0:T(8,128)(2,1)S(1)} %collective-permute-done.5.high_ref, bf16[128,128]{1,0:T(8,128)(2,1)S(1)} %copy-done.4, ...), custom_call_target="tpu_custom_call" | custom-call | tf_op jit(solution)/shard_map/pallas_call | solution.py:440
  105.6 30.5 %all_to_all.16 = bf16[64,48,128]{2,1,0:T(8,128)(2,1)S(1)} all-to-all(bf16[64,48,128]{2,1,0:T(8,128)(2,1)S(1)} %bitcast.24), channel_id=1, replica_groups=mesh['blk'=64,'span'=4] {'blk'}, dimensions={0} | all-to-all | bytes 1572864 | tf_op jit(solution)/shard_map/all_to_all | solution.py:608
  136.1 1.0 fusion.6
  (29 shorter events, 1.0 us)
Async XLA Ops:
  4.9 13.3 %copy-start.3 = (f32[16,32,128]{2,1,0:T(8,128)S(1)}, f32[16,32,128]{2,1,0:T(8,128)}, u32[]{:S(2)}) copy-start(f32[16,32,128]{2,1,0:T(8,128)} %coupling_ref.1) | copy-start | bytes 786436
  4.9 13.3 %copy-start = (f32[3,16,32,128]{3,2,1,0:T(8,128)S(1)}, f32[3,16,32,128]{3,2,1,0:T(8,128)}, u32[]{:S(2)}) copy-start(f32[3,16,32,128]{3,2,1,0:T(8,128)} %velocity_ref.1) | copy-start | bytes 2359300
  4.9 20.9 %copy-start.8 = (s32[16384,1]{0,1:T(1,128)S(1)}, s32[16384,1]{0,1:T(1,128)}, u32[]{:S(2)}) copy-start(s32[16384,1]{0,1:T(1,128)} %param.18) | copy-start | bytes 196612
  4.9 64.8 %all-to-all-start = ((bf16[64,64,256]{2,1,0:T(8,128)(2,1)}), bf16[64,64,256]{2,1,0:T(8,128)(2,1)S(1)}, u32[]{:S(2)}, u32[]{:S(2)}) async-start(bf16[64,64,256]{2,1,0:T(8,128)(2,1)} %shard_map.122), calls=%async_computation | async-start | bytes 4194304 | tf_op jit(solution)/shard_map/all_to_all | solution.py:543
  20.1 24.1 %collective-permute-start = (f32[7,16,3,128]{3,2,1,0:T(4,128)}, f32[7,16,3,128]{3,2,1,0:T(4,128)S(1)}, u32[]{:S(2)}, u32[]{:S(2)}) collective-permute-start(f32[7,16,3,128]{3,2,1,0:T(4,128)} %pad_maximum_fusion), channel_id=1, source_target_pairs={{0,1},{1,2},{2,3},{4,5},{5,6},{6,7},{8,9},{9,10},{10,11},{12,13},{... | collective-permute-start | bytes 516104 | tf_op jit(solution)/shard_map/ppermute | solution.py:562
  23.9 20.2 %collective-permute-start.1 = (f32[7,16,3,128]{3,2,1,0:T(4,128)}, f32[7,16,3,128]{3,2,1,0:T(4,128)}, u32[]{:S(2)}, u32[]{:S(2)}) collective-permute-start(f32[7,16,3,128]{3,2,1,0:T(4,128)} %pad_maximum_fusion.1), channel_id=1, source_target_pairs={{1,0},{2,1},{3,2},{5,4},{6,5},{7,6},{9,8},{10,9},{11,10},{13,12},{... | collective-permute-start | bytes 516104 | tf_op jit(solution)/shard_map/ppermute | solution.py:565
  31.2 0.7 copy-start.6
  43.1 1.1 copy-start.1
  46.1 25.5 %collective-permute-start.2 = (bf16[17,48,128]{2,1,0:T(8,128)(2,1)}, bf16[17,48,128]{2,1,0:T(8,128)(2,1)}, u32[]{:S(2)}, u32[]{:S(2)}) collective-permute-start(bf16[17,48,128]{2,1,0:T(8,128)(2,1)} %get-tuple-element.44), channel_id=1, source_target_pairs={{0,4},{4,8},{8,12},{12,16},{16,20},{20,24},{24,28},{28,32},{32,36}... | collective-permute-start | bytes 626696 | tf_op jit(solution)/shard_map/ppermute | solution.py:572
  49.9 21.6 %collective-permute-start.3 = (bf16[17,48,128]{2,1,0:T(8,128)(2,1)}, bf16[17,48,128]{2,1,0:T(8,128)(2,1)}, u32[]{:S(2)}, u32[]{:S(2)}) collective-permute-start(bf16[17,48,128]{2,1,0:T(8,128)(2,1)} %get-tuple-element.45), channel_id=1, source_target_pairs={{4,0},{8,4},{12,8},{16,12},{20,16},{24,20},{28,24},{32,28},{36,32}... | collective-permute-start | bytes 626696 | tf_op jit(solution)/shard_map/ppermute | solution.py:573
  69.7 29.3 %copy-start.2 = (f32[3,16,32,128]{3,2,1,0:T(8,128)S(1)}, f32[3,16,32,128]{3,2,1,0:T(8,128)}, u32[]{:S(2)}) copy-start(f32[3,16,32,128]{3,2,1,0:T(8,128)} %stretch_ref.1) | copy-start | bytes 2359300
  69.7 29.3 %copy-start.4 = (bf16[128,128]{1,0:T(8,128)(2,1)S(1)}, bf16[128,128]{1,0:T(8,128)(2,1)}, u32[]{:S(2)}) copy-start(bf16[128,128]{1,0:T(8,128)(2,1)} %right_ref.3) | copy-start | bytes 98308
  94.3 7.3 %collective-permute-start.4 = (bf16[128,128]{1,0:T(8,128)(2,1)S(1)}, bf16[128,128]{1,0:T(8,128)(2,1)S(1)}, u32[]{:S(2)}, u32[]{:S(2)}) collective-permute-start(bf16[128,128]{1,0:T(8,128)(2,1)S(1)} %get-tuple-element.55), channel_id=1, source_target_pairs={{0,1},{1,2},{2,3},{4,5},{5,6},{6,7},{8,9},{9,10},{10,11},{12,13},{... | collective-permute-start | bytes 98312 | tf_op jit(solution)/shard_map/ppermute | solution.py:594
  97.5 4.7 %collective-permute-start.5 = (bf16[128,128]{1,0:T(8,128)(2,1)S(1)}, bf16[128,128]{1,0:T(8,128)(2,1)S(1)}, u32[]{:S(2)}, u32[]{:S(2)}) collective-permute-start(bf16[128,128]{1,0:T(8,128)(2,1)S(1)} %get-tuple-element.56), channel_id=1, source_target_pairs={{1,0},{2,1},{3,2},{5,4},{6,5},{7,6},{9,8},{10,9},{11,10},{13,12},{... | collective-permute-start | bytes 98312 | tf_op jit(solution)/shard_map/ppermute | solution.py:595
  102.1 34.0 %copy-start.5 = (bf16[3072,128]{1,0:T(8,128)(2,1)S(1)}, bf16[3072,128]{1,0:T(8,128)(2,1)}, u32[]{:S(2)}) copy-start(bf16[3072,128]{1,0:T(8,128)(2,1)} %shard_map.123) | copy-start | bytes 2359300
  102.1 34.0 %copy-start.7 = (bf16[128,128]{1,0:T(8,128)(2,1)S(1)}, bf16[128,128]{1,0:T(8,128)(2,1)}, u32[]{:S(2)}) copy-start(bf16[128,128]{1,0:T(8,128)(2,1)} %strengths_ref.1) | copy-start | bytes 98308

commit v6 on v5

--- a/solution.py
+++ b/solution.py
@@ -163,10 +163,9 @@
 
 
 def widen(out_ref, centre, low, high):
-    out_ref[0:8, :] = jnp.zeros((8, EDGE), jnp.float32)
-    out_ref[WIDE - 8 : WIDE, :] = jnp.zeros((8, EDGE), jnp.float32)
-    out_ref[FRONT - REACH : FRONT, :] = low
-    out_ref[FRONT + SPAN : FRONT + SPAN + REACH, :] = high
+    edge = jnp.zeros((1, EDGE), jnp.float32)
+    out_ref[0:FRONT, :] = jnp.concatenate([edge, low], axis=0)
+    out_ref[FRONT + SPAN : WIDE, :] = jnp.concatenate([high, edge], axis=0)
     out_ref[FRONT : FRONT + SPAN, :] = centre
 
 
@@ -299,8 +298,8 @@
         rate_ref[layer] = rate
         for component in range(3):
             quarter, entry = entry_of(component, layer)
-            target_ref[component, layer, 0:8, :] = blank
-            target_ref[component, layer, WIDE - 8 : WIDE, :] = blank
+            target_ref[component, layer, 0:FRONT, :] = blank[:FRONT]
+            target_ref[component, layer, FRONT + SPAN : WIDE, :] = blank[:FRONT]
             for side in range(2):
                 start = FRONT + 16 * side
                 target_ref[component, layer, start : start + 16, :] = spread[

time: 138 us -> 138 us (level)
  no operation moved by 1% of the time
where the time goes in v6:
time: 138 us; the launch traced here: 137 us
  blocking collectives  53.3 us (39%)
  starting transfers between devices  28 us (20%)
  Pallas kernels  20.2 us (15%)
  waiting for transfers between devices  18.4 us (13%)
  local copies, waits for them, and re-layouts  7.51 us (5%)
  other arithmetic  6.11 us (4%)
  matrix products  2.78 us (2%)
    all_to_all x1, blocking collectives, shards(): lax.all_to_all(outgoing.reshape(blocks, row_cap, EDGE), 'blk', split_axis...  30.5 us
    all_to_all x1, blocking collectives, shards(): lax.all_to_all(sums.reshape(blocks, 16, 2 * EDGE), 'blk', split_axis=0, c...  22.8 us
    all_to_all x1, waiting for transfers between devices, shards(): lax.all_to_all(pieces, 'blk', split_axis=0, concat_axis=0, tiled=True)  17.9 us
    all_to_all x1, starting transfers between devices, shards(): lax.all_to_all(pieces, 'blk', split_axis=0, concat_axis=0, tiled=True)  13.3 us
    pallas_call x1, Pallas kernels, gathered_rows(): pl.pallas_call(gather_kernel, in_specs=[pl.BlockSpec(memory_space=pltpu.S...  6.16 us
    pallas_call x1, Pallas kernels, tile_pieces(): pl.pallas_call(pieces_kernel, grid=(tiles // GROUP,), in_specs=[pl.BlockS...  4.25 us
    ppermute x1, starting transfers between devices, shards(): low = lax.ppermute(last, 'blk', block_forward)  3.81 us
    pallas_call x1, Pallas kernels, grid_update(): pl.pallas_call(grid_kernel, in_specs=[vmem] * 9 + [pl.BlockSpec(memory_sp...  3.51 us
  transfers between devices with their start and end apart: 7, of which 2 were waited for; matrix products, arithmetic and copies ran while one was open for 11% of the time, Pallas kernels for 9%

profile of v6, /device:TPU:1, one launch (start us, length us, event | category | flops | bytes accessed | tf_op | source)
XLA Modules:
  0.0 137.2 jit_solution(5447652488839283147)
XLA Ops:
  0.6 4.3 %shard_map.122 = bf16[64,64,256]{2,1,0:T(8,128)(2,1)} custom-call(bf16[8192,128]{1,0:T(8,128)(2,1)} %remesh_ref.3, bf16[128,128]{1,0:T(8,128)(2,1)} %strengths_ref.1, bf16[128,128]{1,0:T(8,128)(2,1)} %left_ref.1), custom_call_target="tpu_custom_call" | custom-call | tf_op jit(solution)/shard_map/pallas_call | solution.py:64
  4.9 13.3 %all-to-all-start = ((bf16[64,64,256]{2,1,0:T(8,128)(2,1)}), bf16[64,64,256]{2,1,0:T(8,128)(2,1)S(1)}, u32[]{:S(2)}, u32[]{:S(2)}) async-start(bf16[64,64,256]{2,1,0:T(8,128)(2,1)} %shard_map.122), calls=%async_computation | async-start | bytes 4194304 | tf_op jit(solution)/shard_map/all_to_all | solution.py:542
  18.2 1.1 fusion.11
  19.3 0.7 pad_maximum_fusion
  20.1 3.1 %collective-permute-start = (f32[7,16,3,128]{3,2,1,0:T(4,128)}, f32[7,16,3,128]{3,2,1,0:T(4,128)S(1)}, u32[]{:S(2)}, u32[]{:S(2)}) collective-permute-start(f32[7,16,3,128]{3,2,1,0:T(4,128)} %pad_maximum_fusion), channel_id=1, source_target_pairs={{0,1},{1,2},{2,3},{4,5},{5,6},{6,7},{8,9},{9,10},{10,11},{12,13},{... | collective-permute-start | bytes 516104 | tf_op jit(solution)/shard_map/ppermute | solution.py:561
  23.2 0.7 pad_maximum_fusion.1
  23.9 1.3 collective-permute-start.1
  25.2 0.5 broadcast.24
  25.8 0.8 reduce.9
  26.6 0.8 reshape_reshape_transpose.3
  27.3 0.9 reshape_reshape.3
  28.3 1.0 add_reduce_fusion
  29.4 1.5 %constant_dynamic-slice_fusion = (s32[64,12,128]{2,1,0:T(8,128)S(1)}, s32[64,12,128]{2,1,0:T(8,128)S(1)}) fusion(s32[64,48,128]{2,1,0:T(8,128)} %bitcast.31, s32[]{:T(128)S(6)} %select_n.28, s32[64,48,128]{2,1,0:T(8,128)} %bitcast.32), kind=kLoop, calls=%fused_computation.24 | loop fusion | bytes 1572868 | tf_op jit(solution)/shard_map/dynamic_slice | solution.py:547
  31.2 0.7 copy-done.6
  32.0 0.7 fusion.4
  32.7 2.8 %select_reduce_fusion = s32[64,48]{1,0:T(8,128)S(1)} fusion(s32[64,1536]{1,0:T(8,128)S(1)} %bitcast.28, s32[64,1536]{1,0:T(8,128)S(1)} %fusion.4), kind=kLoop, calls=%fused_computation | loop fusion | flops 14152704 | bytes 798720 | tf_op jit(solution)/shard_map/reduce_sum | solution.py:506
  35.4 0.7 reshape.69.index_ref
  36.1 6.2 %shard_map.123 = bf16[3072,128]{1,0:T(8,128)(2,1)} custom-call(s32[3072]{0:T(1024)} %reshape.69.index_ref, bf16[8192,128]{1,0:T(8,128)(2,1)} %remesh_ref.3), custom_call_target="tpu_custom_call" | custom-call | bytes 16777216 | tf_op jit(solution)/shard_map/pallas_call | solution.py:94
  42.3 0.8 dynamic-slice_reduce_fusion
  43.1 1.0 fusion.5
  44.2 1.8 %shard_map.125 = (bf16[17,48,128]{2,1,0:T(8,128)(2,1)}, bf16[17,48,128]{2,1,0:T(8,128)(2,1)}) custom-call(f32[3,16,32,128]{3,2,1,0:T(8,128)S(1)} %copy-done, f32[3,16,32,128]{3,2,1,0:T(8,128)S(1)} %copy-done.1, f32[16,32,128]{2,1,0:T(8,128)S(1)} %copy-done.3, f32[7,16,3,128]{3,2,1,0:T(4,128)S(1)} %collective-permute-done.low_ref.span_low, ...), custom_call_target="tpu_custom_call" | custom-call | tf_op jit(solution)/shard_map/pallas_call | solution.py:195
  46.0 3.8 %collective-permute-start.2 = (bf16[17,48,128]{2,1,0:T(8,128)(2,1)}, bf16[17,48,128]{2,1,0:T(8,128)(2,1)}, u32[]{:S(2)}, u32[]{:S(2)}) collective-permute-start(bf16[17,48,128]{2,1,0:T(8,128)(2,1)} %get-tuple-element.44), channel_id=1, source_target_pairs={{0,4},{4,8},{8,12},{12,16},{16,20},{20,24},{24,28},{28,32},{32,36}... | collective-permute-start | bytes 626696 | tf_op jit(solution)/shard_map/ppermute | solution.py:571
  49.9 1.9 %collective-permute-start.3 = (bf16[17,48,128]{2,1,0:T(8,128)(2,1)}, bf16[17,48,128]{2,1,0:T(8,128)(2,1)}, u32[]{:S(2)}, u32[]{:S(2)}) collective-permute-start(bf16[17,48,128]{2,1,0:T(8,128)(2,1)} %get-tuple-element.45), channel_id=1, source_target_pairs={{4,0},{8,4},{12,8},{16,12},{20,16},{24,20},{28,24},{32,28},{36,32}... | collective-permute-start | bytes 626696 | tf_op jit(solution)/shard_map/ppermute | solution.py:572
  51.8 17.9 %all-to-all-done = bf16[64,64,256]{2,1,0:T(8,128)(2,1)S(1)} async-done(((bf16[64,64,256]{2,1,0:T(8,128)(2,1)}), bf16[64,64,256]{2,1,0:T(8,128)(2,1)S(1)}, u32[]{:S(2)}, u32[]{:S(2)}) %all-to-all-start) | async-done | bytes 2097184 | tf_op jit(solution)/shard_map/all_to_all | solution.py:542
  69.7 1.8 %shard_map.124 = bf16[1024,256]{1,0:T(8,128)(2,1)S(1)} custom-call(s32[1]{0:T(128)} %bitcast.quarter_ref, s32[1,4096]{1,0:T(1,128)S(1)} %add.37.position_ref, bf16[4096,256]{1,0:T(8,128)(2,1)S(1)} %bitcast.20), custom_call_target="tpu_custom_call" | custom-call | tf_op jit(solution)/shard_map/pallas_call | solution.py:155
  71.5 22.8 %all_to_all.15.sums_ref = bf16[64,16,256]{2,1,0:T(8,128)(2,1)S(1)} all-to-all(bf16[64,16,256]{2,1,0:T(8,128)(2,1)S(1)} %bitcast.22), channel_id=1, replica_groups=mesh['blk'=64,'span'=4] {'blk'}, dimensions={0} | all-to-all | bytes 1048576 | tf_op jit(solution)/shard_map/all_to_all | solution.py:586
  94.3 3.1 %collective-permute-start.4 = (bf16[128,128]{1,0:T(8,128)(2,1)S(1)}, bf16[128,128]{1,0:T(8,128)(2,1)S(1)}, u32[]{:S(2)}, u32[]{:S(2)}) collective-permute-start(bf16[128,128]{1,0:T(8,128)(2,1)S(1)} %get-tuple-element.55), channel_id=1, source_target_pairs={{0,1},{1,2},{2,3},{4,5},{5,6},{6,7},{8,9},{9,10},{10,11},{12,13},{... | collective-permute-start | bytes 98312 | tf_op jit(solution)/shard_map/ppermute | solution.py:593
  97.5 1.5 %collective-permute-start.5 = (bf16[128,128]{1,0:T(8,128)(2,1)S(1)}, bf16[128,128]{1,0:T(8,128)(2,1)S(1)}, u32[]{:S(2)}, u32[]{:S(2)}) collective-permute-start(bf16[128,128]{1,0:T(8,128)(2,1)S(1)} %get-tuple-element.56), channel_id=1, source_target_pairs={{1,0},{2,1},{3,2},{5,4},{6,5},{7,6},{9,8},{10,9},{11,10},{13,12},{... | collective-permute-start | bytes 98312 | tf_op jit(solution)/shard_map/ppermute | solution.py:594
  99.0 2.7 %shard_map.126 = (f32[3,20,40,128]{3,2,1,0:T(8,128)S(1)}, f32[3,20,40,128]{3,2,1,0:T(8,128)S(1)}, f32[3,20,40,128]{3,2,1,0:T(8,128)S(1)}, f32[3,20,40,128]{3,2,1...) custom-call(bf16[1024,256]{1,0:T(8,128)(2,1)S(1)} %bitcast.21, bf16[128,128]{1,0:T(8,128)(2,1)S(1)} %copy-done.4, ...), custom_call_target="tpu_custom_call" | custom-call | flops 164000000 | bytes 8388608 | tf_op jit(solution)/shard_map/pallas_call | solution.py:312
  102.1 3.5 %shard_map.128 = (f32[3,16,32,128]{3,2,1,0:T(8,128)}, bf16[3072,128]{1,0:T(8,128)(2,1)S(1)}) custom-call(f32[3,20,40,128]{3,2,1,0:T(8,128)S(1)} %get-tuple-element.54.target_ref, bf16[128,128]{1,0:T(8,128)(2,1)S(1)} %collective-permute-done.4.low_ref, bf16[128,128]{1,0:T(8,128)(2,1)S(1)} %collective-permute-done.5.high_ref, bf16[128,128]{1,0:T(8,128)(2,1)S(1)} %copy-done.4, ...), custom_call_target="tpu_custom_call" | custom-call | tf_op jit(solution)/shard_map/pallas_call | solution.py:439
  105.6 30.5 %all_to_all.16 = bf16[64,48,128]{2,1,0:T(8,128)(2,1)S(1)} all-to-all(bf16[64,48,128]{2,1,0:T(8,128)(2,1)S(1)} %bitcast.24), channel_id=1, replica_groups=mesh['blk'=64,'span'=4] {'blk'}, dimensions={0} | all-to-all | bytes 1572864 | tf_op jit(solution)/shard_map/all_to_all | solution.py:607
  136.1 1.0 fusion.6
  (29 shorter events, 0.9 us)
Async XLA Ops:
  4.9 13.3 %copy-start.3 = (f32[16,32,128]{2,1,0:T(8,128)S(1)}, f32[16,32,128]{2,1,0:T(8,128)}, u32[]{:S(2)}) copy-start(f32[16,32,128]{2,1,0:T(8,128)} %coupling_ref.1) | copy-start | bytes 786436
  4.9 13.3 %copy-start = (f32[3,16,32,128]{3,2,1,0:T(8,128)S(1)}, f32[3,16,32,128]{3,2,1,0:T(8,128)}, u32[]{:S(2)}) copy-start(f32[3,16,32,128]{3,2,1,0:T(8,128)} %velocity_ref.1) | copy-start | bytes 2359300
  4.9 20.9 %copy-start.8 = (s32[16384,1]{0,1:T(1,128)S(1)}, s32[16384,1]{0,1:T(1,128)}, u32[]{:S(2)}) copy-start(s32[16384,1]{0,1:T(1,128)} %param.18) | copy-start | bytes 196612
  4.9 64.8 %all-to-all-start = ((bf16[64,64,256]{2,1,0:T(8,128)(2,1)}), bf16[64,64,256]{2,1,0:T(8,128)(2,1)S(1)}, u32[]{:S(2)}, u32[]{:S(2)}) async-start(bf16[64,64,256]{2,1,0:T(8,128)(2,1)} %shard_map.122), calls=%async_computation | async-start | bytes 4194304 | tf_op jit(solution)/shard_map/all_to_all | solution.py:542
  20.1 24.1 %collective-permute-start = (f32[7,16,3,128]{3,2,1,0:T(4,128)}, f32[7,16,3,128]{3,2,1,0:T(4,128)S(1)}, u32[]{:S(2)}, u32[]{:S(2)}) collective-permute-start(f32[7,16,3,128]{3,2,1,0:T(4,128)} %pad_maximum_fusion), channel_id=1, source_target_pairs={{0,1},{1,2},{2,3},{4,5},{5,6},{6,7},{8,9},{9,10},{10,11},{12,13},{... | collective-permute-start | bytes 516104 | tf_op jit(solution)/shard_map/ppermute | solution.py:561
  23.9 20.2 %collective-permute-start.1 = (f32[7,16,3,128]{3,2,1,0:T(4,128)}, f32[7,16,3,128]{3,2,1,0:T(4,128)}, u32[]{:S(2)}, u32[]{:S(2)}) collective-permute-start(f32[7,16,3,128]{3,2,1,0:T(4,128)} %pad_maximum_fusion.1), channel_id=1, source_target_pairs={{1,0},{2,1},{3,2},{5,4},{6,5},{7,6},{9,8},{10,9},{11,10},{13,12},{... | collective-permute-start | bytes 516104 | tf_op jit(solution)/shard_map/ppermute | solution.py:564
  31.2 0.7 copy-start.6
  43.1 1.1 copy-start.1
  46.0 25.5 %collective-permute-start.2 = (bf16[17,48,128]{2,1,0:T(8,128)(2,1)}, bf16[17,48,128]{2,1,0:T(8,128)(2,1)}, u32[]{:S(2)}, u32[]{:S(2)}) collective-permute-start(bf16[17,48,128]{2,1,0:T(8,128)(2,1)} %get-tuple-element.44), channel_id=1, source_target_pairs={{0,4},{4,8},{8,12},{12,16},{16,20},{20,24},{24,28},{28,32},{32,36}... | collective-permute-start | bytes 626696 | tf_op jit(solution)/shard_map/ppermute | solution.py:571
  49.9 21.7 %collective-permute-start.3 = (bf16[17,48,128]{2,1,0:T(8,128)(2,1)}, bf16[17,48,128]{2,1,0:T(8,128)(2,1)}, u32[]{:S(2)}, u32[]{:S(2)}) collective-permute-start(bf16[17,48,128]{2,1,0:T(8,128)(2,1)} %get-tuple-element.45), channel_id=1, source_target_pairs={{4,0},{8,4},{12,8},{16,12},{20,16},{24,20},{28,24},{32,28},{36,32}... | collective-permute-start | bytes 626696 | tf_op jit(solution)/shard_map/ppermute | solution.py:572
  69.7 29.3 %copy-start.2 = (f32[3,16,32,128]{3,2,1,0:T(8,128)S(1)}, f32[3,16,32,128]{3,2,1,0:T(8,128)}, u32[]{:S(2)}) copy-start(f32[3,16,32,128]{3,2,1,0:T(8,128)} %stretch_ref.1) | copy-start | bytes 2359300
  69.7 29.3 %copy-start.4 = (bf16[128,128]{1,0:T(8,128)(2,1)S(1)}, bf16[128,128]{1,0:T(8,128)(2,1)}, u32[]{:S(2)}) copy-start(bf16[128,128]{1,0:T(8,128)(2,1)} %right_ref.3) | copy-start | bytes 98308
  94.3 7.3 %collective-permute-start.4 = (bf16[128,128]{1,0:T(8,128)(2,1)S(1)}, bf16[128,128]{1,0:T(8,128)(2,1)S(1)}, u32[]{:S(2)}, u32[]{:S(2)}) collective-permute-start(bf16[128,128]{1,0:T(8,128)(2,1)S(1)} %get-tuple-element.55), channel_id=1, source_target_pairs={{0,1},{1,2},{2,3},{4,5},{5,6},{6,7},{8,9},{9,10},{10,11},{12,13},{... | collective-permute-start | bytes 98312 | tf_op jit(solution)/shard_map/ppermute | solution.py:593
  97.5 4.7 %collective-permute-start.5 = (bf16[128,128]{1,0:T(8,128)(2,1)S(1)}, bf16[128,128]{1,0:T(8,128)(2,1)S(1)}, u32[]{:S(2)}, u32[]{:S(2)}) collective-permute-start(bf16[128,128]{1,0:T(8,128)(2,1)S(1)} %get-tuple-element.56), channel_id=1, source_target_pairs={{1,0},{2,1},{3,2},{5,4},{6,5},{7,6},{9,8},{10,9},{11,10},{13,12},{... | collective-permute-start | bytes 98312 | tf_op jit(solution)/shard_map/ppermute | solution.py:594
  102.1 34.0 %copy-start.5 = (bf16[3072,128]{1,0:T(8,128)(2,1)S(1)}, bf16[3072,128]{1,0:T(8,128)(2,1)}, u32[]{:S(2)}) copy-start(bf16[3072,128]{1,0:T(8,128)(2,1)} %shard_map.123) | copy-start | bytes 2359300
  102.1 34.0 %copy-start.7 = (bf16[128,128]{1,0:T(8,128)(2,1)S(1)}, bf16[128,128]{1,0:T(8,128)(2,1)}, u32[]{:S(2)}) copy-start(bf16[128,128]{1,0:T(8,128)(2,1)} %strengths_ref.1) | copy-start | bytes 98308
